TPU v7x, 128 devices: a whole 4x4x4 slice. The times are simulated.
128 devices in a mesh: batch: 16 (over x, y), proto: 8 (over z, core).
Axes of the slice: x: 4, y: 4, z: 4, core: 2. Of those that a mesh axis runs over, the one named last changes fastest.
Arguments:
- teacher_feats: bfloat16 [6144, 256], P('batch'), may hold values from -6 to 6
- student_feats: bfloat16 [6144, 256], P('batch'), may hold values from -6 to 6
- proto_weight: bfloat16 [256, 131072], P(None, 'proto'), may hold values from -1 to 1
Outputs:
- feat_grad: float32 [6144, 256], P('batch')
- proto_grad: float32 [256, 131072], P(None, ('proto', 'batch'))
All inputs are finite; a program needn't handle non-finite values.
Results may differ from a plain program's by a relative error of at most 0.0005.
The roundings to bfloat16 on the way count: a program that leaves them out, or rounds other values in their place, can miss the bound.
Values may be sent and summed in bfloat16 or wider, within the bound.
No kernel may reach another device: no remote copies, remote signals or barrier semaphores. Data moves between devices by JAX's collectives and lax.ppermute only.
A program may use at most 192 MiB of HBM per device.

v0:
```python
import math

import jax
import jax.numpy as jnp
from jax import lax
from jax.sharding import PartitionSpec as P

D = 256
PROTOS = 131072
ITERS = 3


def unit_rows(feats):
    feats_f = feats.astype(jnp.float32)
    rnorm = lax.rsqrt(jnp.mean(feats_f * feats_f, axis=1, keepdims=True) + 1e-06) / math.sqrt(D)
    return (feats_f * rnorm, rnorm)


def shards(teacher_feats, student_feats, proto_weight):
    weight_f = proto_weight.astype(jnp.float32)
    protos = (
        weight_f
        * lax.rsqrt(jnp.mean(weight_f * weight_f, axis=0, keepdims=True) + 1e-06)
        / math.sqrt(D)
    ).astype(jnp.bfloat16)
    teach_f, unused = unit_rows(teacher_feats)
    teach = teach_f.astype(jnp.bfloat16)
    stud_f, rnorm_s = unit_rows(student_feats)
    stud = stud_f.astype(jnp.bfloat16)
    expo = jnp.exp(jnp.dot(teach, protos, preferred_element_type=jnp.float32) / 0.07)
    s_exp = jnp.exp(jnp.dot(stud, protos, preferred_element_type=jnp.float32) / 0.1)
    zden = lax.psum(jnp.sum(s_exp, axis=1), "proto")
    rowsc = jnp.ones((expo.shape[0],), jnp.float32)
    colsc = jnp.ones((expo.shape[1],), jnp.float32)
    for step in range(ITERS):
        col_part = jnp.sum(expo * rowsc[:, None], axis=0)
        colsc = 1.0 / lax.psum(col_part, "batch")
        row_part = jnp.sum(expo * colsc[None, :], axis=1)
        rowsc = 1.0 / lax.psum(row_part, "proto")
    target = expo * rowsc[:, None] * colsc[None, :]
    grad_s = (PROTOS * (s_exp / zden[:, None] - target) / 0.1).astype(jnp.bfloat16)
    dz_part = lax.dot_general(
        grad_s, protos, (((1,), (1,)), ((), ())), preferred_element_type=jnp.float32
    )
    dz = lax.psum(dz_part, "proto")
    feat_grad = (dz - stud_f * jnp.sum(stud_f * dz, axis=1, keepdims=True)) * rnorm_s
    term = lax.dot_general(
        stud, grad_s, (((0,), (0,)), ((), ())), preferred_element_type=jnp.float32
    )
    proto_grad = lax.psum_scatter(term, "batch", scatter_dimension=1, tiled=True)
    return (feat_grad, proto_grad)


def solution(mesh):
    in_specs = (P("batch", None), P("batch", None), P(None, "proto"))
    out_specs = (P("batch", None), P(None, ("proto", "batch")))
    return jax.shard_map(shards, mesh=mesh, in_specs=in_specs, out_specs=out_specs, check_vma=False)
```

profile of v0, /device:TPU:1, one launch (start us, length us, event | category | flops | bytes accessed | tf_op | source)
XLA Modules:
  0.0 563.2 jit_solution(15601712353400405643)
XLA Ops:
  7.2 1.1 fusion.14
  8.3 5.1 fusion
  13.5 14.2 %fusion.24 = (f32[16384]{0:T(1024)}, f32[384,16384]{1,0:T(8,128)}) fusion(bf16[256,16384]{1,0:T(8,128)(2,1)} %param.5, f32[16384]{0:T(1024)S(1)} %add_rsqrt_fusion, bf16[384,256]{1,0:T(8,128)(2,1)} %param.3, f32[384]{0:T(512)S(1)} %rsqrt_multiply_fusion), kind=kOutput, calls=%fused_computation.41 | convolution fusion | flops 3250864128 | bytes 33883648 | tf_op jit(solution)/shard_map/dot_general | solution.py:30
  27.9 82.3 %all-reduce.6.cloned.1.call-done = f32[16384]{0:T(1024)} async-done(((f32[16384]{0:T(1024)}), f32[16384]{0:T(1024)}) %all-reduce.6.cloned.1.call-update) | async-done | bytes 65552 | tf_op jit(solution)/shard_map/psum | solution.py:37
  111.1 9.5 %multiply_reduce_fusion.4 = f32[384]{0:T(512)S(1)} fusion(f32[384,16384]{1,0:T(8,128)} %get-tuple-element.5, f32[16384]{0:T(1024)S(1)} %broadcast_divide_fusion.2), kind=kLoop, calls=%fused_computation.5 | loop fusion | flops 12582528 | bytes 25232896 | tf_op jit(solution)/shard_map/reduce_sum | solution.py:38
  120.6 14.1 %psum.58 = f32[384]{0:T(512)S(1)} all-reduce(f32[384]{0:T(512)S(1)} %multiply_reduce_fusion.4), channel_id=1, replica_groups=mesh['batch'=16,'proto'=8] {'proto'}, use_global_device_ids=true, to_apply=%region_8.0 | all-reduce | flops 384 | bytes 3072 | tf_op jit(solution)/shard_map/psum | solution.py:39
  134.7 10.3 %multiply_reduce_fusion.3 = f32[16384]{0:T(1024)} fusion(f32[384,16384]{1,0:T(8,128)} %get-tuple-element.5, f32[384]{0:T(512)S(1)} %broadcast_divide_fusion.5), kind=kLoop, calls=%fused_computation.4 | loop fusion | flops 12566528 | bytes 25232896 | tf_op jit(solution)/shard_map/reduce_sum | solution.py:36
  145.1 76.6 %all-reduce.8.cloned.1.call-done = f32[16384]{0:T(1024)} async-done(((f32[16384]{0:T(1024)}), f32[16384]{0:T(1024)}) %all-reduce.8.cloned.1.call-update) | async-done | bytes 65552 | tf_op jit(solution)/shard_map/psum | solution.py:37
  222.6 9.5 %multiply_reduce_fusion.2 = f32[384]{0:T(512)S(1)} fusion(f32[384,16384]{1,0:T(8,128)} %get-tuple-element.5, f32[16384]{0:T(1024)S(1)} %broadcast_divide_fusion.1), kind=kLoop, calls=%fused_computation.3 | loop fusion | flops 12582528 | bytes 25232896 | tf_op jit(solution)/shard_map/reduce_sum | solution.py:38
  232.1 14.1 %psum.60 = f32[384]{0:T(512)S(1)} all-reduce(f32[384]{0:T(512)S(1)} %multiply_reduce_fusion.2), channel_id=1, replica_groups=mesh['batch'=16,'proto'=8] {'proto'}, use_global_device_ids=true, to_apply=%region_12.0 | all-reduce | flops 384 | bytes 3072 | tf_op jit(solution)/shard_map/psum | solution.py:39
  246.2 10.3 %multiply_reduce_fusion.1 = f32[16384]{0:T(1024)} fusion(f32[384,16384]{1,0:T(8,128)} %get-tuple-element.5, f32[384]{0:T(512)S(1)} %broadcast_divide_fusion.4), kind=kLoop, calls=%fused_computation.2 | loop fusion | flops 12566528 | bytes 25232896 | tf_op jit(solution)/shard_map/reduce_sum | solution.py:36
  256.6 13.5 %fusion.25 = (f32[384]{0:T(512)S(1)}, f32[384,16384]{1,0:T(8,128)}) fusion(bf16[256,16384]{1,0:T(8,128)(2,1)} %param.5, f32[16384]{0:T(1024)S(1)} %add_rsqrt_fusion, bf16[384,256]{1,0:T(8,128)(2,1)S(1)} %copy-done.1, f32[384]{0:T(512)S(1)} %rsqrt_multiply_fusion.1), kind=kOutput, calls=%fused_computation.42 | convolution fusion | flops 3250880000 | bytes 33819648 | tf_op jit(solution)/shard_map/dot_general | solution.py:31
  270.1 63.1 %all-reduce.10.cloned.1.call-done = f32[16384]{0:T(1024)} async-done(((f32[16384]{0:T(1024)}), f32[16384]{0:T(1024)}) %all-reduce.10.cloned.1.call-update) | async-done | bytes 65552 | tf_op jit(solution)/shard_map/psum | solution.py:37
  333.2 0.9 broadcast_divide_fusion
  334.1 9.4 %multiply_reduce_fusion = f32[384]{0:T(512)S(1)} fusion(f32[384,16384]{1,0:T(8,128)} %get-tuple-element.5, f32[16384]{0:T(1024)S(1)} %broadcast_divide_fusion), kind=kLoop, calls=%fused_computation.1 | loop fusion | flops 12582528 | bytes 25232896 | tf_op jit(solution)/shard_map/reduce_sum | solution.py:38
  343.5 14.3 %all-reduce = (f32[384]{0:T(512)S(1)}, f32[384]{0:T(512)S(1)}) all-reduce(f32[384]{0:T(512)S(1)} %multiply_reduce_fusion, f32[384]{0:T(512)S(1)} %get-tuple-element.6), channel_id=1, replica_groups=mesh['batch'=16,'proto'=8] {'proto'}, use_global_device_ids=true, to_apply=%region_16.0 | all-reduce | flops 768 | bytes 6144 | tf_op jit(solution)/shard_map/psum | solution.py:39
  357.8 16.5 %multiply_convert_fusion = bf16[384,16384]{1,0:T(8,128)(2,1)S(1)} fusion(f32[384,16384]{1,0:T(8,128)} %get-tuple-element.5, f32[384,16384]{1,0:T(8,128)} %get-tuple-element.7, f32[384]{0:T(512)S(1)} %broadcast_divide_fusion.3, f32[16384]{0:T(1024)S(1)} %broadcast_divide_fusion, f32[384]{0:T(512)S(1)} %get-tuple-element.3), kind=kLoop, calls=%fused_computation | loop fusion | flops 37748736 | bytes 62983168 | tf_op jit(solution)/shard_map/convert_element_type | solution.py:41
  374.3 4.6 copy-done
  378.9 6.7 %fusion.3 = f32[384,256]{1,0:T(8,128)} fusion(bf16[384,16384]{1,0:T(8,128)(2,1)S(1)} %multiply_convert_fusion, bf16[256,16384]{1,0:T(8,128)(2,1)} %param.5, f32[16384]{0:T(1024)S(1)} %add_rsqrt_fusion), kind=kOutput, calls=%fused_computation.13 | convolution fusion | flops 3238002688 | bytes 21430272 | tf_op jit(solution)/shard_map/dot_general | solution.py:42
  385.6 12.8 %fusion.18 = f32[256,16384]{1,0:T(8,128)} fusion(bf16[384,16384]{1,0:T(8,128)(2,1)} %copy-done, bf16[384,256]{1,0:T(8,128)(2,1)S(1)} %copy-done.1, f32[384]{0:T(512)S(1)} %rsqrt_multiply_fusion.1), kind=kOutput, calls=%fused_computation.28 | convolution fusion | flops 3221520384 | bytes 29558272 | tf_op jit(solution)/shard_map/dot_general | solution.py:47
  398.5 43.2 %all-reduce.12.cloned.1.call-done = f32[384,256]{1,0:T(8,128)} async-done(((f32[384,256]{1,0:T(8,128)}), f32[384,256]{1,0:T(8,128)}) %all-reduce.12.cloned.1.call-update) | async-done | bytes 393232 | tf_op jit(solution)/shard_map/psum | solution.py:45
  441.6 1.2 fusion.10
  442.9 1.9 fusion.12
  444.8 111.9 %reduce-scatter.2.cloned.1.call-done = f32[256,1024]{1,0:T(8,128)} async-done(((f32[256,16384]{1,0:T(8,128)}), f32[256,1024]{1,0:T(8,128)}) %reduce-scatter.2.cloned.1.call-update) | async-done | bytes 1048592 | tf_op jit(solution)/shard_map/reduce_scatter | solution.py:50
  (22 shorter events, 2.2 us)
Async XLA Ops:
  7.2 103.1 %all-reduce.6.cloned.1.call-start = ((), (), s32[]{:S(2)}) async-start(), calls=%async_computation.1 | async-start | bytes 131072 | tf_op jit(solution)/shard_map/psum | solution.py:37
  13.5 14.3 %copy-start.1 = (bf16[384,256]{1,0:T(8,128)(2,1)S(1)}, bf16[384,256]{1,0:T(8,128)(2,1)}, u32[]{:S(2)}) copy-start(bf16[384,256]{1,0:T(8,128)(2,1)} %param.4) | copy-start | bytes 589828
  27.7 194.1 %all-reduce.8.cloned.1.call-start = ((), (), s32[]{:S(2)}) async-start(), calls=%async_computation.2 | async-start | bytes 131072 | tf_op jit(solution)/shard_map/psum | solution.py:37
  145.1 188.2 %all-reduce.10.cloned.1.call-start = ((), (), s32[]{:S(2)}) async-start(), calls=%async_computation.3 | async-start | bytes 131072 | tf_op jit(solution)/shard_map/psum | solution.py:37
  256.6 185.1 %all-reduce.12.cloned.1.call-start = ((), (), s32[]{:S(2)}) async-start(), calls=%async_computation.4 | async-start | bytes 786432 | tf_op jit(solution)/shard_map/psum | solution.py:45
  374.3 4.6 copy-start
  385.6 171.1 %reduce-scatter.2.cloned.1.call-start = ((), (), s32[]{:S(2)}) async-start(), calls=%async_computation.5 | async-start | bytes 17825792 | tf_op jit(solution)/shard_map/reduce_scatter | solution.py:50
Sparse Core Ops, SparseCore 0:
  27.8 82.3 all-reduce.5
  145.2 76.5 all-reduce.7
  256.7 76.5 all-reduce.9
  385.7 55.8 all-reduce.11
  445.5 111.1 reduce-scatter.1
where the time goes:
time: 564 us; the launch traced here: 563 us
  waiting for transfers between devices  377 us (67%)
  other arithmetic  77.6 us (14%)
  matrix products  47.2 us (8%)
  blocking collectives  42.5 us (8%)
  between operations  13.9 us (2%)
    psum x3, waiting for transfers between devices, shards(): colsc = 1.0 / lax.psum(col_part, 'batch')  222 us
    reduce_scatter x1, waiting for transfers between devices, shards(): lax.psum_scatter(term, 'batch', scatter_dimension=1, tiled=True)  112 us
    psum x1, waiting for transfers between devices, shards(): dz = lax.psum(dz_part, 'proto')  43.2 us
    psum x3, blocking collectives, shards(): rowsc = 1.0 / lax.psum(row_part, 'proto')  42.5 us
    reduce_sum x3, other arithmetic, shards(): row_part = jnp.sum(expo * colsc[None, :], axis=1)  28.3 us
    reduce_sum x2, other arithmetic, shards(): col_part = jnp.sum(expo * rowsc[:, None], axis=0)  20.7 us
    convert_element_type x1, other arithmetic, shards(): (PROTOS * (s_exp / zden[:, None] - target) / 0.1).astype(jnp.bfloat16)  16.5 us
    dot_general x1, matrix products, shards(): jnp.dot(teach, protos, preferred_element_type=jnp.float32) / 0.07  14.2 us
  transfers between devices with their start and end apart: 5, of which 5 were waited for; matrix products, arithmetic and copies ran while one was open for 5% of the time, Pallas kernels for 0%

commit v1 on v0

v1 whole, which is shorter than its diff:
```python
import math

import jax
import jax.numpy as jnp
from jax import lax
from jax.experimental import pallas as pl
from jax.experimental.pallas import tpu as pltpu
from jax.sharding import Mesh, PartitionSpec as P

D = 256
PROTOS = 131072
ITERS = 3
ROWS = 384
COLS = 16384
OWN = 1024
GROUPS = COLS // 128
NB = 16
NP = 8
KT = math.log2(math.e) / 0.07
KS = math.log2(math.e) / 0.1
GSCALE = PROTOS / 0.1

f32 = jnp.float32
bf16 = jnp.bfloat16
XY = ("x", "y")
ZC = ("z", "c")
MIB = 2**20


def whole():
    return pl.BlockSpec(memory_space=pltpu.VMEM)


def params(mib):
    return pltpu.CompilerParams(vmem_limit_bytes=mib * MIB)


def row_norm(feats):
    return lax.rsqrt(jnp.mean(feats * feats, axis=1, keepdims=True) + 1e-06) / math.sqrt(D)


def lanes_to_rows(vec, width):
    return jnp.transpose(jnp.broadcast_to(vec, (width, vec.shape[1])))


def rows_to_lanes(acc):
    return jnp.sum(jnp.transpose(acc), axis=0, keepdims=True)


def norm_kernel(t_ref, s_ref, t_out, s_out):
    for src, dst in ((t_ref, t_out), (s_ref, s_out)):
        feats = src[...].astype(f32)
        dst[...] = (feats * row_norm(feats)).astype(bf16)


def first_kernel(w_ref, t_ref, s_ref, p_ref, e_ref, col_ref, z_ref, zacc):
    step = pl.program_id(0)

    @pl.when(step == 0)
    def _():
        zacc[...] = jnp.zeros_like(zacc)

    w = w_ref[...].astype(f32)
    inv = lax.rsqrt(jnp.mean(w * w, axis=0, keepdims=True) + 1e-06) / math.sqrt(D)
    p_ref[...] = (w * inv).astype(bf16)
    sums = []
    zsum = zacc[...]
    for n in range(4):
        p = p_ref[:, n * 256 : (n + 1) * 256]
        e = jnp.exp2(jnp.dot(t_ref[...], p, preferred_element_type=f32) * KT)
        e_ref[:, pl.ds(pl.multiple_of(step * 1024 + n * 256, 256), 256)] = e
        for h in range(2):
            sums.append(jnp.sum(e[:, h * 128 : (h + 1) * 128], axis=0, keepdims=True))
        s = jnp.exp2(jnp.dot(s_ref[...], p, preferred_element_type=f32) * KS)
        zsum = zsum + s[:, :128] + s[:, 128:]
    zacc[...] = zsum
    part = jnp.concatenate(sums, axis=0)
    col_ref[:, pl.ds(pl.multiple_of(step * 8, 8), 8), :] = jnp.broadcast_to(part, (NB, 8, 128))

    @pl.when(step == pl.num_programs(0) - 1)
    def _():
        z_ref[...] = rows_to_lanes(zacc[...])


def row_pass(colp_ref, e_ref, c_ref):
    c_ref[...] = 1.0 / jnp.sum(colp_ref[...], axis=0)
    halves = []
    for half in range(2):
        rows = slice(half * 192, (half + 1) * 192)

        def body(q, acc):
            c8 = c_ref[pl.ds(pl.multiple_of(q * 8, 8), 8), :]
            for u in range(8):
                e = e_ref[rows, pl.ds(pl.multiple_of(q * 1024 + u * 128, 128), 128)]
                acc = acc + e * c8[u : u + 1, :]
            return acc

        halves.append(lax.fori_loop(0, GROUPS // 8, body, jnp.zeros((192, 128), f32)))
    return rows_to_lanes(jnp.concatenate(halves, axis=0))


def row_z_kernel(colp_ref, z_ref, e_ref, c_ref, row_ref):
    row = row_pass(colp_ref, e_ref, c_ref)
    both = jnp.concatenate([row, z_ref[...]], axis=0)
    row_ref[...] = jnp.broadcast_to(both, (NP, 2, ROWS))


def row_kernel(colp_ref, e_ref, c_ref, row_ref):
    row = row_pass(colp_ref, e_ref, c_ref)
    row_ref[...] = jnp.broadcast_to(row, (NP, 1, ROWS))


def col_kernel(rowp_ref, e_ref, col_ref, rb):
    rb[...] = lanes_to_rows(1.0 / jnp.sum(rowp_ref[:, 0, :], axis=0, keepdims=True), 128)

    @pl.loop(0, GROUPS // 8)
    def _(q):
        accs = [jnp.zeros((8, 128), f32) for _ in range(8)]
        for i in range(ROWS // 8):
            r = rb[i * 8 : (i + 1) * 8, :]
            e = e_ref[i * 8 : (i + 1) * 8, pl.ds(pl.multiple_of(q * 1024, 1024), 1024)]
            for u in range(8):
                accs[u] = accs[u] + e[:, u * 128 : (u + 1) * 128] * r
        part = jnp.concatenate([jnp.sum(a, axis=0, keepdims=True) for a in accs], axis=0)
        col_ref[:, pl.ds(pl.multiple_of(q * 8, 8), 8), :] = jnp.broadcast_to(part, (NB, 8, 128))


def dz_kernel(rz_ref, c_ref, s_ref, e_ref, p_ref, dz_ref, rb, zb):
    step = pl.program_id(0)

    @pl.when(step == 0)
    def _():
        rb[...] = lanes_to_rows(rz_ref[0:1, :], 128)
        zb[...] = lanes_to_rows(rz_ref[1:2, :], 128)
        dz_ref[...] = jnp.zeros_like(dz_ref)

    c8 = c_ref[pl.ds(pl.multiple_of(step * 8, 8), 8), :]
    r = rb[...]
    z = zb[...]
    acc = dz_ref[...]
    for n in range(4):
        p = p_ref[:, n * 256 : (n + 1) * 256]
        s = jnp.exp2(jnp.dot(s_ref[...], p, preferred_element_type=f32) * KS)
        e = e_ref[:, pl.ds(pl.multiple_of(step * 1024 + n * 256, 256), 256)]
        parts = []
        for h in range(2):
            lane = slice(h * 128, (h + 1) * 128)
            u = n * 2 + h
            parts.append((s[:, lane] * z - e[:, lane] * r * c8[u : u + 1, :]).astype(bf16))
        g = jnp.concatenate(parts, axis=1)
        acc = acc + lax.dot_general(g, p, (((1,), (1,)), ((), ())), preferred_element_type=f32)
    dz_ref[...] = acc


def pg_kernel(rz_ref, c_ref, p_ref, t_ref, s_ref, out_ref, pt, cb, acc):
    step = pl.program_id(0)

    @pl.when(step == 0)
    def _():
        pt[...] = jnp.transpose(p_ref[...].astype(f32)).astype(bf16)
        for q in range(8):
            cb[q * 128 : (q + 1) * 128, :] = lanes_to_rows(c_ref[q : q + 1, :], 128)
        acc[...] = jnp.zeros_like(acc)

    t = t_ref[...]
    s = s_ref[...]
    r = jnp.concatenate([rz_ref[0, 0:1, :], rz_ref[1, 0:1, :]], axis=1)
    z = jnp.concatenate([rz_ref[0, 1:2, :], rz_ref[1, 1:2, :]], axis=1)
    nt = (((1,), (1,)), ((), ()))
    for m in range(4):
        rows = slice(m * 256, (m + 1) * 256)
        pm = pt[rows, :]
        c = cb[rows, :]
        et = jnp.exp2(lax.dot_general(pm, t, nt, preferred_element_type=f32) * KT)
        es = jnp.exp2(lax.dot_general(pm, s, nt, preferred_element_type=f32) * KS)
        parts = []
        for k in range(6):
            lane = slice(k * 128, (k + 1) * 128)
            parts.append((es[:, lane] * z[:, lane] - et[:, lane] * r[:, lane] * c).astype(bf16))
        g = jnp.concatenate(parts, axis=1)
        acc[rows, :] += jnp.dot(g, s, preferred_element_type=f32)

    @pl.when(step == pl.num_programs(0) - 1)
    def _():
        out_ref[...] = jnp.transpose(acc[...])


def in_vmem(x):
    return pltpu.with_memory_space_constraint(x, pltpu.VMEM)


def exchange(x, axes):
    return lax.all_to_all(x, axes, 0, 0, tiled=True)


def sum_over_z(x):
    parts = [x]
    for d in (1, 2, 3):
        parts.append(lax.ppermute(x, "z", [(i, (i + d) % 4) for i in range(4)]))
    return parts


def shards(teacher_feats, student_feats, proto_weight):
    core = lax.axis_index("c")
    block = lax.axis_index("x") * 4 + lax.axis_index("y")
    sds = jax.ShapeDtypeStruct

    teach, stud = pl.pallas_call(
        norm_kernel,
        out_shape=(sds((ROWS, D), bf16), sds((ROWS, D), bf16)),
        in_specs=[whole()] * 2,
        out_specs=(whole(), whole()),
        compiler_params=params(8),
        name="norm",
    )(teacher_feats, student_feats)
    teach_all = lax.all_gather(teach, XY, axis=0, tiled=True)
    stud_all = lax.all_gather(stud, XY, axis=0, tiled=True)

    protos, expo, colp, zpart = pl.pallas_call(
        first_kernel,
        grid=(COLS // 1024,),
        out_shape=(
            sds((D, COLS), bf16),
            pltpu.VMEM((ROWS, COLS), f32),
            sds((NB, GROUPS, 128), f32),
            sds((1, ROWS), f32),
        ),
        in_specs=[pl.BlockSpec((D, 1024), lambda i: (0, i)), whole(), whole()],
        out_specs=(pl.BlockSpec((D, 1024), lambda i: (0, i)), whole(), whole(), whole()),
        scratch_shapes=[pltpu.VMEM((ROWS, 128), f32)],
        compiler_params=params(16),
        name="first",
    )(proto_weight, teach, stud)

    row_out = (sds((GROUPS, 128), f32), sds((NP, 1, ROWS), f32))
    row_out_z = (sds((GROUPS, 128), f32), sds((NP, 2, ROWS), f32))
    for step in range(ITERS):
        colp = exchange(colp, XY)
        if step == 0:
            colsc, rowp = pl.pallas_call(
                row_z_kernel,
                out_shape=row_out_z,
                in_specs=[whole()] * 3,
                out_specs=(whole(), whole()),
                compiler_params=params(8),
                name="row_z",
            )(colp, zpart, in_vmem(expo))
        else:
            colsc, rowp = pl.pallas_call(
                row_kernel,
                out_shape=row_out,
                in_specs=[whole()] * 2,
                out_specs=(whole(), whole()),
                compiler_params=params(8),
                name="row",
            )(colp, in_vmem(expo))
        rowp = exchange(rowp, ZC)
        if step == 0:
            zinv = GSCALE / jnp.sum(rowp[:, 1, :], axis=0, keepdims=True)
        if step < ITERS - 1:
            colp = pl.pallas_call(
                col_kernel,
                out_shape=sds((NB, GROUPS, 128), f32),
                in_specs=[whole()] * 2,
                out_specs=whole(),
                scratch_shapes=[pltpu.VMEM((ROWS, 128), f32)],
                compiler_params=params(8),
                name="col",
            )(rowp, in_vmem(expo))

    rowsc = GSCALE / jnp.sum(rowp[:, 0, :], axis=0, keepdims=True)
    rz = jnp.concatenate([rowsc, zinv], axis=0)
    rz_all = exchange(jnp.broadcast_to(rz[None], (NB, 2, ROWS)), XY)

    dz_part = pl.pallas_call(
        dz_kernel,
        grid=(COLS // 1024,),
        out_shape=sds((ROWS, D), f32),
        in_specs=[whole()] * 4 + [pl.BlockSpec((D, 1024), lambda i: (0, i))],
        out_specs=whole(),
        scratch_shapes=[pltpu.VMEM((ROWS, 128), f32)] * 2,
        compiler_params=params(12),
        name="dz",
    )(rz, colsc, stud, in_vmem(expo), protos)

    half = ROWS // 2
    mine = lax.dynamic_slice(dz_part, (core * half, 0), (half, D))
    other = lax.dynamic_slice(dz_part, ((1 - core) * half, 0), (half, D))
    got = lax.ppermute(other, "c", [(0, 1), (1, 0)])
    parts = sum_over_z(mine + got)

    proto_grad = pl.pallas_call(
        pg_kernel,
        grid=(8,),
        out_shape=sds((D, OWN), f32),
        in_specs=[
            pl.BlockSpec((2, 2, ROWS), lambda i: (i, 0, 0)),
            whole(),
            whole(),
            pl.BlockSpec((2 * ROWS, D), lambda i: (i, 0)),
            pl.BlockSpec((2 * ROWS, D), lambda i: (i, 0)),
        ],
        out_specs=whole(),
        scratch_shapes=[
            pltpu.VMEM((OWN, D), bf16),
            pltpu.VMEM((OWN, 128), f32),
            pltpu.VMEM((OWN, D), f32),
        ],
        compiler_params=params(24),
        cost_estimate=pl.CostEstimate(flops=9700000000, bytes_accessed=8000000, transcendentals=12600000),
        name="pg",
    )(
        rz_all,
        lax.dynamic_slice(colsc, (block * 8, 0), (8, 128)),
        lax.dynamic_slice(protos, (0, block * OWN), (D, OWN)),
        teach_all,
        stud_all,
    )

    dz = (parts[0] + parts[2]) + (parts[1] + parts[3])
    feats = lax.dynamic_slice(student_feats, (core * half, 0), (half, D)).astype(f32)
    rnorm = row_norm(feats)
    stud_f = feats * rnorm
    grad = (dz - stud_f * jnp.sum(stud_f * dz, axis=1, keepdims=True)) * rnorm
    sibling = lax.ppermute(grad, "c", [(0, 1), (1, 0)])
    feat_grad = jnp.where(
        core == 0,
        jnp.concatenate([grad, sibling], axis=0),
        jnp.concatenate([sibling, grad], axis=0),
    )
    return (feat_grad, proto_grad)


def solution(mesh):
    grid = Mesh(mesh.devices.reshape(4, 4, 4, 2), ("x", "y", "z", "c"))
    in_specs = (P(XY, None), P(XY, None), P(None, ZC))
    out_specs = (P(XY, None), P(None, ZC + XY))
    return jax.shard_map(shards, mesh=grid, in_specs=in_specs, out_specs=out_specs, check_vma=False)
```

time: 564 us -> 263 us (0.47)
  waiting for transfers between devices: 377 us -> 35.6 us
  other arithmetic: 77.6 us -> 1.32 us
  Pallas kernels: 0 us -> 64 us
  matrix products: 47.2 us -> 0 us
  blocking collectives: 42.5 us -> 82.2 us
  local copies, waits for them, and re-layouts: 4.57 us -> 43.7 us
  starting transfers between devices: 0.21 us -> 20.8 us
    psum x4 -> x0, waiting for transfers between devices: 265 us -> none  [the longest x3 222 us: shards(): colsc = 1.0 / lax.psum(col_part, 'batch')]
    reduce_scatter x1 -> x0, waiting for transfers between devices: 112 us -> none  [shards(): lax.psum_scatter(term, 'batch', scatter_dimension=1, tiled=True)]
    all_to_all x0 -> x4, blocking collectives: none -> 82.2 us  [exchange(): return lax.all_to_all(x, axes, 0, 0, tiled=True)]
    pallas_call x0 -> x9, Pallas kernels: none -> 64 us  [the longest x1 16.2 us: shards(): pl.pallas_call(first_kernel, grid=(COLS // 1024,), out_shape=(sds((D, COL...]
    reduce_sum x9 -> x4, other arithmetic: 56.6 us -> 0.36 us  [the longest x1 0.19 us: shards(): grad = (dz - stud_f * jnp.sum(stud_f * dz, axis=1, keepdims=True)) * rnorm]
    dot_general x4 -> x0, matrix products: 47.2 us -> none  [the longest x1 14.2 us: shards(): jnp.dot(teach, protos, preferred_element_type=jnp.float32) / 0.07]
    psum x3 -> x0, blocking collectives: 42.5 us -> none  [shards(): rowsc = 1.0 / lax.psum(row_part, 'proto')]
    unnamed x4 -> x22, local copies, waits for them, and re-layouts: 4.57 us -> 41.9 us
  transfers between devices with their start and end apart: 5 -> 10, of which waited for: 5 -> 6; matrix products, arithmetic and copies ran while one was open for 5% -> 1% of each run, Pallas kernels for 0% -> 18%
where the time goes in v1:
time: 263 us; the launch traced here: 262 us
  blocking collectives  82.2 us (31%)
  Pallas kernels  64 us (24%)
  local copies, waits for them, and re-layouts  43.7 us (17%)
  waiting for transfers between devices  35.6 us (14%)
  starting transfers between devices  20.8 us (8%)
  between operations  14.2 us (5%)
    all_to_all x4, blocking collectives, exchange(): return lax.all_to_all(x, axes, 0, 0, tiled=True)  82.2 us
    unnamed x22, local copies, waits for them, and re-layouts  41.9 us
    all_to_all x3, waiting for transfers between devices, exchange(): return lax.all_to_all(x, axes, 0, 0, tiled=True)  25.7 us
    pallas_call x1, Pallas kernels, shards(): pl.pallas_call(first_kernel, grid=(COLS // 1024,), out_shape=(sds((D, COL...  16.2 us
    pallas_call x1, Pallas kernels, shards(): pl.pallas_call(pg_kernel, grid=(8,), out_shape=sds((D, OWN), f32), in_spe...  15.6 us
    all_to_all x3, starting transfers between devices, exchange(): return lax.all_to_all(x, axes, 0, 0, tiled=True)  15.3 us
    pallas_call x1, Pallas kernels, shards(): pl.pallas_call(dz_kernel, grid=(COLS // 1024,), out_shape=sds((ROWS, D),...  13.2 us
    pallas_call x2, Pallas kernels, shards(): pl.pallas_call(row_kernel, out_shape=row_out, in_specs=[whole()] * 2, out...  8.74 us
  transfers between devices with their start and end apart: 10, of which 6 were waited for; matrix products, arithmetic and copies ran while one was open for 1% of the time, Pallas kernels for 18%

profile of v1, /device:TPU:1, one launch (start us, length us, event | category | flops | bytes accessed | tf_op | source)
XLA Modules:
  0.0 261.7 jit_solution(7537047094301094855)
XLA Ops:
  10.8 16.2 %first.1 = (bf16[256,16384]{1,0:T(8,128)(2,1)S(1)}, f32[384,16384]{1,0:T(8,128)S(1)}, f32[16,128,128]{2,1,0:T(8,128)S(1)}, f32[1,384]{1,0:T(1,128)S(1)}) custom-call(bf16[256,16384]{1,0:T(8,128)(2,1)} %w_ref.1, bf16[384,256]{1,0:T(8,128)(2,1)} %get-tuple-element.12.t_ref, bf16[384,256]{1,0:T(8,128)(2,1)} %get-tuple-element.13.s_ref), custom_call_target="tpu_custom_call" | custom-call | tf_op jit(solution)/shard_map/first/pallas_call | solution.py:219
  26.9 8.4 %copy-done = f32[384,16384]{1,0:T(8,128)} copy-done((f32[384,16384]{1,0:T(8,128)}, f32[384,16384]{1,0:T(8,128)S(1)}, u32[]{:S(2)}) %copy-start) | copy-done | bytes 25165848
  35.4 31.5 %all_to_all.35.colp_ref = f32[16,128,128]{2,1,0:T(8,128)S(1)} all-to-all(f32[16,128,128]{2,1,0:T(8,128)S(1)} %get-tuple-element.14), channel_id=1, replica_groups=mesh['x'=4,'y'=4,'z'=4,'c'=2] {'x','y'}, dimensions={0} | all-to-all | bytes 2097152 | tf_op jit(solution)/shard_map/all_to_all | solution.py:193
  66.8 8.2 %copy-done.1 = f32[384,16384]{1,0:T(8,128)S(1)} copy-done((f32[384,16384]{1,0:T(8,128)S(1)}, f32[384,16384]{1,0:T(8,128)}, u32[]{:S(2)}) %copy-start.1) | copy-done | bytes 25165848
  75.0 4.3 %row_z.1 = (f32[128,128]{1,0:T(8,128)}, f32[8,2,384]{2,1,0:T(2,128)S(1)}) custom-call(f32[16,128,128]{2,1,0:T(8,128)S(1)} %all_to_all.35.colp_ref, f32[1,384]{1,0:T(1,128)S(1)} %get-tuple-element.15.z_ref, f32[384,16384]{1,0:T(8,128)S(1)} %copy-done.1), custom_call_target="tpu_custom_call" | custom-call | tf_op jit(solution)/shard_map/row_z/pallas_call | solution.py:240
  79.3 13.5 %all_to_all.36.rowp_ref = f32[8,2,384]{2,1,0:T(2,128)S(1)} all-to-all(f32[8,2,384]{2,1,0:T(2,128)S(1)} %get-tuple-element.17), channel_id=1, replica_groups=mesh['x'=4,'y'=4,'z'=4,'c'=2] {'z','c'}, dimensions={0} | all-to-all | bytes 49152 | tf_op jit(solution)/shard_map/all_to_all | solution.py:193
  94.9 24.8 %all_to_all.37.colp_ref = f32[16,128,128]{2,1,0:T(8,128)S(1)} all-to-all(f32[16,128,128]{2,1,0:T(8,128)S(1)} %col.2), channel_id=1, replica_groups=mesh['x'=4,'y'=4,'z'=4,'c'=2] {'x','y'}, dimensions={0} | all-to-all | bytes 2097152 | tf_op jit(solution)/shard_map/all_to_all | solution.py:193
  119.7 4.3 %row.2 = (f32[128,128]{1,0:T(8,128)}, f32[8,1,384]{2,1,0:T(1,128)S(1)}) custom-call(f32[16,128,128]{2,1,0:T(8,128)S(1)} %all_to_all.37.colp_ref, f32[384,16384]{1,0:T(8,128)S(1)} %copy-done.1), custom_call_target="tpu_custom_call" | custom-call | tf_op jit(solution)/shard_map/row/pallas_call | solution.py:249
  124.0 12.4 %all_to_all.38.rowp_ref = f32[8,1,384]{2,1,0:T(1,128)S(1)} all-to-all(f32[8,1,384]{2,1,0:T(1,128)S(1)} %get-tuple-element.18), channel_id=1, replica_groups=mesh['x'=4,'y'=4,'z'=4,'c'=2] {'z','c'}, dimensions={0} | all-to-all | bytes 24576 | tf_op jit(solution)/shard_map/all_to_all | solution.py:193
  136.4 3.0 %col.3 = f32[16,128,128]{2,1,0:T(8,128)} custom-call(f32[8,1,384]{2,1,0:T(1,128)S(1)} %all_to_all.38.rowp_ref, f32[384,16384]{1,0:T(8,128)S(1)} %copy-done.1), custom_call_target="tpu_custom_call" | custom-call | tf_op jit(solution)/shard_map/col/pallas_call | solution.py:261
  139.4 5.4 %all-to-all-start.4 = ((f32[16,128,128]{2,1,0:T(8,128)}), f32[16,128,128]{2,1,0:T(8,128)S(1)}, u32[]{:S(2)}, u32[]{:S(2)}) async-start(f32[16,128,128]{2,1,0:T(8,128)} %col.3), calls=%async_computation.4 | async-start | bytes 2097152 | tf_op jit(solution)/shard_map/all_to_all | solution.py:193
  144.8 15.4 %all-to-all-done.4.colp_ref = f32[16,128,128]{2,1,0:T(8,128)S(1)} async-done(((f32[16,128,128]{2,1,0:T(8,128)}), f32[16,128,128]{2,1,0:T(8,128)S(1)}, u32[]{:S(2)}, u32[]{:S(2)}) %all-to-all-start.4) | async-done | bytes 1048608 | tf_op jit(solution)/shard_map/all_to_all | solution.py:193
  160.3 8.2 %copy-done.2 = f32[384,16384]{1,0:T(8,128)S(1)} copy-done((f32[384,16384]{1,0:T(8,128)S(1)}, f32[384,16384]{1,0:T(8,128)}, u32[]{:S(2)}) %copy-start.2) | copy-done | bytes 25165848
  168.4 4.4 %row.3 = (f32[128,128]{1,0:T(8,128)S(1)}, f32[8,1,384]{2,1,0:T(1,128)}) custom-call(f32[16,128,128]{2,1,0:T(8,128)S(1)} %all-to-all-done.4.colp_ref, f32[384,16384]{1,0:T(8,128)S(1)} %copy-done.2), custom_call_target="tpu_custom_call" | custom-call | tf_op jit(solution)/shard_map/row/pallas_call | solution.py:249
  172.8 6.4 %all-to-all-start.5 = ((f32[8,1,384]{2,1,0:T(1,128)}), f32[8,1,384]{2,1,0:T(1,128)S(1)}, u32[]{:S(2)}, u32[]{:S(2)}) async-start(f32[8,1,384]{2,1,0:T(1,128)} %get-tuple-element.19), calls=%async_computation.5 | async-start | bytes 24576 | tf_op jit(solution)/shard_map/all_to_all | solution.py:193
  179.3 4.6 %all-to-all-done.5 = f32[8,1,384]{2,1,0:T(1,128)S(1)} async-done(((f32[8,1,384]{2,1,0:T(1,128)}), f32[8,1,384]{2,1,0:T(1,128)S(1)}, u32[]{:S(2)}, u32[]{:S(2)}) %all-to-all-start.5) | async-done | bytes 12320 | tf_op jit(solution)/shard_map/all_to_all | solution.py:193
  184.0 8.1 %copy-done.3 = f32[384,16384]{1,0:T(8,128)S(1)} copy-done((f32[384,16384]{1,0:T(8,128)S(1)}, f32[384,16384]{1,0:T(8,128)}, u32[]{:S(2)}) %copy-start.3) | copy-done | bytes 25165848
  192.1 3.4 %copy-done.5 = bf16[256,16384]{1,0:T(8,128)(2,1)S(1)} copy-done((bf16[256,16384]{1,0:T(8,128)(2,1)S(1)}, bf16[256,16384]{1,0:T(8,128)(2,1)}, u32[]{:S(2)}) %copy-start.5) | copy-done | bytes 8388632
  195.5 13.2 %dz.1 = f32[384,256]{1,0:T(8,128)S(1)} custom-call(f32[2,384]{1,0:T(2,128)S(1)} %pad_maximum_fusion.rz_ref, f32[128,128]{1,0:T(8,128)S(1)} %get-tuple-element.20.c_ref, bf16[384,256]{1,0:T(8,128)(2,1)} %get-tuple-element.13.s_ref, f32[384,16384]{1,0:T(8,128)S(1)} %copy-done.3, bf16[256,16384]{1,0:T(8,128)(2,1)S(1)} %copy-done.5), custom_call_target="tpu_custom_call" | custom-call | tf_op jit(solution)/shard_map/dz/pallas_call | solution.py:275
  213.4 5.0 %collective-permute-done.2 = f32[192,256]{1,0:T(8,128)S(1)} collective-permute-done((f32[192,256]{1,0:T(8,128)S(1)}, f32[192,256]{1,0:T(8,128)S(1)}, u32[]{:S(2)}, u32[]{:S(2)}) %collective-permute-start.2) | collective-permute-done | bytes 196640 | tf_op jit(solution)/shard_map/ppermute | solution.py:199
  218.4 3.3 %collective-permute-done.1 = f32[192,256]{1,0:T(8,128)S(1)} collective-permute-done((f32[192,256]{1,0:T(8,128)S(1)}, f32[192,256]{1,0:T(8,128)S(1)}, u32[]{:S(2)}, u32[]{:S(2)}) %collective-permute-start.1) | collective-permute-done | bytes 196640 | tf_op jit(solution)/shard_map/ppermute | solution.py:199
  225.6 3.5 %all-to-all-start.6 = ((f32[16,2,384]{2,1,0:T(2,128)}), f32[16,2,384]{2,1,0:T(2,128)S(1)}, u32[]{:S(2)}, u32[]{:S(2)}) async-start(f32[16,2,384]{2,1,0:T(2,128)} %broadcast_in_dim.2), calls=%async_computation.6 | async-start | bytes 98304 | tf_op jit(solution)/shard_map/all_to_all | solution.py:193
  229.9 5.6 %all-to-all-done.6.rz_ref = f32[16,2,384]{2,1,0:T(2,128)S(1)} async-done(((f32[16,2,384]{2,1,0:T(2,128)}), f32[16,2,384]{2,1,0:T(2,128)S(1)}, u32[]{:S(2)}, u32[]{:S(2)}) %all-to-all-start.6) | async-done | bytes 49184 | tf_op jit(solution)/shard_map/all_to_all | solution.py:193
  239.3 15.6 %pg.1 = f32[256,1024]{1,0:T(8,128)} custom-call(f32[16,2,384]{2,1,0:T(2,128)S(1)} %all-to-all-done.6.rz_ref, f32[8,128]{1,0:T(8,128)S(1)} %constant_dynamic-slice_fusion.1.c_ref, bf16[256,1024]{1,0:T(8,128)(2,1)S(1)} %constant_dynamic-slice_fusion.p_ref, bf16[6144,256]{1,0:T(8,128)(2,1)S(1)} %copy-done.9, bf16[6144,256]{1,0:T(8,128)(2,1)S(1)} %copy-done.10), custom_call_target="tpu_custom_call" | custom-call | flops 9699999744 | bytes 8000000 | tf_op jit(solution)/shard_map/pg/pallas_call | solution.py:292
  (50 shorter events, 18.9 us)
Async XLA Ops:
  7.2 228.3 %all-gather.3.cloned.1.call-start = ((), (), s32[]{:S(2)}) async-start(), calls=%async_computation.7 | async-start | bytes 3342336 | tf_op jit(solution)/shard_map/all_gather | solution.py:216
  7.2 0.9 copy-start.6
  8.1 0.9 copy-start.8
  10.0 225.5 %all-gather.5.cloned.1.call-start = ((), (), s32[]{:S(2)}) async-start(), calls=%async_computation.8 | async-start | bytes 3342336 | tf_op jit(solution)/shard_map/all_gather | solution.py:217
  26.9 8.4 %copy-start = (f32[384,16384]{1,0:T(8,128)}, f32[384,16384]{1,0:T(8,128)S(1)}, u32[]{:S(2)}) copy-start(f32[384,16384]{1,0:T(8,128)S(1)} %get-tuple-element.16.e_ref) | copy-start | bytes 75497472
  35.4 44.0 %copy-start.4 = (bf16[256,16384]{1,0:T(8,128)(2,1)}, bf16[256,16384]{1,0:T(8,128)(2,1)S(1)}, u32[]{:S(2)}) copy-start(bf16[256,16384]{1,0:T(8,128)(2,1)S(1)} %get-tuple-element.21.p_ref) | copy-start | bytes 25165828
  66.8 8.2 %copy-start.1 = (f32[384,16384]{1,0:T(8,128)S(1)}, f32[384,16384]{1,0:T(8,128)}, u32[]{:S(2)}) copy-start(f32[384,16384]{1,0:T(8,128)} %copy-done) | copy-start | bytes 75497472
  139.4 20.8 %all-to-all-start.4 = ((f32[16,128,128]{2,1,0:T(8,128)}), f32[16,128,128]{2,1,0:T(8,128)S(1)}, u32[]{:S(2)}, u32[]{:S(2)}) async-start(f32[16,128,128]{2,1,0:T(8,128)} %col.3), calls=%async_computation.4 | async-start | bytes 2097152 | tf_op jit(solution)/shard_map/all_to_all | solution.py:193
  160.3 8.2 %copy-start.2 = (f32[384,16384]{1,0:T(8,128)S(1)}, f32[384,16384]{1,0:T(8,128)}, u32[]{:S(2)}) copy-start(f32[384,16384]{1,0:T(8,128)} %copy-done) | copy-start | bytes 75497472
  172.8 11.1 %all-to-all-start.5 = ((f32[8,1,384]{2,1,0:T(1,128)}), f32[8,1,384]{2,1,0:T(1,128)S(1)}, u32[]{:S(2)}, u32[]{:S(2)}) async-start(f32[8,1,384]{2,1,0:T(1,128)} %get-tuple-element.19), calls=%async_computation.5 | async-start | bytes 24576 | tf_op jit(solution)/shard_map/all_to_all | solution.py:193
  184.0 8.2 %copy-start.3 = (f32[384,16384]{1,0:T(8,128)S(1)}, f32[384,16384]{1,0:T(8,128)}, u32[]{:S(2)}) copy-start(f32[384,16384]{1,0:T(8,128)} %copy-done) | copy-start | bytes 75497472
  192.1 3.4 %copy-start.5 = (bf16[256,16384]{1,0:T(8,128)(2,1)S(1)}, bf16[256,16384]{1,0:T(8,128)(2,1)}, u32[]{:S(2)}) copy-start(bf16[256,16384]{1,0:T(8,128)(2,1)} %copy-done.4) | copy-start | bytes 25165828
  195.5 14.0 %copy-start.7 = (bf16[384,256]{1,0:T(8,128)(2,1)S(1)}, bf16[384,256]{1,0:T(8,128)(2,1)}, u32[]{:S(2)}) copy-start(bf16[384,256]{1,0:T(8,128)(2,1)} %s_ref.1) | copy-start | bytes 589828
  208.7 1.9 collective-permute-start
  210.6 7.8 %collective-permute-start.2 = (f32[192,256]{1,0:T(8,128)S(1)}, f32[192,256]{1,0:T(8,128)S(1)}, u32[]{:S(2)}, u32[]{:S(2)}) collective-permute-start(f32[192,256]{1,0:T(8,128)S(1)} %dynamic-slice_add_fusion), channel_id=1, source_target_pairs={{0,2},{2,4},{4,6},{6,0},{1,3},{3,5},{5,7},{7,1},{8,10},{10,12},{12... | collective-permute-start | bytes 589832 | tf_op jit(solution)/shard_map/ppermute | solution.py:199
  211.0 7.4 %collective-permute-start.3 = (f32[192,256]{1,0:T(8,128)S(1)}, f32[192,256]{1,0:T(8,128)S(1)}, u32[]{:S(2)}, u32[]{:S(2)}) collective-permute-start(f32[192,256]{1,0:T(8,128)S(1)} %dynamic-slice_add_fusion), channel_id=1, source_target_pairs={{0,6},{2,0},{4,2},{6,4},{1,7},{3,1},{5,3},{7,5},{8,14},{10,8},{12,... | collective-permute-start | bytes 589832 | tf_op jit(solution)/shard_map/ppermute | solution.py:199
  213.4 8.3 %collective-permute-start.1 = (f32[192,256]{1,0:T(8,128)S(1)}, f32[192,256]{1,0:T(8,128)S(1)}, u32[]{:S(2)}, u32[]{:S(2)}) collective-permute-start(f32[192,256]{1,0:T(8,128)S(1)} %dynamic-slice_add_fusion), channel_id=1, source_target_pairs={{0,4},{2,6},{4,0},{6,2},{1,5},{3,7},{5,1},{7,3},{8,12},{10,14},{12... | collective-permute-start | bytes 589832 | tf_op jit(solution)/shard_map/ppermute | solution.py:199
  222.0 7.1 %collective-permute-start.4 = (f32[192,256]{1,0:T(8,128)S(1)}, f32[192,256]{1,0:T(8,128)S(1)}, u32[]{:S(2)}, u32[]{:S(2)}) collective-permute-start(f32[192,256]{1,0:T(8,128)S(1)} %fusion.4), channel_id=1, source_target_pairs={{0,1},{1,0},{2,3},{3,2},{4,5},{5,4},{6,7},{7,6},{8,9},{9,8},{10,11... | collective-permute-start | bytes 589832 | tf_op jit(solution)/shard_map/ppermute | solution.py:325
  225.6 9.9 %all-to-all-start.6 = ((f32[16,2,384]{2,1,0:T(2,128)}), f32[16,2,384]{2,1,0:T(2,128)S(1)}, u32[]{:S(2)}, u32[]{:S(2)}) async-start(f32[16,2,384]{2,1,0:T(2,128)} %broadcast_in_dim.2), calls=%async_computation.6 | async-start | bytes 98304 | tf_op jit(solution)/shard_map/all_to_all | solution.py:193
  235.5 1.9 copy-start.9
  237.4 1.9 copy-start.10
Sparse Core Ops, SparseCore 0:
  10.2 60.8 all-gather.2
  73.2 54.9 all-gather.4

commit v2 on v1

v2 whole, which is shorter than its diff:
```python
import math

import jax
import jax.numpy as jnp
from jax import lax
from jax.experimental import pallas as pl
from jax.experimental.pallas import tpu as pltpu
from jax.sharding import Mesh, PartitionSpec as P

D = 256
PROTOS = 131072
ITERS = 3
ROWS = 384
COLS = 16384
OWN = 1024
SHARE = 48
BLOCK = 4096
PG_ROWS = 1536
GROUPS = COLS // 128
NB = 16
NP = 8
ND = 128
KT = math.log2(math.e) / 0.07
KS = math.log2(math.e) / 0.1
GSCALE = PROTOS / 0.1

f32 = jnp.float32
bf16 = jnp.bfloat16
XY = ("x", "y")
ZC = ("z", "c")
ALL = XY + ZC
MIB = 2**20


def whole():
    return pl.BlockSpec(memory_space=pltpu.VMEM)


def params(mib):
    return pltpu.CompilerParams(vmem_limit_bytes=mib * MIB)


def row_norm(feats):
    return lax.rsqrt(jnp.mean(feats * feats, axis=1, keepdims=True) + 1e-06) / math.sqrt(D)


def lanes_to_rows(vec, width):
    return jnp.transpose(jnp.broadcast_to(vec, (width, vec.shape[1])))


def rows_to_lanes(acc):
    return jnp.sum(jnp.transpose(acc), axis=0, keepdims=True)


def norm_kernel(t_ref, s_ref, out_ref, share_ref):
    for src, rows in ((t_ref, slice(0, ROWS)), (s_ref, slice(ROWS, 2 * ROWS))):
        feats = src[...].astype(f32)
        out_ref[rows, :] = (feats * row_norm(feats)).astype(bf16)
    start = (lax.axis_index("z") * 2 + lax.axis_index("c")) * SHARE
    for k in range(2):
        rows = pl.ds(pl.multiple_of(k * ROWS + start, SHARE), SHARE)
        share_ref[:, k * D : (k + 1) * D] = out_ref[rows, :]


def first_kernel(w_ref, f_ref, p_ref, e_ref, col_ref, z_ref, zacc):
    step = pl.program_id(0)

    @pl.when(step == 0)
    def _():
        zacc[...] = jnp.zeros_like(zacc)

    sums = []
    zsum = zacc[...]
    for n in range(BLOCK // 256):
        lanes = slice(n * 256, (n + 1) * 256)
        w = w_ref[:, lanes].astype(f32)
        inv = lax.rsqrt(jnp.mean(w * w, axis=0, keepdims=True) + 1e-06) / math.sqrt(D)
        p = (w * inv).astype(bf16)
        p_ref[:, lanes] = p
        x = jnp.dot(f_ref[...], p, preferred_element_type=f32)
        e = jnp.exp2(x[:ROWS] * KT)
        e_ref[:, pl.ds(pl.multiple_of(step * BLOCK + n * 256, 256), 256)] = e
        for h in range(2):
            sums.append(jnp.sum(e[:, h * 128 : (h + 1) * 128], axis=0, keepdims=True))
        s = jnp.exp2(x[ROWS:] * KS)
        zsum = zsum + s[:, :128] + s[:, 128:]
    zacc[...] = zsum
    part = jnp.concatenate(sums, axis=0)
    tall = BLOCK // 128
    col_ref[:, pl.ds(pl.multiple_of(step * tall, tall), tall), :] = jnp.broadcast_to(
        part, (NB, tall, 128)
    )

    @pl.when(step == pl.num_programs(0) - 1)
    def _():
        z_ref[...] = rows_to_lanes(zacc[...])


def row_pass(colp_ref, e_ref, c_ref, acc_ref):
    c_ref[...] = 1.0 / jnp.sum(colp_ref[...], axis=0)
    tiles = 12

    @pl.loop(0, ROWS // (8 * tiles))
    def _(k):
        base = pl.multiple_of(k * 8 * tiles, 8 * tiles)

        def body(q, accs):
            c8 = c_ref[pl.ds(pl.multiple_of(q * 8, 8), 8), :]
            cs = [jnp.broadcast_to(c8[u : u + 1, :], (8, 128)) for u in range(8)]
            out = []
            for i in range(tiles):
                e = e_ref[
                    pl.ds(pl.multiple_of(base + i * 8, 8), 8),
                    pl.ds(pl.multiple_of(q * 1024, 1024), 1024),
                ]
                p = [e[:, u * 128 : (u + 1) * 128] * cs[u] for u in range(8)]
                while len(p) > 1:
                    p = [p[m] + p[m + 1] for m in range(0, len(p), 2)]
                out.append(accs[i] + p[0])
            return tuple(out)

        zero = jnp.zeros((8, 128), f32)
        accs = lax.fori_loop(0, GROUPS // 8, body, (zero,) * tiles)
        for i in range(tiles):
            acc_ref[pl.ds(pl.multiple_of(base + i * 8, 8), 8), :] = accs[i]

    return rows_to_lanes(acc_ref[...])


def last_row_kernel(colp_ref, z_ref, e_ref, c_ref, row_ref, kept_ref, acc):
    row = row_pass(colp_ref, e_ref, c_ref, acc)
    both = jnp.concatenate([row, z_ref[...]], axis=0)
    row_ref[...] = jnp.broadcast_to(both, (ND, 2, ROWS))


def row_kernel(colp_ref, e_ref, c_ref, row_ref, kept_ref, acc):
    row = row_pass(colp_ref, e_ref, c_ref, acc)
    row_ref[...] = jnp.broadcast_to(row, (NP, 1, ROWS))


def col_kernel(rowp_ref, e_ref, col_ref, kept_ref, rb):
    rb[...] = lanes_to_rows(1.0 / jnp.sum(rowp_ref[:, 0, :], axis=0, keepdims=True), 128)

    @pl.loop(0, GROUPS // 8)
    def _(q):
        accs = [jnp.zeros((8, 128), f32) for _ in range(8)]
        for i in range(ROWS // 8):
            r = rb[i * 8 : (i + 1) * 8, :]
            e = e_ref[i * 8 : (i + 1) * 8, pl.ds(pl.multiple_of(q * 1024, 1024), 1024)]
            for u in range(8):
                accs[u] = accs[u] + e[:, u * 128 : (u + 1) * 128] * r
        part = jnp.concatenate([jnp.sum(a, axis=0, keepdims=True) for a in accs], axis=0)
        col_ref[:, pl.ds(pl.multiple_of(q * 8, 8), 8), :] = jnp.broadcast_to(part, (NB, 8, 128))


def dz_kernel(rzp_ref, c_ref, f_ref, e_ref, p_ref, mine_ref, other_ref, rz_ref, rb, zb, dz_ref):
    step = pl.program_id(0)

    @pl.when(step == 0)
    def _():
        block = lax.axis_index("x") * 4 + lax.axis_index("y")
        for b in range(NB):
            rz_ref[b] = GSCALE / jnp.sum(rzp_ref[b * NP : (b + 1) * NP], axis=0)
        rz = rz_ref[block]
        rb[...] = lanes_to_rows(rz[0:1, :], 128)
        zb[...] = lanes_to_rows(rz[1:2, :], 128)
        dz_ref[...] = jnp.zeros_like(dz_ref)

    tall = BLOCK // 128
    cs = c_ref[pl.ds(pl.multiple_of(step * tall, tall), tall), :]
    r = rb[...]
    z = zb[...]
    acc = dz_ref[...]
    for n in range(BLOCK // 256):
        p = p_ref[:, n * 256 : (n + 1) * 256]
        s = jnp.exp2(jnp.dot(f_ref[ROWS:, :], p, preferred_element_type=f32) * KS)
        e = e_ref[:, pl.ds(pl.multiple_of(step * BLOCK + n * 256, 256), 256)]
        parts = []
        for h in range(2):
            lane = slice(h * 128, (h + 1) * 128)
            u = n * 2 + h
            parts.append((s[:, lane] * z - e[:, lane] * r * cs[u : u + 1, :]).astype(bf16))
        g = jnp.concatenate(parts, axis=1)
        acc = acc + lax.dot_general(g, p, (((1,), (1,)), ((), ())), preferred_element_type=f32)
    dz_ref[...] = acc

    @pl.when(step == pl.num_programs(0) - 1)
    def _():
        half = ROWS // 2
        core = lax.axis_index("c")
        mine_ref[...] = dz_ref[pl.ds(pl.multiple_of(core * half, half), half), :]
        other_ref[...] = dz_ref[pl.ds(pl.multiple_of((1 - core) * half, half), half), :]


def pg_kernel(block_ref, rz_ref, c_ref, p_ref, f_ref, out_ref, pt, cb, acc, g):
    step = pl.program_id(0)

    @pl.when(step == 0)
    def _():
        pt[...] = jnp.transpose(p_ref[...].astype(f32)).astype(bf16)
        for q in range(8):
            cb[q * 128 : (q + 1) * 128, :] = lanes_to_rows(c_ref[q : q + 1, :], 128)
        acc[...] = jnp.zeros_like(acc)

    t = f_ref[:, :D]
    s = f_ref[:, D:]
    blocks = range(PG_ROWS // ROWS)
    r = jnp.concatenate([rz_ref[b, 0:1, :] for b in blocks], axis=1)
    z = jnp.concatenate([rz_ref[b, 1:2, :] for b in blocks], axis=1)
    nt = (((1,), (1,)), ((), ()))
    for n in range(PG_ROWS // 256):
        rows = slice(n * 256, (n + 1) * 256)
        et = jnp.exp2(lax.dot_general(pt[...], t[rows], nt, preferred_element_type=f32) * KT)
        es = jnp.exp2(lax.dot_general(pt[...], s[rows], nt, preferred_element_type=f32) * KS)
        for h in range(2):
            lane = slice(h * 128, (h + 1) * 128)
            to = slice(n * 256 + h * 128, n * 256 + (h + 1) * 128)
            g[:, to] = (es[:, lane] * z[:, to] - et[:, lane] * r[:, to] * cb[...]).astype(bf16)
    acc[...] += jnp.dot(g[...], s, preferred_element_type=f32)

    @pl.when(step == pl.num_programs(0) - 1)
    def _():
        out_ref[...] = jnp.transpose(acc[...])


def in_vmem(x):
    return pltpu.with_memory_space_constraint(x, pltpu.VMEM)


def in_hbm(x):
    return pltpu.with_memory_space_constraint(x, pltpu.HBM)


def exchange(x, axes):
    return lax.all_to_all(x, axes, 0, 0, tiled=True)


def sum_over_z(x):
    parts = [x]
    for d in (1, 2, 3):
        parts.append(lax.ppermute(x, "z", [(i, (i + d) % 4) for i in range(4)]))
    return parts


def shards(teacher_feats, student_feats, proto_weight):
    core = lax.axis_index("c")
    block = lax.axis_index("x") * 4 + lax.axis_index("y")
    sds = jax.ShapeDtypeStruct
    vmem = pltpu.VMEM
    kept = vmem((ROWS, COLS), f32)

    feats, share = pl.pallas_call(
        norm_kernel,
        grid=(1,),
        out_shape=(vmem((2 * ROWS, D), bf16), sds((SHARE, 2 * D), bf16)),
        in_specs=[pl.BlockSpec((ROWS, D), lambda i: (0, 0))] * 2,
        out_specs=(whole(), whole()),
        compiler_params=params(14),
        name="norm",
    )(in_hbm(teacher_feats), in_hbm(student_feats))
    feats_all = lax.all_gather(share, ALL, axis=0, tiled=True)

    protos, expo, colp, zpart = pl.pallas_call(
        first_kernel,
        grid=(COLS // BLOCK,),
        out_shape=(
            pltpu.HBM((D, COLS), bf16),
            kept,
            vmem((NB, GROUPS, 128), f32),
            vmem((1, ROWS), f32),
        ),
        in_specs=[pl.BlockSpec((D, BLOCK), lambda i: (0, i)), whole()],
        out_specs=(pl.BlockSpec((D, BLOCK), lambda i: (0, i)), whole(), whole(), whole()),
        scratch_shapes=[vmem((ROWS, 128), f32)],
        compiler_params=params(14),
        name="first",
    )(in_hbm(proto_weight), in_vmem(feats))

    for step in range(ITERS):
        colp = in_vmem(exchange(colp, XY))
        if step == ITERS - 1:
            break
        unused, rowp, expo = pl.pallas_call(
            row_kernel,
            out_shape=(vmem((GROUPS, 128), f32), vmem((NP, 1, ROWS), f32), kept),
            in_specs=[whole()] * 2,
            out_specs=(whole(),) * 3,
            input_output_aliases={1: 2},
            scratch_shapes=[vmem((ROWS, 128), f32)],
            compiler_params=params(14),
            name="row",
        )(colp, in_vmem(expo))
        rowp = in_vmem(exchange(rowp, ZC))
        colp, expo = pl.pallas_call(
            col_kernel,
            out_shape=(vmem((NB, GROUPS, 128), f32), kept),
            in_specs=[whole()] * 2,
            out_specs=(whole(), whole()),
            input_output_aliases={1: 1},
            scratch_shapes=[vmem((ROWS, 128), f32)],
            compiler_params=params(14),
            name="col",
        )(rowp, in_vmem(expo))

    colsc, rzp, expo = pl.pallas_call(
        last_row_kernel,
        out_shape=(vmem((GROUPS, 128), f32), vmem((ND, 2, ROWS), f32), kept),
        in_specs=[whole()] * 3,
        out_specs=(whole(),) * 3,
        input_output_aliases={2: 2},
        scratch_shapes=[vmem((ROWS, 128), f32)],
        compiler_params=params(14),
        name="row_last",
    )(colp, in_vmem(zpart), in_vmem(expo))
    rzp = in_vmem(exchange(rzp, ALL))

    half = ROWS // 2
    mine, other, rz_all = pl.pallas_call(
        dz_kernel,
        grid=(COLS // BLOCK,),
        out_shape=(vmem((half, D), f32), vmem((half, D), f32), sds((NB, 2, ROWS), f32)),
        in_specs=[whole()] * 4 + [pl.BlockSpec((D, BLOCK), lambda i: (0, i))],
        out_specs=(whole(), whole(), whole()),
        scratch_shapes=[vmem((ROWS, 128), f32)] * 2 + [vmem((ROWS, D), f32)],
        compiler_params=params(14),
        name="dz",
    )(rzp, in_vmem(colsc), in_vmem(feats), in_vmem(expo), in_hbm(protos))

    got = lax.ppermute(other, "c", [(0, 1), (1, 0)])
    parts = sum_over_z(mine + got)

    proto_grad = pl.pallas_call(
        pg_kernel,
        grid_spec=pltpu.PrefetchScalarGridSpec(
            num_scalar_prefetch=1,
            grid=(NB * ROWS // PG_ROWS,),
            in_specs=[
                pl.BlockSpec((PG_ROWS // ROWS, 2, ROWS), lambda i, b: (i, 0, 0)),
                pl.BlockSpec((8, 128), lambda i, b: (b[0], 0)),
                pl.BlockSpec((D, OWN), lambda i, b: (0, b[0])),
                pl.BlockSpec((PG_ROWS, 2 * D), lambda i, b: (i, 0)),
            ],
            out_specs=pl.BlockSpec((D, OWN), lambda i, b: (0, 0)),
            scratch_shapes=[
                vmem((OWN, D), bf16),
                vmem((OWN, 128), f32),
                vmem((OWN, D), f32),
                vmem((OWN, PG_ROWS), bf16),
            ],
        ),
        out_shape=sds((D, OWN), f32),
        compiler_params=params(14),
        cost_estimate=pl.CostEstimate(flops=9700000000, bytes_accessed=8000000, transcendentals=12600000),
        name="pg",
    )(block.reshape(1), rz_all, colsc, in_hbm(protos), in_hbm(feats_all))

    parts, proto_grad, student_feats = lax.optimization_barrier(
        (parts, proto_grad, student_feats)
    )
    dz = (parts[0] + parts[2]) + (parts[1] + parts[3])
    feats = lax.dynamic_slice(student_feats, (core * half, 0), (half, D)).astype(f32)
    rnorm = row_norm(feats)
    stud_f = feats * rnorm
    grad = (dz - stud_f * jnp.sum(stud_f * dz, axis=1, keepdims=True)) * rnorm
    sibling = lax.ppermute(grad, "c", [(0, 1), (1, 0)])
    feat_grad = jnp.where(
        core == 0,
        jnp.concatenate([grad, sibling], axis=0),
        jnp.concatenate([sibling, grad], axis=0),
    )
    return (feat_grad, proto_grad)


def solution(mesh):
    grid = Mesh(mesh.devices.reshape(4, 4, 4, 2), ("x", "y", "z", "c"))
    in_specs = (P(XY, None), P(XY, None), P(None, ZC))
    out_specs = (P(XY, None), P(None, ZC + XY))
    return jax.shard_map(shards, mesh=grid, in_specs=in_specs, out_specs=out_specs, check_vma=False)
```

time: 263 us -> 190 us (0.72)
  local copies, waits for them, and re-layouts: 43.7 us -> 0.68 us
  waiting for transfers between devices: 35.6 us -> 2.38 us
  blocking collectives: 82.2 us -> 109 us
  starting transfers between devices: 20.8 us -> 4.95 us
  Pallas kernels: 64 us -> 56.8 us
    unnamed x22 -> x4, local copies, waits for them, and re-layouts: 41.9 us -> 0.68 us
    all_to_all x4 -> x6, blocking collectives: 82.2 us -> 109 us  [exchange(): return lax.all_to_all(x, axes, 0, 0, tiled=True)]
    all_to_all x3 -> x0, waiting for transfers between devices: 25.7 us -> none  [exchange(): return lax.all_to_all(x, axes, 0, 0, tiled=True)]
    all_to_all x3 -> x0, starting transfers between devices: 15.3 us -> none  [exchange(): return lax.all_to_all(x, axes, 0, 0, tiled=True)]
    ppermute x3, waiting for transfers between devices: 8.26 us -> 0.01 us  [sum_over_z(): parts.append(lax.ppermute(x, 'z', [(i, (i + d) % 4) for i in range(4)]))]
    pallas_call x9, Pallas kernels: 64 us -> 56.8 us  [the longest x1 16.3 us: shards(): pl.pallas_call(pg_kernel, grid_spec=pltpu.PrefetchScalarGridSpec(num_scal...]
  transfers between devices with their start and end apart: 10 -> 6, of which waited for: 6 -> 2; matrix products, arithmetic and copies ran while one was open for 1% -> 1% of each run, Pallas kernels for 18% -> 29%
where the time goes in v2:
time: 190 us
  blocking collectives  109 us (57%)
  Pallas kernels  56.8 us (30%)
  between operations  14.1 us (7%)
  starting transfers between devices  4.95 us (3%)
  waiting for transfers between devices  2.38 us (1%)
  other arithmetic  2.18 us (1%)
    all_to_all x6, blocking collectives, exchange(): return lax.all_to_all(x, axes, 0, 0, tiled=True)  109 us
    pallas_call x1, Pallas kernels, shards(): pl.pallas_call(pg_kernel, grid_spec=pltpu.PrefetchScalarGridSpec(num_scal...  16.3 us
    pallas_call x1, Pallas kernels, shards(): pl.pallas_call(first_kernel, grid=(COLS // BLOCK,), out_shape=(pltpu.HBM(...  14.4 us
    pallas_call x1, Pallas kernels, shards(): pl.pallas_call(dz_kernel, grid=(COLS // BLOCK,), out_shape=(vmem((half, D...  11.3 us
    pallas_call x2, Pallas kernels, shards(): pl.pallas_call(row_kernel, out_shape=(vmem((GROUPS, 128), f32), vmem((NP,...  5.92 us
    pallas_call x2, Pallas kernels, shards(): pl.pallas_call(col_kernel, out_shape=(vmem((NB, GROUPS, 128), f32), kept)...  4.49 us
  transfers between devices with their start and end apart: 6, of which 2 were waited for; matrix products, arithmetic and copies ran while one was open for 1% of the time, Pallas kernels for 29%

profile of v2, /device:TPU:1, one launch (start us, length us, event | category | flops | bytes accessed | tf_op | source)
XLA Modules:
  0.0 189.6 jit_solution(8388285281842317123)
XLA Ops:
  7.2 1.8 norm.1
  9.1 14.4 %first.1 = (bf16[256,16384]{1,0:T(8,128)(2,1)}, f32[384,16384]{1,0:T(8,128)S(1)}, f32[16,128,128]{2,1,0:T(8,128)S(1)}, f32[1,384]{1,0:T(1,128)S(1)}) custom-call(bf16[256,16384]{1,0:T(8,128)(2,1)} %w_ref.1, bf16[768,256]{1,0:T(8,128)(2,1)S(1)} %get-tuple-element.28.f_ref), custom_call_target="tpu_custom_call" | custom-call | tf_op jit(solution)/shard_map/first/pallas_call | solution.py:263
  23.5 23.5 %all_to_all.30.colp_ref = f32[16,128,128]{2,1,0:T(8,128)S(1)} all-to-all(f32[16,128,128]{2,1,0:T(8,128)S(1)} %get-tuple-element.29), channel_id=1, replica_groups=mesh['x'=4,'y'=4,'z'=4,'c'=2] {'x','y'}, dimensions={0} | all-to-all | bytes 2097152 | tf_op jit(solution)/shard_map/all_to_all | solution.py:235
  47.0 3.0 %row.2 = (f32[128,128]{1,0:T(8,128)}, f32[8,1,384]{2,1,0:T(1,128)S(1)}, f32[384,16384]{1,0:T(8,128)S(1)}) custom-call(f32[16,128,128]{2,1,0:T(8,128)S(1)} %all_to_all.30.colp_ref, f32[384,16384]{1,0:T(8,128)S(1)} %get-tuple-element.30.e_ref), custom_call_target="tpu_custom_call", output_to_operand_aliasing={{2}: (1, {})} | custom-call | tf_op jit(solution)/shard_map/row/pallas_call | solution.py:283
  50.0 11.6 %all_to_all.31.rowp_ref = f32[8,1,384]{2,1,0:T(1,128)S(1)} all-to-all(f32[8,1,384]{2,1,0:T(1,128)S(1)} %get-tuple-element.31), channel_id=1, replica_groups=mesh['x'=4,'y'=4,'z'=4,'c'=2] {'z','c'}, dimensions={0} | all-to-all | bytes 24576 | tf_op jit(solution)/shard_map/all_to_all | solution.py:235
  61.6 2.2 %col.2 = (f32[16,128,128]{2,1,0:T(8,128)S(1)}, f32[384,16384]{1,0:T(8,128)S(1)}) custom-call(f32[8,1,384]{2,1,0:T(1,128)S(1)} %all_to_all.31.rowp_ref, f32[384,16384]{1,0:T(8,128)S(1)} %get-tuple-element.32.e_ref), custom_call_target="tpu_custom_call", output_to_operand_aliasing={{1}: (1, {})} | custom-call | tf_op jit(solution)/shard_map/col/pallas_call | solution.py:294
  63.8 27.0 %all_to_all.32.colp_ref = f32[16,128,128]{2,1,0:T(8,128)S(1)} all-to-all(f32[16,128,128]{2,1,0:T(8,128)S(1)} %get-tuple-element.33), channel_id=1, replica_groups=mesh['x'=4,'y'=4,'z'=4,'c'=2] {'x','y'}, dimensions={0} | all-to-all | bytes 2097152 | tf_op jit(solution)/shard_map/all_to_all | solution.py:235
  90.8 3.0 %row.3 = (f32[128,128]{1,0:T(8,128)}, f32[8,1,384]{2,1,0:T(1,128)S(1)}, f32[384,16384]{1,0:T(8,128)S(1)}) custom-call(f32[16,128,128]{2,1,0:T(8,128)S(1)} %all_to_all.32.colp_ref, f32[384,16384]{1,0:T(8,128)S(1)} %get-tuple-element.34.e_ref), custom_call_target="tpu_custom_call", output_to_operand_aliasing={{2}: (1, {})} | custom-call | tf_op jit(solution)/shard_map/row/pallas_call | solution.py:283
  93.8 8.6 %all_to_all.33.rowp_ref = f32[8,1,384]{2,1,0:T(1,128)S(1)} all-to-all(f32[8,1,384]{2,1,0:T(1,128)S(1)} %get-tuple-element.35), channel_id=1, replica_groups=mesh['x'=4,'y'=4,'z'=4,'c'=2] {'z','c'}, dimensions={0} | all-to-all | bytes 24576 | tf_op jit(solution)/shard_map/all_to_all | solution.py:235
  102.3 2.2 %col.3 = (f32[16,128,128]{2,1,0:T(8,128)S(1)}, f32[384,16384]{1,0:T(8,128)S(1)}) custom-call(f32[8,1,384]{2,1,0:T(1,128)S(1)} %all_to_all.33.rowp_ref, f32[384,16384]{1,0:T(8,128)S(1)} %get-tuple-element.36.e_ref), custom_call_target="tpu_custom_call", output_to_operand_aliasing={{1}: (1, {})} | custom-call | tf_op jit(solution)/shard_map/col/pallas_call | solution.py:294
  104.6 20.0 %all_to_all.34.colp_ref = f32[16,128,128]{2,1,0:T(8,128)S(1)} all-to-all(f32[16,128,128]{2,1,0:T(8,128)S(1)} %get-tuple-element.37), channel_id=1, replica_groups=mesh['x'=4,'y'=4,'z'=4,'c'=2] {'x','y'}, dimensions={0} | all-to-all | bytes 2097152 | tf_op jit(solution)/shard_map/all_to_all | solution.py:235
  124.6 2.5 %row_last.1 = (f32[128,128]{1,0:T(8,128)S(1)}, f32[128,2,384]{2,1,0:T(2,128)S(1)}, f32[384,16384]{1,0:T(8,128)S(1)}) custom-call(f32[16,128,128]{2,1,0:T(8,128)S(1)} %all_to_all.34.colp_ref, f32[1,384]{1,0:T(1,128)S(1)} %get-tuple-element.38.z_ref, f32[384,16384]{1,0:T(8,128)S(1)} %get-tuple-element.39.e_ref), custom_call_target="tpu_custom_call", output_to_operand_aliasing={{2}: (2, {})} | custom-call | tf_op jit(solution)/shard_map/row_last/pallas_call | solution.py:305
  127.1 17.9 %all_to_all.35.rzp_ref = f32[128,2,384]{2,1,0:T(2,128)S(1)} all-to-all(f32[128,2,384]{2,1,0:T(2,128)S(1)} %get-tuple-element.40), channel_id=1, replica_groups=mesh['x'=4,'y'=4,'z'=4,'c'=2] {'x','y','z','c'}, dimensions={0} | all-to-all | bytes 786432 | tf_op jit(solution)/shard_map/all_to_all | solution.py:235
  145.0 11.3 %dz.1 = (f32[192,256]{1,0:T(8,128)S(1)}, f32[192,256]{1,0:T(8,128)}, f32[16,2,384]{2,1,0:T(2,128)S(1)}) custom-call(f32[128,2,384]{2,1,0:T(2,128)S(1)} %all_to_all.35.rzp_ref, f32[128,128]{1,0:T(8,128)S(1)} %get-tuple-element.41.c_ref, bf16[768,256]{1,0:T(8,128)(2,1)S(1)} %get-tuple-element.28.f_ref, f32[384,16384]{1,0:T(8,128)S(1)} %get-tuple-element.42.e_ref, ...), custom_call_target="tpu_custom_call" | custom-call | tf_op jit(solution)/shard_map/dz/pallas_call | solution.py:318
  156.3 0.7 copy-done
  157.0 1.2 collective-permute-start
  158.2 1.3 collective-permute-done
  159.4 1.0 add.29
  160.5 1.4 collective-permute-start.2
  161.8 1.3 collective-permute-start.3
  163.1 16.3 %pg.1 = f32[256,1024]{1,0:T(8,128)} custom-call(s32[1]{0:T(128)} %bitcast.block_ref, f32[16,2,384]{2,1,0:T(2,128)S(1)} %get-tuple-element.46.rz_ref, f32[128,128]{1,0:T(8,128)S(1)} %get-tuple-element.41.c_ref, bf16[256,16384]{1,0:T(8,128)(2,1)} %get-tuple-element.43.p_ref, bf16[6144,512]{1,0:T(8,128)(2,1)} %all-gather.2.cloned.1.call-done.f_ref), custom_call_target="tpu_custom_call" | custom-call | flops 9699999744 | bytes 8000000 | tf_op jit(solution)/shard_map/pg/pallas_call | solution.py:332
  179.9 1.0 collective-permute-start.4
  180.9 1.1 collective-permute-done.4
  182.0 0.8 maximum_select_fusion
  (14 shorter events, 0.6 us)
Async XLA Ops:
  7.2 156.0 %all-gather.2.cloned.1.call-start = ((), (), s32[]{:S(2)}) async-start(), calls=%async_computation.6 | async-start | bytes 6340608 | tf_op jit(solution)/shard_map/all_gather | solution.py:261
  156.3 0.7 copy-start
  157.0 22.5 %copy-start.1 = (bf16[384,256]{1,0:T(8,128)(2,1)S(1)}, bf16[384,256]{1,0:T(8,128)(2,1)}, u32[]{:S(2)}) copy-start(bf16[384,256]{1,0:T(8,128)(2,1)} %s_ref.1) | copy-start | bytes 589828
  157.0 2.4 %collective-permute-start = (f32[192,256]{1,0:T(8,128)}, f32[192,256]{1,0:T(8,128)S(1)}, u32[]{:S(2)}, u32[]{:S(2)}) collective-permute-start(f32[192,256]{1,0:T(8,128)} %get-tuple-element.45), channel_id=1, source_target_pairs={{0,1},{1,0},{2,3},{3,2},{4,5},{5,4},{6,7},{7,6},{8,9},{9,8},{10,11... | collective-permute-start | bytes 589832 | tf_op jit(solution)/shard_map/ppermute | solution.py:329
  160.4 19.0 %collective-permute-start.1 = (f32[192,256]{1,0:T(8,128)S(1)}, f32[192,256]{1,0:T(8,128)S(1)}, u32[]{:S(2)}, u32[]{:S(2)}) collective-permute-start(f32[192,256]{1,0:T(8,128)S(1)} %add.29), channel_id=1, source_target_pairs={{0,2},{2,4},{4,6},{6,0},{1,3},{3,5},{5,7},{7,1},{8,10},{10,12},{12... | collective-permute-start | bytes 589832 | tf_op jit(solution)/shard_map/ppermute | solution.py:241
  160.5 19.0 %collective-permute-start.2 = (f32[192,256]{1,0:T(8,128)S(1)}, f32[192,256]{1,0:T(8,128)S(1)}, u32[]{:S(2)}, u32[]{:S(2)}) collective-permute-start(f32[192,256]{1,0:T(8,128)S(1)} %add.29), channel_id=1, source_target_pairs={{0,4},{2,6},{4,0},{6,2},{1,5},{3,7},{5,1},{7,3},{8,12},{10,14},{12... | collective-permute-start | bytes 589832 | tf_op jit(solution)/shard_map/ppermute | solution.py:241
  161.8 17.6 %collective-permute-start.3 = (f32[192,256]{1,0:T(8,128)S(1)}, f32[192,256]{1,0:T(8,128)S(1)}, u32[]{:S(2)}, u32[]{:S(2)}) collective-permute-start(f32[192,256]{1,0:T(8,128)S(1)} %add.29), channel_id=1, source_target_pairs={{0,6},{2,0},{4,2},{6,4},{1,7},{3,1},{5,3},{7,5},{8,14},{10,8},{12,... | collective-permute-start | bytes 589832 | tf_op jit(solution)/shard_map/ppermute | solution.py:241
  179.9 2.1 %collective-permute-start.4 = (f32[192,256]{1,0:T(8,128)S(1)}, f32[192,256]{1,0:T(8,128)S(1)}, u32[]{:S(2)}, u32[]{:S(2)}) collective-permute-start(f32[192,256]{1,0:T(8,128)S(1)} %fusion.4), channel_id=1, source_target_pairs={{0,1},{1,0},{2,3},{3,2},{4,5},{5,4},{6,7},{7,6},{8,9},{9,8},{10,11... | collective-permute-start | bytes 589832 | tf_op jit(solution)/shard_map/ppermute | solution.py:365
Sparse Core Ops, SparseCore 0:
  11.0 82.2 all-gather.1

commit v3 on v2

--- a/solution.py
+++ b/solution.py
@@ -18,8 +18,6 @@
 PG_ROWS = 1536
 GROUPS = COLS // 128
 NB = 16
-NP = 8
-ND = 128
 KT = math.log2(math.e) / 0.07
 KS = math.log2(math.e) / 0.1
 GSCALE = PROTOS / 0.1
@@ -62,42 +60,66 @@
         share_ref[:, k * D : (k + 1) * D] = out_ref[rows, :]
 
 
-def first_kernel(w_ref, f_ref, p_ref, e_ref, col_ref, z_ref, zacc):
+def first_kernel(w_ref, f_ref, p_ref, e_ref, col_ref):
     step = pl.program_id(0)
-
-    @pl.when(step == 0)
-    def _():
-        zacc[...] = jnp.zeros_like(zacc)
-
     sums = []
-    zsum = zacc[...]
     for n in range(BLOCK // 256):
         lanes = slice(n * 256, (n + 1) * 256)
         w = w_ref[:, lanes].astype(f32)
         inv = lax.rsqrt(jnp.mean(w * w, axis=0, keepdims=True) + 1e-06) / math.sqrt(D)
         p = (w * inv).astype(bf16)
         p_ref[:, lanes] = p
-        x = jnp.dot(f_ref[...], p, preferred_element_type=f32)
-        e = jnp.exp2(x[:ROWS] * KT)
+        e = jnp.exp2(jnp.dot(f_ref[:ROWS, :], p, preferred_element_type=f32) * KT)
         e_ref[:, pl.ds(pl.multiple_of(step * BLOCK + n * 256, 256), 256)] = e
         for h in range(2):
             sums.append(jnp.sum(e[:, h * 128 : (h + 1) * 128], axis=0, keepdims=True))
-        s = jnp.exp2(x[ROWS:] * KS)
+    tall = BLOCK // 128
+    col_ref[pl.ds(pl.multiple_of(step * tall, tall), tall), :] = jnp.concatenate(sums, axis=0)
+
+
+def z_kernel(after_ref, f_ref, p_ref, z_ref, zacc):
+    step = pl.program_id(0)
+
+    @pl.when(step == 0)
+    def _():
+        zacc[...] = jnp.zeros_like(zacc)
+
+    zsum = zacc[...]
+    for n in range(BLOCK // 256):
+        p = p_ref[:, n * 256 : (n + 1) * 256]
+        s = jnp.exp2(jnp.dot(f_ref[ROWS:, :], p, preferred_element_type=f32) * KS)
         zsum = zsum + s[:, :128] + s[:, 128:]
     zacc[...] = zsum
-    part = jnp.concatenate(sums, axis=0)
-    tall = BLOCK // 128
-    col_ref[:, pl.ds(pl.multiple_of(step * tall, tall), tall), :] = jnp.broadcast_to(
-        part, (NB, tall, 128)
-    )
 
     @pl.when(step == pl.num_programs(0) - 1)
     def _():
         z_ref[...] = rows_to_lanes(zacc[...])
 
 
-def row_pass(colp_ref, e_ref, c_ref, acc_ref):
-    c_ref[...] = 1.0 / jnp.sum(colp_ref[...], axis=0)
+def sum_kernel(a_ref, b_ref, c_ref, d_ref, out_ref):
+    out_ref[...] = (a_ref[...] + b_ref[...]) + (c_ref[...] + d_ref[...])
+
+
+def pair_kernel(a_ref, b_ref, out_ref):
+    out_ref[...] = a_ref[...] + b_ref[...]
+
+
+def rz_kernel(a_ref, b_ref, c_ref, d_ref, out_ref):
+    out_ref[...] = GSCALE / ((a_ref[...] + b_ref[...]) + (c_ref[...] + d_ref[...]))
+
+
+def stack_kernel(a_ref, b_ref, c_ref, d_ref, other_ref, out_ref, kept_ref):
+    for d, ref in enumerate((a_ref, b_ref, c_ref, d_ref)):
+        out_ref[d] = ref[...]
+
+
+def sum_z_kernel(a_ref, b_ref, c_ref, d_ref, z_ref, out_ref, z_out):
+    out_ref[...] = (a_ref[...] + b_ref[...]) + (c_ref[...] + d_ref[...])
+    z_out[...] = z_ref[...]
+
+
+def row_pass(cols, e_ref, c_ref, acc_ref):
+    c_ref[...] = 1.0 / ((cols[0][...] + cols[1][...]) + (cols[2][...] + cols[3][...]))
     tiles = 12
 
     @pl.loop(0, ROWS // (8 * tiles))
@@ -127,19 +149,19 @@
     return rows_to_lanes(acc_ref[...])
 
 
-def last_row_kernel(colp_ref, z_ref, e_ref, c_ref, row_ref, kept_ref, acc):
-    row = row_pass(colp_ref, e_ref, c_ref, acc)
-    both = jnp.concatenate([row, z_ref[...]], axis=0)
-    row_ref[...] = jnp.broadcast_to(both, (ND, 2, ROWS))
-
-
-def row_kernel(colp_ref, e_ref, c_ref, row_ref, kept_ref, acc):
-    row = row_pass(colp_ref, e_ref, c_ref, acc)
-    row_ref[...] = jnp.broadcast_to(row, (NP, 1, ROWS))
-
-
-def col_kernel(rowp_ref, e_ref, col_ref, kept_ref, rb):
-    rb[...] = lanes_to_rows(1.0 / jnp.sum(rowp_ref[:, 0, :], axis=0, keepdims=True), 128)
+def last_row_kernel(c0, c1, c2, c3, z0_ref, z1_ref, e_ref, c_ref, row_ref, kept_ref, acc):
+    row = row_pass((c0, c1, c2, c3), e_ref, c_ref, acc)
+    row_ref[...] = jnp.concatenate([row, z0_ref[...] + z1_ref[...]], axis=0)
+
+
+def row_kernel(c0, c1, c2, c3, z_ref, e_ref, c_ref, row_ref, z_out, kept_ref, acc):
+    z_out[...] = z_ref[...]
+    row = row_pass((c0, c1, c2, c3), e_ref, c_ref, acc)
+    row_ref[...] = row
+
+
+def col_kernel(r0, r1, r2, r3, e_ref, col_ref, kept_ref, rb):
+    rb[...] = lanes_to_rows(1.0 / ((r0[...] + r1[...]) + (r2[...] + r3[...])), 128)
 
     @pl.loop(0, GROUPS // 8)
     def _(q):
@@ -150,20 +172,16 @@
             for u in range(8):
                 accs[u] = accs[u] + e[:, u * 128 : (u + 1) * 128] * r
         part = jnp.concatenate([jnp.sum(a, axis=0, keepdims=True) for a in accs], axis=0)
-        col_ref[:, pl.ds(pl.multiple_of(q * 8, 8), 8), :] = jnp.broadcast_to(part, (NB, 8, 128))
-
-
-def dz_kernel(rzp_ref, c_ref, f_ref, e_ref, p_ref, mine_ref, other_ref, rz_ref, rb, zb, dz_ref):
+        col_ref[pl.ds(pl.multiple_of(q * 8, 8), 8), :] = part
+
+
+def dz_kernel(rz_ref, c_ref, f_ref, e_ref, p_ref, mine_ref, other_ref, rb, zb, dz_ref):
     step = pl.program_id(0)
 
     @pl.when(step == 0)
     def _():
-        block = lax.axis_index("x") * 4 + lax.axis_index("y")
-        for b in range(NB):
-            rz_ref[b] = GSCALE / jnp.sum(rzp_ref[b * NP : (b + 1) * NP], axis=0)
-        rz = rz_ref[block]
-        rb[...] = lanes_to_rows(rz[0:1, :], 128)
-        zb[...] = lanes_to_rows(rz[1:2, :], 128)
+        rb[...] = lanes_to_rows(rz_ref[0:1, :], 128)
+        zb[...] = lanes_to_rows(rz_ref[1:2, :], 128)
         dz_ref[...] = jnp.zeros_like(dz_ref)
 
     tall = BLOCK // 128
@@ -192,7 +210,7 @@
         other_ref[...] = dz_ref[pl.ds(pl.multiple_of((1 - core) * half, half), half), :]
 
 
-def pg_kernel(block_ref, rz_ref, c_ref, p_ref, f_ref, out_ref, pt, cb, acc, g):
+def pg_kernel(block_ref, r0, r1, r2, r3, c_ref, p_ref, f_ref, out_ref, pt, cb, acc, g, rz):
     step = pl.program_id(0)
 
     @pl.when(step == 0)
@@ -201,12 +219,18 @@
         for q in range(8):
             cb[q * 128 : (q + 1) * 128, :] = lanes_to_rows(c_ref[q : q + 1, :], 128)
         acc[...] = jnp.zeros_like(acc)
+        x = lax.axis_index("x")
+        y = lax.axis_index("y")
+        for dx, ref in enumerate((r0, r1, r2, r3)):
+            for dy in range(4):
+                rz[lax.rem(x - dx + 4, 4) * 4 + lax.rem(y - dy + 4, 4)] = ref[dy]
 
     t = f_ref[:, :D]
     s = f_ref[:, D:]
     blocks = range(PG_ROWS // ROWS)
-    r = jnp.concatenate([rz_ref[b, 0:1, :] for b in blocks], axis=1)
-    z = jnp.concatenate([rz_ref[b, 1:2, :] for b in blocks], axis=1)
+    rzs = [rz[step * len(blocks) + b] for b in blocks]
+    r = jnp.concatenate([v[0:1, :] for v in rzs], axis=1)
+    z = jnp.concatenate([v[1:2, :] for v in rzs], axis=1)
     nt = (((1,), (1,)), ((), ()))
     for n in range(PG_ROWS // 256):
         rows = slice(n * 256, (n + 1) * 256)
@@ -231,15 +255,41 @@
     return pltpu.with_memory_space_constraint(x, pltpu.HBM)
 
 
-def exchange(x, axes):
-    return lax.all_to_all(x, axes, 0, 0, tiled=True)
-
-
-def sum_over_z(x):
+def around(x, axis):
     parts = [x]
     for d in (1, 2, 3):
-        parts.append(lax.ppermute(x, "z", [(i, (i + d) % 4) for i in range(4)]))
+        parts.append(lax.ppermute(x, axis, [(i, (i + d) % 4) for i in range(4)]))
     return parts
+
+
+def row_terms(rowp):
+    pair = pl.pallas_call(
+        pair_kernel,
+        out_shape=pltpu.VMEM(rowp.shape, f32),
+        in_specs=[whole()] * 2,
+        out_specs=whole(),
+        compiler_params=params(14),
+        name="pair",
+    )(rowp, lax.ppermute(rowp, "c", [(0, 1), (1, 0)]))
+    return around(pair, "z")
+
+
+def z_call(half, after, feats, protos):
+    steps = COLS // 2 // BLOCK
+    return pl.pallas_call(
+        z_kernel,
+        grid=(steps,),
+        out_shape=pltpu.VMEM((1, ROWS), f32),
+        in_specs=[
+            pl.BlockSpec((8, 128), lambda i: (0, 0)),
+            whole(),
+            pl.BlockSpec((D, BLOCK), lambda i: (0, half * steps + i)),
+        ],
+        out_specs=whole(),
+        scratch_shapes=[pltpu.VMEM((ROWS, 128), f32)],
+        compiler_params=params(14),
+        name="zden",
+    )(after, in_vmem(feats), in_hbm(protos))
 
 
 def shards(teacher_feats, student_feats, proto_weight):
@@ -260,74 +310,118 @@
     )(in_hbm(teacher_feats), in_hbm(student_feats))
     feats_all = lax.all_gather(share, ALL, axis=0, tiled=True)
 
-    protos, expo, colp, zpart = pl.pallas_call(
+    protos, expo, colp = pl.pallas_call(
         first_kernel,
         grid=(COLS // BLOCK,),
         out_shape=(
             pltpu.HBM((D, COLS), bf16),
             kept,
-            vmem((NB, GROUPS, 128), f32),
-            vmem((1, ROWS), f32),
+            vmem((GROUPS, 128), f32),
         ),
         in_specs=[pl.BlockSpec((D, BLOCK), lambda i: (0, i)), whole()],
-        out_specs=(pl.BlockSpec((D, BLOCK), lambda i: (0, i)), whole(), whole(), whole()),
-        scratch_shapes=[vmem((ROWS, 128), f32)],
+        out_specs=(pl.BlockSpec((D, BLOCK), lambda i: (0, i)), whole(), whole()),
         compiler_params=params(14),
         name="first",
     )(in_hbm(proto_weight), in_vmem(feats))
 
     for step in range(ITERS):
-        colp = in_vmem(exchange(colp, XY))
+        parts = around(colp, "y")
+        if step == 0:
+            z0 = z_call(0, colp, feats, protos)
+            colp, z0 = pl.pallas_call(
+                sum_z_kernel,
+                out_shape=(vmem((GROUPS, 128), f32), vmem((1, ROWS), f32)),
+                in_specs=[whole()] * 5,
+                out_specs=(whole(), whole()),
+                compiler_params=params(14),
+                name="sum_z",
+            )(*parts, z0)
+        else:
+            colp = pl.pallas_call(
+                sum_kernel,
+                out_shape=vmem((GROUPS, 128), f32),
+                in_specs=[whole()] * 4,
+                out_specs=whole(),
+                compiler_params=params(14),
+                name="sum",
+            )(*parts)
+        parts = around(colp, "x")
+        if step == 0:
+            z1 = z_call(1, colp, feats, protos)
         if step == ITERS - 1:
             break
-        unused, rowp, expo = pl.pallas_call(
+        unused, rowp, z1, expo = pl.pallas_call(
             row_kernel,
-            out_shape=(vmem((GROUPS, 128), f32), vmem((NP, 1, ROWS), f32), kept),
-            in_specs=[whole()] * 2,
-            out_specs=(whole(),) * 3,
-            input_output_aliases={1: 2},
+            out_shape=(
+                vmem((GROUPS, 128), f32),
+                vmem((1, ROWS), f32),
+                vmem((1, ROWS), f32),
+                kept,
+            ),
+            in_specs=[whole()] * 6,
+            out_specs=(whole(),) * 4,
+            input_output_aliases={5: 3},
             scratch_shapes=[vmem((ROWS, 128), f32)],
             compiler_params=params(14),
             name="row",
-        )(colp, in_vmem(expo))
-        rowp = in_vmem(exchange(rowp, ZC))
+        )(*parts, in_vmem(z1), in_vmem(expo))
+        rowps = row_terms(rowp)
         colp, expo = pl.pallas_call(
             col_kernel,
-            out_shape=(vmem((NB, GROUPS, 128), f32), kept),
-            in_specs=[whole()] * 2,
+            out_shape=(vmem((GROUPS, 128), f32), kept),
+            in_specs=[whole()] * 5,
             out_specs=(whole(), whole()),
-            input_output_aliases={1: 1},
+            input_output_aliases={4: 1},
             scratch_shapes=[vmem((ROWS, 128), f32)],
             compiler_params=params(14),
             name="col",
-        )(rowp, in_vmem(expo))
+        )(*rowps, in_vmem(expo))
 
     colsc, rzp, expo = pl.pallas_call(
         last_row_kernel,
-        out_shape=(vmem((GROUPS, 128), f32), vmem((ND, 2, ROWS), f32), kept),
-        in_specs=[whole()] * 3,
+        out_shape=(vmem((GROUPS, 128), f32), vmem((2, ROWS), f32), kept),
+        in_specs=[whole()] * 7,
         out_specs=(whole(),) * 3,
-        input_output_aliases={2: 2},
+        input_output_aliases={6: 2},
         scratch_shapes=[vmem((ROWS, 128), f32)],
         compiler_params=params(14),
         name="row_last",
-    )(colp, in_vmem(zpart), in_vmem(expo))
-    rzp = in_vmem(exchange(rzp, ALL))
+    )(*parts, in_vmem(z0), in_vmem(z1), in_vmem(expo))
+    rz = pl.pallas_call(
+        rz_kernel,
+        out_shape=vmem((2, ROWS), f32),
+        in_specs=[whole()] * 4,
+        out_specs=whole(),
+        compiler_params=params(14),
+        name="rz",
+    )(*row_terms(rzp))
+    rz_y = around(rz, "y")
 
     half = ROWS // 2
-    mine, other, rz_all = pl.pallas_call(
+    mine, other = pl.pallas_call(
         dz_kernel,
         grid=(COLS // BLOCK,),
-        out_shape=(vmem((half, D), f32), vmem((half, D), f32), sds((NB, 2, ROWS), f32)),
+        out_shape=(vmem((half, D), f32), vmem((half, D), f32)),
         in_specs=[whole()] * 4 + [pl.BlockSpec((D, BLOCK), lambda i: (0, i))],
-        out_specs=(whole(), whole(), whole()),
+        out_specs=(whole(), whole()),
         scratch_shapes=[vmem((ROWS, 128), f32)] * 2 + [vmem((ROWS, D), f32)],
         compiler_params=params(14),
         name="dz",
-    )(rzp, in_vmem(colsc), in_vmem(feats), in_vmem(expo), in_hbm(protos))
+    )(in_vmem(rz), in_vmem(colsc), in_vmem(feats), in_vmem(expo), in_hbm(protos))
+
+    rz_rows, other = pl.pallas_call(
+        stack_kernel,
+        out_shape=(vmem((4, 2, ROWS), f32), vmem((half, D), f32)),
+        in_specs=[whole()] * 5,
+        out_specs=(whole(), whole()),
+        input_output_aliases={4: 1},
+        compiler_params=params(14),
+        name="stack",
+    )(*rz_y, other)
+    rz_all = around(rz_rows, "x")
 
     got = lax.ppermute(other, "c", [(0, 1), (1, 0)])
-    parts = sum_over_z(mine + got)
+    parts = around(mine + got, "z")
 
     proto_grad = pl.pallas_call(
         pg_kernel,
@@ -335,7 +429,7 @@
             num_scalar_prefetch=1,
             grid=(NB * ROWS // PG_ROWS,),
             in_specs=[
-                pl.BlockSpec((PG_ROWS // ROWS, 2, ROWS), lambda i, b: (i, 0, 0)),
+                *[pl.BlockSpec((4, 2, ROWS), lambda i, b: (0, 0, 0))] * 4,
                 pl.BlockSpec((8, 128), lambda i, b: (b[0], 0)),
                 pl.BlockSpec((D, OWN), lambda i, b: (0, b[0])),
                 pl.BlockSpec((PG_ROWS, 2 * D), lambda i, b: (i, 0)),
@@ -346,13 +440,14 @@
                 vmem((OWN, 128), f32),
                 vmem((OWN, D), f32),
                 vmem((OWN, PG_ROWS), bf16),
+                vmem((NB, 2, ROWS), f32),
             ],
         ),
         out_shape=sds((D, OWN), f32),
         compiler_params=params(14),
         cost_estimate=pl.CostEstimate(flops=9700000000, bytes_accessed=8000000, transcendentals=12600000),
         name="pg",
-    )(block.reshape(1), rz_all, colsc, in_hbm(protos), in_hbm(feats_all))
+    )(block.reshape(1), *rz_all, colsc, in_hbm(protos), in_hbm(feats_all))
 
     parts, proto_grad, student_feats = lax.optimization_barrier(
         (parts, proto_grad, student_feats)

time: 190 us -> 161 us (0.85)
  blocking collectives: 109 us -> 0 us
  starting transfers between devices: 4.95 us -> 64.1 us
  waiting for transfers between devices: 2.38 us -> 21.8 us
  Pallas kernels: 56.8 us -> 59.9 us
    all_to_all x6 -> x0, blocking collectives: 109 us -> none  [exchange(): return lax.all_to_all(x, axes, 0, 0, tiled=True)]
    ppermute x3 -> x39, starting transfers between devices: 2.74 us -> 59.8 us  [the longest x36 46.2 us: around(): parts.append(lax.ppermute(x, axis, [(i, (i + d) % 4) for i in range(4)]))]
    ppermute x3 -> x39, waiting for transfers between devices: 0.01 us -> 20.7 us  [the longest x36 18.2 us: around(): parts.append(lax.ppermute(x, axis, [(i, (i + d) % 4) for i in range(4)]))]
    pallas_call x4 -> x14, Pallas kernels: 10.4 us -> 17.8 us  [the longest x2 7.58 us: z_call(): pl.pallas_call(z_kernel, grid=(steps,), out_shape=pltpu.VMEM((1, ROWS), f...]
    pallas_call x1, Pallas kernels: 14.4 us -> 11.1 us  [shards(): pl.pallas_call(first_kernel, grid=(COLS // BLOCK,), out_shape=(pltpu.HBM(...]
  transfers between devices with their start and end apart: 6 -> 42, of which waited for: 2 -> 22; matrix products, arithmetic and copies ran while one was open for 1% -> 0% of each run, Pallas kernels for 29% -> 36%
where the time goes in v3:
time: 161 us
  starting transfers between devices  64.1 us (40%)
  Pallas kernels  59.9 us (37%)
  waiting for transfers between devices  21.8 us (14%)
  between operations  14.3 us (9%)
    ppermute x36, starting transfers between devices, around(): parts.append(lax.ppermute(x, axis, [(i, (i + d) % 4) for i in range(4)]))  46.2 us
    ppermute x36, waiting for transfers between devices, around(): parts.append(lax.ppermute(x, axis, [(i, (i + d) % 4) for i in range(4)]))  18.2 us
    pallas_call x1, Pallas kernels, shards(): pl.pallas_call(pg_kernel, grid_spec=pltpu.PrefetchScalarGridSpec(num_scal...  16.3 us
    ppermute x3, starting transfers between devices, row_terms(): lax.ppermute(rowp, 'c', [(0, 1), (1, 0)])  13.6 us
    pallas_call x1, Pallas kernels, shards(): pl.pallas_call(first_kernel, grid=(COLS // BLOCK,), out_shape=(pltpu.HBM(...  11.1 us
    pallas_call x1, Pallas kernels, shards(): pl.pallas_call(dz_kernel, grid=(COLS // BLOCK,), out_shape=(vmem((half, D...  10.4 us
    pallas_call x2, Pallas kernels, z_call(): pl.pallas_call(z_kernel, grid=(steps,), out_shape=pltpu.VMEM((1, ROWS), f...  7.58 us
    pallas_call x2, Pallas kernels, shards(): pl.pallas_call(row_kernel, out_shape=(vmem((GROUPS, 128), f32), vmem((1,...  5.85 us
  transfers between devices with their start and end apart: 42, of which 22 were waited for; matrix products, arithmetic and copies ran while one was open for 0% of the time, Pallas kernels for 36%

profile of v3, /device:TPU:1, one launch (start us, length us, event | category | flops | bytes accessed | tf_op | source)
XLA Modules:
  0.0 161.2 jit_solution(2560476918961189444)
XLA Ops:
  9.1 11.1 %first.1 = (bf16[256,16384]{1,0:T(8,128)(2,1)}, f32[384,16384]{1,0:T(8,128)S(1)}, f32[128,128]{1,0:T(8,128)S(1)}) custom-call(bf16[256,16384]{1,0:T(8,128)(2,1)} %w_ref.1, bf16[768,256]{1,0:T(8,128)(2,1)S(1)} %get-tuple-element.32.f_ref), custom_call_target="tpu_custom_call" | custom-call | tf_op jit(solution)/shard_map/first/pallas_call | solution.py:313
  22.3 2.6 %collective-permute-start.1 = (f32[128,128]{1,0:T(8,128)S(1)}, f32[128,128]{1,0:T(8,128)S(1)}, u32[]{:S(2)}, u32[]{:S(2)}) collective-permute-start(f32[128,128]{1,0:T(8,128)S(1)} %get-tuple-element.33.after_ref.a_ref), channel_id=1, source_target_pairs={{0,16},{8,24},{16,0},{24,8},{1,17},{9,25},{17,1},{25,9},{2,18},{10... | collective-permute-start | bytes 196616 | tf_op jit(solution)/shard_map/ppermute | solution.py:261
  25.9 3.8 %zden.2.z_ref = f32[1,384]{1,0:T(1,128)S(1)} custom-call(f32[128,128]{1,0:T(8,128)S(1)} %get-tuple-element.33.after_ref.a_ref, bf16[768,256]{1,0:T(8,128)(2,1)S(1)} %get-tuple-element.32.f_ref, bf16[256,16384]{1,0:T(8,128)(2,1)} %get-tuple-element.34.p_ref), custom_call_target="tpu_custom_call" | custom-call | tf_op jit(solution)/shard_map/zden/pallas_call | solution.py:279
  31.1 2.4 %collective-permute-start.4 = (f32[128,128]{1,0:T(8,128)S(1)}, f32[128,128]{1,0:T(8,128)S(1)}, u32[]{:S(2)}, u32[]{:S(2)}) collective-permute-start(f32[128,128]{1,0:T(8,128)S(1)} %get-tuple-element.35.after_ref.c0), channel_id=1, source_target_pairs={{0,64},{32,96},{64,0},{96,32},{1,65},{33,97},{65,1},{97,33},{2,66}... | collective-permute-start | bytes 196616 | tf_op jit(solution)/shard_map/ppermute | solution.py:261
  34.7 3.8 %zden.3.z_ref = f32[1,384]{1,0:T(1,128)S(1)} custom-call(f32[128,128]{1,0:T(8,128)S(1)} %get-tuple-element.35.after_ref.c0, bf16[768,256]{1,0:T(8,128)(2,1)S(1)} %get-tuple-element.32.f_ref, bf16[256,16384]{1,0:T(8,128)(2,1)} %get-tuple-element.34.p_ref), custom_call_target="tpu_custom_call" | custom-call | tf_op jit(solution)/shard_map/zden/pallas_call | solution.py:279
  38.5 2.9 %row.2 = (f32[128,128]{1,0:T(8,128)}, f32[1,384]{1,0:T(1,128)S(1)}, f32[1,384]{1,0:T(1,128)S(1)}, f32[384,16384]{1,0:T(8,128)S(1)}) custom-call(f32[128,128]{1,0:T(8,128)S(1)} %get-tuple-element.35.after_ref.c0, f32[128,128]{1,0:T(8,128)S(1)} %collective-permute-done.3.c1, ...), custom_call_target="tpu_custom_call", output_to_operand_aliasing={{3}: (5, {})} | custom-call | tf_op jit(solution)/shard_map/row/pallas_call | solution.py:353
  41.5 2.3 %collective-permute-start.6 = (f32[1,384]{1,0:T(1,128)S(1)}, f32[1,384]{1,0:T(1,128)S(1)}, u32[]{:S(2)}, u32[]{:S(2)}) collective-permute-start(f32[1,384]{1,0:T(1,128)S(1)} %get-tuple-element.37.a_ref), channel_id=1, source_target_pairs={{0,1},{1,0},{2,3},{3,2},{4,5},{5,4},{6,7},{7,6},{8,9},{9,8},{10,11... | collective-permute-start | bytes 4616 | tf_op jit(solution)/shard_map/ppermute | solution.py:273
  46.3 3.3 %collective-permute-start.8 = (f32[1,384]{1,0:T(1,128)S(1)}, f32[1,384]{1,0:T(1,128)S(1)}, u32[]{:S(2)}, u32[]{:S(2)}) collective-permute-start(f32[1,384]{1,0:T(1,128)S(1)} %pair.3.r0), channel_id=1, source_target_pairs={{0,4},{2,6},{4,0},{6,2},{1,5},{3,7},{5,1},{7,3},{8,12},{10,14},{12... | collective-permute-start | bytes 4616 | tf_op jit(solution)/shard_map/ppermute | solution.py:261
  54.8 2.4 %collective-permute-start.11 = (f32[128,128]{1,0:T(8,128)S(1)}, f32[128,128]{1,0:T(8,128)S(1)}, u32[]{:S(2)}, u32[]{:S(2)}) collective-permute-start(f32[128,128]{1,0:T(8,128)S(1)} %get-tuple-element.39.a_ref), channel_id=1, source_target_pairs={{0,16},{8,24},{16,0},{24,8},{1,17},{9,25},{17,1},{25,9},{2,18},{10... | collective-permute-start | bytes 196616 | tf_op jit(solution)/shard_map/ppermute | solution.py:261
  63.1 2.3 %collective-permute-done.13.c1 = f32[128,128]{1,0:T(8,128)S(1)} collective-permute-done((f32[128,128]{1,0:T(8,128)S(1)}, f32[128,128]{1,0:T(8,128)S(1)}, u32[]{:S(2)}, u32[]{:S(2)}) %collective-permute-start.13) | collective-permute-done | bytes 65568 | tf_op jit(solution)/shard_map/ppermute | solution.py:261
  66.0 2.9 %row.3 = (f32[128,128]{1,0:T(8,128)}, f32[1,384]{1,0:T(1,128)S(1)}, f32[1,384]{1,0:T(1,128)S(1)}, f32[384,16384]{1,0:T(8,128)S(1)}) custom-call(f32[128,128]{1,0:T(8,128)S(1)} %sum.2.c0, f32[128,128]{1,0:T(8,128)S(1)} %collective-permute-done.13.c1, f32[128,128]{1,0:T(8,128)S(1)} %collective-permute-done.14.c2, ...), custom_call_target="tpu_custom_call", output_to_operand_aliasing={{3}: (5, {})} | custom-call | tf_op jit(solution)/shard_map/row/pallas_call | solution.py:353
  68.9 6.3 %collective-permute-start.16 = (f32[1,384]{1,0:T(1,128)S(1)}, f32[1,384]{1,0:T(1,128)S(1)}, u32[]{:S(2)}, u32[]{:S(2)}) collective-permute-start(f32[1,384]{1,0:T(1,128)S(1)} %get-tuple-element.42.a_ref), channel_id=1, source_target_pairs={{0,1},{1,0},{2,3},{3,2},{4,5},{5,4},{6,7},{7,6},{8,9},{9,8},{10,11... | collective-permute-start | bytes 4616 | tf_op jit(solution)/shard_map/ppermute | solution.py:273
  76.1 4.0 %collective-permute-start.18 = (f32[1,384]{1,0:T(1,128)S(1)}, f32[1,384]{1,0:T(1,128)S(1)}, u32[]{:S(2)}, u32[]{:S(2)}) collective-permute-start(f32[1,384]{1,0:T(1,128)S(1)} %pair.4.r0), channel_id=1, source_target_pairs={{0,4},{2,6},{4,0},{6,2},{1,5},{3,7},{5,1},{7,3},{8,12},{10,14},{12... | collective-permute-start | bytes 4616 | tf_op jit(solution)/shard_map/ppermute | solution.py:261
  85.9 2.4 %collective-permute-start.21 = (f32[128,128]{1,0:T(8,128)S(1)}, f32[128,128]{1,0:T(8,128)S(1)}, u32[]{:S(2)}, u32[]{:S(2)}) collective-permute-start(f32[128,128]{1,0:T(8,128)S(1)} %get-tuple-element.44.a_ref), channel_id=1, source_target_pairs={{0,16},{8,24},{16,0},{24,8},{1,17},{9,25},{17,1},{25,9},{2,18},{10... | collective-permute-start | bytes 196616 | tf_op jit(solution)/shard_map/ppermute | solution.py:261
  94.5 2.3 %collective-permute-done.23.c1 = f32[128,128]{1,0:T(8,128)S(1)} collective-permute-done((f32[128,128]{1,0:T(8,128)S(1)}, f32[128,128]{1,0:T(8,128)S(1)}, u32[]{:S(2)}, u32[]{:S(2)}) %collective-permute-start.23) | collective-permute-done | bytes 65568 | tf_op jit(solution)/shard_map/ppermute | solution.py:261
  97.4 2.4 %row_last.1 = (f32[128,128]{1,0:T(8,128)S(1)}, f32[2,384]{1,0:T(2,128)S(1)}, f32[384,16384]{1,0:T(8,128)S(1)}) custom-call(f32[128,128]{1,0:T(8,128)S(1)} %sum.3.c0, f32[128,128]{1,0:T(8,128)S(1)} %collective-permute-done.23.c1, f32[128,128]{1,0:T(8,128)S(1)} %collective-permute-done.24.c2, ...), custom_call_target="tpu_custom_call", output_to_operand_aliasing={{2}: (6, {})} | custom-call | tf_op jit(solution)/shard_map/row_last/pallas_call | solution.py:380
  99.9 5.0 %collective-permute-start.26 = (f32[2,384]{1,0:T(2,128)S(1)}, f32[2,384]{1,0:T(2,128)S(1)}, u32[]{:S(2)}, u32[]{:S(2)}) collective-permute-start(f32[2,384]{1,0:T(2,128)S(1)} %get-tuple-element.48.a_ref), channel_id=1, source_target_pairs={{0,1},{1,0},{2,3},{3,2},{4,5},{5,4},{6,7},{7,6},{8,9},{9,8},{10,11... | collective-permute-start | bytes 9224 | tf_op jit(solution)/shard_map/ppermute | solution.py:273
  105.7 2.2 %collective-permute-start.28 = (f32[2,384]{1,0:T(2,128)S(1)}, f32[2,384]{1,0:T(2,128)S(1)}, u32[]{:S(2)}, u32[]{:S(2)}) collective-permute-start(f32[2,384]{1,0:T(2,128)S(1)} %pair.5.a_ref), channel_id=1, source_target_pairs={{0,4},{2,6},{4,0},{6,2},{1,5},{3,7},{5,1},{7,3},{8,12},{10,14},{12... | collective-permute-start | bytes 9224 | tf_op jit(solution)/shard_map/ppermute | solution.py:261
  110.6 2.7 %collective-permute-start.31 = (f32[2,384]{1,0:T(2,128)S(1)}, f32[2,384]{1,0:T(2,128)S(1)}, u32[]{:S(2)}, u32[]{:S(2)}) collective-permute-start(f32[2,384]{1,0:T(2,128)S(1)} %rz.1.rz_ref.a_ref), channel_id=1, source_target_pairs={{0,16},{8,24},{16,0},{24,8},{1,17},{9,25},{17,1},{25,9},{2,18},{10... | collective-permute-start | bytes 9224 | tf_op jit(solution)/shard_map/ppermute | solution.py:261
  113.9 10.4 %dz.1 = (f32[192,256]{1,0:T(8,128)S(1)}, f32[192,256]{1,0:T(8,128)S(1)}) custom-call(f32[2,384]{1,0:T(2,128)S(1)} %rz.1.rz_ref.a_ref, f32[128,128]{1,0:T(8,128)S(1)} %get-tuple-element.49.c_ref, bf16[768,256]{1,0:T(8,128)(2,1)S(1)} %get-tuple-element.32.f_ref, f32[384,16384]{1,0:T(8,128)S(1)} %get-tuple-element.50.e_ref, ...), custom_call_target="tpu_custom_call" | custom-call | tf_op jit(solution)/shard_map/dz/pallas_call | solution.py:401
  124.4 2.7 %collective-permute-start.33 = (f32[192,256]{1,0:T(8,128)S(1)}, f32[192,256]{1,0:T(8,128)S(1)}, u32[]{:S(2)}, u32[]{:S(2)}) collective-permute-start(f32[192,256]{1,0:T(8,128)S(1)} %get-tuple-element.53), channel_id=1, source_target_pairs={{0,1},{1,0},{2,3},{3,2},{4,5},{5,4},{6,7},{7,6},{8,9},{9,8},{10,11... | collective-permute-start | bytes 589832 | tf_op jit(solution)/shard_map/ppermute | solution.py:423
  128.1 2.2 %collective-permute-start.38 = (f32[4,2,384]{2,1,0:T(2,128)S(1)}, f32[4,2,384]{2,1,0:T(2,128)S(1)}, u32[]{:S(2)}, u32[]{:S(2)}) collective-permute-start(f32[4,2,384]{2,1,0:T(2,128)S(1)} %get-tuple-element.54.r0), channel_id=1, source_target_pairs={{0,64},{32,96},{64,0},{96,32},{1,65},{33,97},{65,1},{97,33},{2,66}... | collective-permute-start | bytes 36872 | tf_op jit(solution)/shard_map/ppermute | solution.py:261
  131.7 2.4 %collective-permute-start.35 = (f32[192,256]{1,0:T(8,128)S(1)}, f32[192,256]{1,0:T(8,128)S(1)}, u32[]{:S(2)}, u32[]{:S(2)}) collective-permute-start(f32[192,256]{1,0:T(8,128)S(1)} %add.29), channel_id=1, source_target_pairs={{0,4},{2,6},{4,0},{6,2},{1,5},{3,7},{5,1},{7,3},{8,12},{10,14},{12... | collective-permute-start | bytes 589832 | tf_op jit(solution)/shard_map/ppermute | solution.py:261
  134.2 16.3 %pg.1 = f32[256,1024]{1,0:T(8,128)} custom-call(s32[1]{0:T(128)} %bitcast.block_ref, f32[4,2,384]{2,1,0:T(2,128)S(1)} %get-tuple-element.54.r0, f32[4,2,384]{2,1,0:T(2,128)S(1)} %collective-permute-done.37.r1, f32[4,2,384]{2,1,0:T(2,128)S(1)} %collective-permute-done.38.r2, f32[4,2,384]{2,1,0:T(2,128)S(1)} %collective-permute-done.39.r3, ...), custom_call_target="tpu_custom_call" | custom-call | flops 9699999744 | bytes 8000000 | tf_op jit(solution)/shard_map/pg/pallas_call | solution.py:426
  (88 shorter events, 45.6 us)
Async XLA Ops:
  7.2 127.0 %all-gather.2.cloned.1.call-start = ((), (), s32[]{:S(2)}) async-start(), calls=%async_computation | async-start | bytes 6340608 | tf_op jit(solution)/shard_map/all_gather | solution.py:311
  20.1 9.6 %collective-permute-start = (f32[128,128]{1,0:T(8,128)S(1)}, f32[128,128]{1,0:T(8,128)S(1)}, u32[]{:S(2)}, u32[]{:S(2)}) collective-permute-start(f32[128,128]{1,0:T(8,128)S(1)} %get-tuple-element.33.after_ref.a_ref), channel_id=1, source_target_pairs={{0,8},{8,16},{16,24},{24,0},{1,9},{9,17},{17,25},{25,1},{2,10},{10... | collective-permute-start | bytes 196616 | tf_op jit(solution)/shard_map/ppermute | solution.py:261
  22.3 7.5 %collective-permute-start.1 = (f32[128,128]{1,0:T(8,128)S(1)}, f32[128,128]{1,0:T(8,128)S(1)}, u32[]{:S(2)}, u32[]{:S(2)}) collective-permute-start(f32[128,128]{1,0:T(8,128)S(1)} %get-tuple-element.33.after_ref.a_ref), channel_id=1, source_target_pairs={{0,16},{8,24},{16,0},{24,8},{1,17},{9,25},{17,1},{25,9},{2,18},{10... | collective-permute-start | bytes 196616 | tf_op jit(solution)/shard_map/ppermute | solution.py:261
  29.8 8.7 %collective-permute-start.3 = (f32[128,128]{1,0:T(8,128)S(1)}, f32[128,128]{1,0:T(8,128)S(1)}, u32[]{:S(2)}, u32[]{:S(2)}) collective-permute-start(f32[128,128]{1,0:T(8,128)S(1)} %get-tuple-element.35.after_ref.c0), channel_id=1, source_target_pairs={{0,32},{32,64},{64,96},{96,0},{1,33},{33,65},{65,97},{97,1},{2,34}... | collective-permute-start | bytes 196616 | tf_op jit(solution)/shard_map/ppermute | solution.py:261
  31.1 7.4 %collective-permute-start.4 = (f32[128,128]{1,0:T(8,128)S(1)}, f32[128,128]{1,0:T(8,128)S(1)}, u32[]{:S(2)}, u32[]{:S(2)}) collective-permute-start(f32[128,128]{1,0:T(8,128)S(1)} %get-tuple-element.35.after_ref.c0), channel_id=1, source_target_pairs={{0,64},{32,96},{64,0},{96,32},{1,65},{33,97},{65,1},{97,33},{2,66}... | collective-permute-start | bytes 196616 | tf_op jit(solution)/shard_map/ppermute | solution.py:261
  33.5 5.0 %collective-permute-start.5 = (f32[128,128]{1,0:T(8,128)S(1)}, f32[128,128]{1,0:T(8,128)S(1)}, u32[]{:S(2)}, u32[]{:S(2)}) collective-permute-start(f32[128,128]{1,0:T(8,128)S(1)} %get-tuple-element.35.after_ref.c0), channel_id=1, source_target_pairs={{0,96},{32,0},{64,32},{96,64},{1,97},{33,1},{65,33},{97,65},{2,98}... | collective-permute-start | bytes 196616 | tf_op jit(solution)/shard_map/ppermute | solution.py:261
  44.6 5.7 %collective-permute-start.7 = (f32[1,384]{1,0:T(1,128)S(1)}, f32[1,384]{1,0:T(1,128)S(1)}, u32[]{:S(2)}, u32[]{:S(2)}) collective-permute-start(f32[1,384]{1,0:T(1,128)S(1)} %pair.3.r0), channel_id=1, source_target_pairs={{0,2},{2,4},{4,6},{6,0},{1,3},{3,5},{5,7},{7,1},{8,10},{10,12},{12... | collective-permute-start | bytes 4616 | tf_op jit(solution)/shard_map/ppermute | solution.py:261
  54.4 5.1 %collective-permute-start.10 = (f32[128,128]{1,0:T(8,128)S(1)}, f32[128,128]{1,0:T(8,128)S(1)}, u32[]{:S(2)}, u32[]{:S(2)}) collective-permute-start(f32[128,128]{1,0:T(8,128)S(1)} %get-tuple-element.39.a_ref), channel_id=1, source_target_pairs={{0,8},{8,16},{16,24},{24,0},{1,9},{9,17},{17,25},{25,1},{2,10},{10... | collective-permute-start | bytes 196616 | tf_op jit(solution)/shard_map/ppermute | solution.py:261
  54.8 5.0 %collective-permute-start.11 = (f32[128,128]{1,0:T(8,128)S(1)}, f32[128,128]{1,0:T(8,128)S(1)}, u32[]{:S(2)}, u32[]{:S(2)}) collective-permute-start(f32[128,128]{1,0:T(8,128)S(1)} %get-tuple-element.39.a_ref), channel_id=1, source_target_pairs={{0,16},{8,24},{16,0},{24,8},{1,17},{9,25},{17,1},{25,9},{2,18},{10... | collective-permute-start | bytes 196616 | tf_op jit(solution)/shard_map/ppermute | solution.py:261
  60.3 5.1 %collective-permute-start.13 = (f32[128,128]{1,0:T(8,128)S(1)}, f32[128,128]{1,0:T(8,128)S(1)}, u32[]{:S(2)}, u32[]{:S(2)}) collective-permute-start(f32[128,128]{1,0:T(8,128)S(1)} %sum.2.c0), channel_id=1, source_target_pairs={{0,32},{32,64},{64,96},{96,0},{1,33},{33,65},{65,97},{97,1},{2,34}... | collective-permute-start | bytes 196616 | tf_op jit(solution)/shard_map/ppermute | solution.py:261
  68.9 7.1 %collective-permute-start.16 = (f32[1,384]{1,0:T(1,128)S(1)}, f32[1,384]{1,0:T(1,128)S(1)}, u32[]{:S(2)}, u32[]{:S(2)}) collective-permute-start(f32[1,384]{1,0:T(1,128)S(1)} %get-tuple-element.42.a_ref), channel_id=1, source_target_pairs={{0,1},{1,0},{2,3},{3,2},{4,5},{5,4},{6,7},{7,6},{8,9},{9,8},{10,11... | collective-permute-start | bytes 4616 | tf_op jit(solution)/shard_map/ppermute | solution.py:273
  76.1 5.0 %collective-permute-start.18 = (f32[1,384]{1,0:T(1,128)S(1)}, f32[1,384]{1,0:T(1,128)S(1)}, u32[]{:S(2)}, u32[]{:S(2)}) collective-permute-start(f32[1,384]{1,0:T(1,128)S(1)} %pair.4.r0), channel_id=1, source_target_pairs={{0,4},{2,6},{4,0},{6,2},{1,5},{3,7},{5,1},{7,3},{8,12},{10,14},{12... | collective-permute-start | bytes 4616 | tf_op jit(solution)/shard_map/ppermute | solution.py:261
  91.8 5.1 %collective-permute-start.23 = (f32[128,128]{1,0:T(8,128)S(1)}, f32[128,128]{1,0:T(8,128)S(1)}, u32[]{:S(2)}, u32[]{:S(2)}) collective-permute-start(f32[128,128]{1,0:T(8,128)S(1)} %sum.3.c0), channel_id=1, source_target_pairs={{0,32},{32,64},{64,96},{96,0},{1,33},{33,65},{65,97},{97,1},{2,34}... | collective-permute-start | bytes 196616 | tf_op jit(solution)/shard_map/ppermute | solution.py:261
  91.9 5.0 %collective-permute-start.24 = (f32[128,128]{1,0:T(8,128)S(1)}, f32[128,128]{1,0:T(8,128)S(1)}, u32[]{:S(2)}, u32[]{:S(2)}) collective-permute-start(f32[128,128]{1,0:T(8,128)S(1)} %sum.3.c0), channel_id=1, source_target_pairs={{0,64},{32,96},{64,0},{96,32},{1,65},{33,97},{65,1},{97,33},{2,66}... | collective-permute-start | bytes 196616 | tf_op jit(solution)/shard_map/ppermute | solution.py:261
  99.9 5.8 %collective-permute-start.26 = (f32[2,384]{1,0:T(2,128)S(1)}, f32[2,384]{1,0:T(2,128)S(1)}, u32[]{:S(2)}, u32[]{:S(2)}) collective-permute-start(f32[2,384]{1,0:T(2,128)S(1)} %get-tuple-element.48.a_ref), channel_id=1, source_target_pairs={{0,1},{1,0},{2,3},{3,2},{4,5},{5,4},{6,7},{7,6},{8,9},{9,8},{10,11... | collective-permute-start | bytes 9224 | tf_op jit(solution)/shard_map/ppermute | solution.py:273
  110.6 13.8 %collective-permute-start.30 = (f32[2,384]{1,0:T(2,128)S(1)}, f32[2,384]{1,0:T(2,128)S(1)}, u32[]{:S(2)}, u32[]{:S(2)}) collective-permute-start(f32[2,384]{1,0:T(2,128)S(1)} %rz.1.rz_ref.a_ref), channel_id=1, source_target_pairs={{0,8},{8,16},{16,24},{24,0},{1,9},{9,17},{17,25},{25,1},{2,10},{10... | collective-permute-start | bytes 9224 | tf_op jit(solution)/shard_map/ppermute | solution.py:261
  110.6 13.8 %collective-permute-start.31 = (f32[2,384]{1,0:T(2,128)S(1)}, f32[2,384]{1,0:T(2,128)S(1)}, u32[]{:S(2)}, u32[]{:S(2)}) collective-permute-start(f32[2,384]{1,0:T(2,128)S(1)} %rz.1.rz_ref.a_ref), channel_id=1, source_target_pairs={{0,16},{8,24},{16,0},{24,8},{1,17},{9,25},{17,1},{25,9},{2,18},{10... | collective-permute-start | bytes 9224 | tf_op jit(solution)/shard_map/ppermute | solution.py:261
  113.3 11.1 %collective-permute-start.32 = (f32[2,384]{1,0:T(2,128)S(1)}, f32[2,384]{1,0:T(2,128)S(1)}, u32[]{:S(2)}, u32[]{:S(2)}) collective-permute-start(f32[2,384]{1,0:T(2,128)S(1)} %rz.1.rz_ref.a_ref), channel_id=1, source_target_pairs={{0,24},{8,0},{16,8},{24,16},{1,25},{9,1},{17,9},{25,17},{2,26},{10... | collective-permute-start | bytes 9224 | tf_op jit(solution)/shard_map/ppermute | solution.py:261
  124.4 6.0 %collective-permute-start.33 = (f32[192,256]{1,0:T(8,128)S(1)}, f32[192,256]{1,0:T(8,128)S(1)}, u32[]{:S(2)}, u32[]{:S(2)}) collective-permute-start(f32[192,256]{1,0:T(8,128)S(1)} %get-tuple-element.53), channel_id=1, source_target_pairs={{0,1},{1,0},{2,3},{3,2},{4,5},{5,4},{6,7},{7,6},{8,9},{9,8},{10,11... | collective-permute-start | bytes 589832 | tf_op jit(solution)/shard_map/ppermute | solution.py:423
  127.1 7.0 %collective-permute-start.37 = (f32[4,2,384]{2,1,0:T(2,128)S(1)}, f32[4,2,384]{2,1,0:T(2,128)S(1)}, u32[]{:S(2)}, u32[]{:S(2)}) collective-permute-start(f32[4,2,384]{2,1,0:T(2,128)S(1)} %get-tuple-element.54.r0), channel_id=1, source_target_pairs={{0,32},{32,64},{64,96},{96,0},{1,33},{33,65},{65,97},{97,1},{2,34}... | collective-permute-start | bytes 36872 | tf_op jit(solution)/shard_map/ppermute | solution.py:261
  128.1 6.1 %collective-permute-start.38 = (f32[4,2,384]{2,1,0:T(2,128)S(1)}, f32[4,2,384]{2,1,0:T(2,128)S(1)}, u32[]{:S(2)}, u32[]{:S(2)}) collective-permute-start(f32[4,2,384]{2,1,0:T(2,128)S(1)} %get-tuple-element.54.r0), channel_id=1, source_target_pairs={{0,64},{32,96},{64,0},{96,32},{1,65},{33,97},{65,1},{97,33},{2,66}... | collective-permute-start | bytes 36872 | tf_op jit(solution)/shard_map/ppermute | solution.py:261
  130.5 20.0 %collective-permute-start.34 = (f32[192,256]{1,0:T(8,128)S(1)}, f32[192,256]{1,0:T(8,128)S(1)}, u32[]{:S(2)}, u32[]{:S(2)}) collective-permute-start(f32[192,256]{1,0:T(8,128)S(1)} %add.29), channel_id=1, source_target_pairs={{0,2},{2,4},{4,6},{6,0},{1,3},{3,5},{5,7},{7,1},{8,10},{10,12},{12... | collective-permute-start | bytes 589832 | tf_op jit(solution)/shard_map/ppermute | solution.py:261
  131.7 18.8 %collective-permute-start.35 = (f32[192,256]{1,0:T(8,128)S(1)}, f32[192,256]{1,0:T(8,128)S(1)}, u32[]{:S(2)}, u32[]{:S(2)}) collective-permute-start(f32[192,256]{1,0:T(8,128)S(1)} %add.29), channel_id=1, source_target_pairs={{0,4},{2,6},{4,0},{6,2},{1,5},{3,7},{5,1},{7,3},{8,12},{10,14},{12... | collective-permute-start | bytes 589832 | tf_op jit(solution)/shard_map/ppermute | solution.py:261
  134.1 16.4 %collective-permute-start.36 = (f32[192,256]{1,0:T(8,128)S(1)}, f32[192,256]{1,0:T(8,128)S(1)}, u32[]{:S(2)}, u32[]{:S(2)}) collective-permute-start(f32[192,256]{1,0:T(8,128)S(1)} %add.29), channel_id=1, source_target_pairs={{0,6},{2,0},{4,2},{6,4},{1,7},{3,1},{5,3},{7,5},{8,14},{10,8},{12,... | collective-permute-start | bytes 589832 | tf_op jit(solution)/shard_map/ppermute | solution.py:261
  (19 other events, 92.9 us)
Sparse Core Ops, SparseCore 0:
  11.6 72.3 all-gather.1

commit v4 on v3

v4 whole, which is shorter than its diff:
```python
import functools
import math

import jax
import jax.numpy as jnp
from jax import lax
from jax.experimental import pallas as pl
from jax.experimental.pallas import tpu as pltpu
from jax.sharding import Mesh, PartitionSpec as P

D = 256
PROTOS = 131072
ITERS = 3
ROWS = 384
COLS = 16384
OWN = 1024
SHARE = 48
BLOCK = 4096
PG_ROWS = 3072
CHUNK = 2048
KEPT = 2
GROUPS = COLS // 128
NB = 16
KT = math.log2(math.e) / 0.07
KS = math.log2(math.e) / 0.1
GSCALE = PROTOS / 0.1

f32 = jnp.float32
bf16 = jnp.bfloat16
XY = ("x", "y")
ZC = ("z", "c")
ALL = XY + ZC
MIB = 2**20


def whole():
    return pl.BlockSpec(memory_space=pltpu.VMEM)


def params(mib):
    return pltpu.CompilerParams(vmem_limit_bytes=mib * MIB)


def row_norm(feats):
    return lax.rsqrt(jnp.mean(feats * feats, axis=1, keepdims=True) + 1e-06) / math.sqrt(D)


def lanes_to_rows(vec, width):
    return jnp.transpose(jnp.broadcast_to(vec, (width, vec.shape[1])))


def rows_to_lanes(acc):
    return jnp.sum(jnp.transpose(acc), axis=0, keepdims=True)


def norm_kernel(t_ref, s_ref, out_ref, share_ref):
    for src, rows in ((t_ref, slice(0, ROWS)), (s_ref, slice(ROWS, 2 * ROWS))):
        feats = src[...].astype(f32)
        out_ref[rows, :] = (feats * row_norm(feats)).astype(bf16)
    start = (lax.axis_index("z") * 2 + lax.axis_index("c")) * SHARE
    for k in range(2):
        rows = pl.ds(pl.multiple_of(k * ROWS + start, SHARE), SHARE)
        share_ref[:, k * D : (k + 1) * D] = out_ref[rows, :]


def first_kernel(w_ref, f_ref, p_ref, e_ref, col_ref, sems):
    count = COLS // CHUNK

    def fetch(k):
        lanes = pl.ds(pl.multiple_of(k * CHUNK, CHUNK), CHUNK)
        return pltpu.make_async_copy(w_ref.at[:, lanes], p_ref.at[k], sems.at[k])

    for k in range(count):
        fetch(k).start()

    @pl.loop(0, count)
    def _(k):
        fetch(k).wait()
        sums = []
        for n in range(CHUNK // 256):
            lanes = slice(n * 256, (n + 1) * 256)
            w = p_ref[k, :, lanes].astype(f32)
            inv = lax.rsqrt(jnp.mean(w * w, axis=0, keepdims=True) + 1e-06) / math.sqrt(D)
            p = (w * inv).astype(bf16)
            p_ref[k, :, lanes] = p
            e = jnp.exp2(jnp.dot(f_ref[:ROWS, :], p, preferred_element_type=f32) * KT)
            e_ref[:, pl.ds(pl.multiple_of(k * CHUNK + n * 256, 256), 256)] = e
            for h in range(2):
                sums.append(jnp.sum(e[:, h * 128 : (h + 1) * 128], axis=0, keepdims=True))
        tall = CHUNK // 128
        col_ref[pl.ds(pl.multiple_of(k * tall, tall), tall), :] = jnp.concatenate(sums, axis=0)


def z_kernel(half, after_ref, f_ref, p_ref, z_ref):
    pairs = COLS // CHUNK // 4

    def body(k, zsum):
        for m in range(2):
            chunk = (half * pairs + k) * 2 + m
            for n in range(CHUNK // 256):
                p = p_ref[chunk, :, n * 256 : (n + 1) * 256]
                s = jnp.exp2(jnp.dot(f_ref[ROWS:, :], p, preferred_element_type=f32) * KS)
                zsum = zsum + s[:, :128] + s[:, 128:]
        return zsum

    z_ref[...] = rows_to_lanes(lax.fori_loop(0, pairs, body, jnp.zeros((ROWS, 128), f32)))


def sum_kernel(a_ref, b_ref, c_ref, d_ref, out_ref):
    out_ref[...] = (a_ref[...] + b_ref[...]) + (c_ref[...] + d_ref[...])


def pair_kernel(a_ref, b_ref, out_ref):
    out_ref[...] = a_ref[...] + b_ref[...]


def prep_kernel(after_ref, c_ref, p_ref, pt_ref, cb_ref, done_ref):
    x = lax.axis_index("x")
    y = lax.axis_index("y")
    lanes = pl.ds(pl.multiple_of(lax.rem(y, 2) * OWN, OWN), OWN)
    pt_ref[...] = jnp.transpose(p_ref[x * 2 + lax.div(y, 2), :, lanes].astype(f32)).astype(bf16)
    own = c_ref[pl.ds(pl.multiple_of((x * 4 + y) * 8, 8), 8), :]
    for q in range(8):
        cb_ref[q * 128 : (q + 1) * 128, :] = lanes_to_rows(own[q : q + 1, :], 128)
    done_ref[...] = jnp.zeros_like(done_ref)


def rz_kernel(a_ref, b_ref, c_ref, d_ref, after_ref, out_ref):
    out_ref[...] = GSCALE / ((a_ref[...] + b_ref[...]) + (c_ref[...] + d_ref[...]))


def stack_kernel(a_ref, b_ref, c_ref, d_ref, other_ref, out_ref, kept_ref):
    for d, ref in enumerate((a_ref, b_ref, c_ref, d_ref)):
        out_ref[d] = ref[...]


def sum_z_kernel(a_ref, b_ref, c_ref, d_ref, z_ref, out_ref, z_out):
    out_ref[...] = (a_ref[...] + b_ref[...]) + (c_ref[...] + d_ref[...])
    z_out[...] = z_ref[...]


def row_pass(cols, e_ref, c_ref, acc_ref):
    c_ref[...] = 1.0 / ((cols[0][...] + cols[1][...]) + (cols[2][...] + cols[3][...]))
    tiles = 12

    @pl.loop(0, ROWS // (8 * tiles))
    def _(k):
        base = pl.multiple_of(k * 8 * tiles, 8 * tiles)

        def body(q, accs):
            c8 = c_ref[pl.ds(pl.multiple_of(q * 8, 8), 8), :]
            cs = [jnp.broadcast_to(c8[u : u + 1, :], (8, 128)) for u in range(8)]
            out = []
            for i in range(tiles):
                e = e_ref[
                    pl.ds(pl.multiple_of(base + i * 8, 8), 8),
                    pl.ds(pl.multiple_of(q * 1024, 1024), 1024),
                ]
                p = [e[:, u * 128 : (u + 1) * 128] * cs[u] for u in range(8)]
                while len(p) > 1:
                    p = [p[m] + p[m + 1] for m in range(0, len(p), 2)]
                out.append(accs[i] + p[0])
            return tuple(out)

        zero = jnp.zeros((8, 128), f32)
        accs = lax.fori_loop(0, GROUPS // 8, body, (zero,) * tiles)
        for i in range(tiles):
            acc_ref[pl.ds(pl.multiple_of(base + i * 8, 8), 8), :] = accs[i]

    return rows_to_lanes(acc_ref[...])


def last_row_kernel(c0, c1, c2, c3, z0_ref, z1_ref, *refs):
    e_ref, (c_ref, row_ref), acc = refs[0], refs[KEPT : KEPT + 2], refs[-1]
    row = row_pass((c0, c1, c2, c3), e_ref, c_ref, acc)
    row_ref[...] = jnp.concatenate([row, z0_ref[...] + z1_ref[...]], axis=0)


def row_kernel(c0, c1, c2, c3, *refs):
    e_ref, (c_ref, row_ref), acc = refs[0], refs[KEPT : KEPT + 2], refs[-1]
    row_ref[...] = row_pass((c0, c1, c2, c3), e_ref, c_ref, acc)


def row_z_kernel(c0, c1, c2, c3, z_ref, *refs):
    e_ref, (c_ref, row_ref, z_out), acc = refs[0], refs[KEPT : KEPT + 3], refs[-1]
    row_ref[...] = row_pass((c0, c1, c2, c3), e_ref, c_ref, acc)
    z_out[...] = z_ref[...]


def col_kernel(r0, r1, r2, r3, *refs):
    e_ref, col_ref, rb = refs[0], refs[len(refs) // 2 - 1], refs[-1]
    rb[...] = lanes_to_rows(1.0 / ((r0[...] + r1[...]) + (r2[...] + r3[...])), 128)

    @pl.loop(0, GROUPS // 8)
    def _(q):
        accs = [jnp.zeros((8, 128), f32) for _ in range(8)]
        for i in range(ROWS // 8):
            r = rb[i * 8 : (i + 1) * 8, :]
            e = e_ref[i * 8 : (i + 1) * 8, pl.ds(pl.multiple_of(q * 1024, 1024), 1024)]
            for u in range(8):
                accs[u] = accs[u] + e[:, u * 128 : (u + 1) * 128] * r
        part = jnp.concatenate([jnp.sum(a, axis=0, keepdims=True) for a in accs], axis=0)
        col_ref[pl.ds(pl.multiple_of(q * 8, 8), 8), :] = part


def dz_kernel(rz_ref, c_ref, f_ref, e_ref, p_ref, mine_ref, other_ref, rb, zb, dz_ref):
    rb[...] = lanes_to_rows(rz_ref[0:1, :], 128)
    zb[...] = lanes_to_rows(rz_ref[1:2, :], 128)
    dz_ref[...] = jnp.zeros_like(dz_ref)
    tall = BLOCK // 128

    @pl.loop(0, COLS // BLOCK)
    def _(k):
        cs = c_ref[pl.ds(pl.multiple_of(k * tall, tall), tall), :]
        r = rb[...]
        z = zb[...]
        acc = dz_ref[...]
        for n in range(BLOCK // 256):
            m, at = divmod(n * 256, CHUNK)
            p = p_ref[k * (BLOCK // CHUNK) + m, :, at : at + 256]
            s = jnp.exp2(jnp.dot(f_ref[ROWS:, :], p, preferred_element_type=f32) * KS)
            e = e_ref[:, pl.ds(pl.multiple_of(k * BLOCK + n * 256, 256), 256)]
            parts = []
            for h in range(2):
                lane = slice(h * 128, (h + 1) * 128)
                u = n * 2 + h
                parts.append((s[:, lane] * z - e[:, lane] * r * cs[u : u + 1, :]).astype(bf16))
            g = jnp.concatenate(parts, axis=1)
            acc = acc + lax.dot_general(
                g, p, (((1,), (1,)), ((), ())), preferred_element_type=f32
            )
        dz_ref[...] = acc

    half = ROWS // 2
    core = lax.axis_index("c")
    mine_ref[...] = dz_ref[pl.ds(pl.multiple_of(core * half, half), half), :]
    other_ref[...] = dz_ref[pl.ds(pl.multiple_of((1 - core) * half, half), half), :]


def pg_kernel(r0, r1, r2, r3, pt, cb, f_ref, out_ref, acc, g, rz):
    step = pl.program_id(0)

    @pl.when(step == 0)
    def _():
        acc[...] = jnp.zeros_like(acc)
        x = lax.axis_index("x")
        y = lax.axis_index("y")
        for dx, ref in enumerate((r0, r1, r2, r3)):
            for dy in range(4):
                rz[lax.rem(x - dx + 4, 4) * 4 + lax.rem(y - dy + 4, 4)] = ref[dy]

    t = f_ref[:, :D]
    s = f_ref[:, D:]
    blocks = range(PG_ROWS // ROWS)
    rzs = [rz[step * len(blocks) + b] for b in blocks]
    r = jnp.concatenate([v[0:1, :] for v in rzs], axis=1)
    z = jnp.concatenate([v[1:2, :] for v in rzs], axis=1)
    nt = (((1,), (1,)), ((), ()))
    for n in range(PG_ROWS // 256):
        rows = slice(n * 256, (n + 1) * 256)
        et = jnp.exp2(lax.dot_general(pt[...], t[rows], nt, preferred_element_type=f32) * KT)
        es = jnp.exp2(lax.dot_general(pt[...], s[rows], nt, preferred_element_type=f32) * KS)
        for h in range(2):
            lane = slice(h * 128, (h + 1) * 128)
            to = slice(n * 256 + h * 128, n * 256 + (h + 1) * 128)
            g[:, to] = (es[:, lane] * z[:, to] - et[:, lane] * r[:, to] * cb[...]).astype(bf16)
    acc[...] += jnp.dot(g[...], s, preferred_element_type=f32)

    @pl.when(step == pl.num_programs(0) - 1)
    def _():
        out_ref[...] = jnp.transpose(acc[...])


def in_vmem(x):
    return pltpu.with_memory_space_constraint(x, pltpu.VMEM)


def in_hbm(x):
    return pltpu.with_memory_space_constraint(x, pltpu.HBM)


def around(x, axis):
    parts = [x]
    for d in (1, 2, 3):
        parts.append(lax.ppermute(x, axis, [(i, (i + d) % 4) for i in range(4)]))
    return parts


def row_terms(rowp):
    pair = pl.pallas_call(
        pair_kernel,
        out_shape=pltpu.VMEM(rowp.shape, f32),
        in_specs=[whole()] * 2,
        out_specs=whole(),
        compiler_params=params(5),
        name="pair",
    )(rowp, lax.ppermute(rowp, "c", [(0, 1), (1, 0)]))
    return around(pair, "z")


def z_call(half, after, feats, protos):
    return pl.pallas_call(
        functools.partial(z_kernel, half),
        out_shape=pltpu.VMEM((1, ROWS), f32),
        in_specs=[whole()] * 3,
        out_specs=whole(),
        compiler_params=params(5),
        name="zden",
    )(after, in_vmem(feats), in_vmem(protos))


def shards(teacher_feats, student_feats, proto_weight):
    core = lax.axis_index("c")
    sds = jax.ShapeDtypeStruct
    vmem = pltpu.VMEM
    kept = vmem((ROWS, COLS), f32)

    feats, share = pl.pallas_call(
        norm_kernel,
        grid=(1,),
        out_shape=(vmem((2 * ROWS, D), bf16), sds((SHARE, 2 * D), bf16)),
        in_specs=[pl.BlockSpec((ROWS, D), lambda i: (0, 0))] * 2,
        out_specs=(whole(), whole()),
        compiler_params=params(5),
        name="norm",
    )(in_hbm(teacher_feats), in_hbm(student_feats))
    feats_all = lax.all_gather(share, ALL, axis=0, tiled=True)

    packed = vmem((COLS // CHUNK, D, CHUNK), bf16)
    protos, expo, colp = pl.pallas_call(
        first_kernel,
        out_shape=(packed, kept, vmem((GROUPS, 128), f32)),
        in_specs=[pl.BlockSpec(memory_space=pl.ANY), whole()],
        out_specs=(whole(), whole(), whole()),
        scratch_shapes=[pltpu.SemaphoreType.DMA((COLS // CHUNK,))],
        compiler_params=params(5),
        name="first",
    )(in_hbm(proto_weight), in_vmem(feats))

    keep = [expo, protos]
    shapes = [kept, packed]
    for step in range(ITERS):
        parts = around(colp, "y")
        if step == 2:
            z1 = z_call(1, colp, feats, keep[1])
            colp, z1 = pl.pallas_call(
                sum_z_kernel,
                out_shape=(vmem((GROUPS, 128), f32), vmem((1, ROWS), f32)),
                in_specs=[whole()] * 5,
                out_specs=(whole(), whole()),
                compiler_params=params(5),
                name="sum_z",
            )(*parts, z1)
        else:
            colp = pl.pallas_call(
                sum_kernel,
                out_shape=vmem((GROUPS, 128), f32),
                in_specs=[whole()] * 4,
                out_specs=whole(),
                compiler_params=params(5),
                name="sum",
            )(*parts)
        parts = around(colp, "x")
        if step == 2:
            break
        if step == 0:
            unused, rowp, *keep = pl.pallas_call(
                row_kernel,
                out_shape=[vmem((GROUPS, 128), f32), vmem((1, ROWS), f32)] + shapes,
                in_specs=[whole()] * (4 + KEPT),
                out_specs=[whole()] * (2 + KEPT),
                input_output_aliases={4 + k: 2 + k for k in range(KEPT)},
                scratch_shapes=[vmem((ROWS, 128), f32)],
                compiler_params=params(5),
                name="row",
            )(*parts, *map(in_vmem, keep))
        else:
            z0 = z_call(0, colp, feats, keep[1])
            unused, rowp, z0, *keep = pl.pallas_call(
                row_z_kernel,
                out_shape=[vmem((GROUPS, 128), f32), vmem((1, ROWS), f32), vmem((1, ROWS), f32)]
                + shapes,
                in_specs=[whole()] * (5 + KEPT),
                out_specs=[whole()] * (3 + KEPT),
                input_output_aliases={5 + k: 3 + k for k in range(KEPT)},
                scratch_shapes=[vmem((ROWS, 128), f32)],
                compiler_params=params(5),
                name="row",
            )(*parts, in_vmem(z0), *map(in_vmem, keep))
        rowps = row_terms(rowp)
        colp, *keep = pl.pallas_call(
            col_kernel,
            out_shape=[vmem((GROUPS, 128), f32)] + shapes,
            in_specs=[whole()] * (4 + len(keep)),
            out_specs=[whole()] * (1 + len(keep)),
            input_output_aliases={4 + k: 1 + k for k in range(len(keep))},
            scratch_shapes=[vmem((ROWS, 128), f32)],
            compiler_params=params(5),
            name="col",
        )(*rowps, *map(in_vmem, keep))

    colsc, rzp, *keep = pl.pallas_call(
        last_row_kernel,
        out_shape=[vmem((GROUPS, 128), f32), vmem((2, ROWS), f32)] + shapes,
        in_specs=[whole()] * (6 + KEPT),
        out_specs=[whole()] * (2 + KEPT),
        input_output_aliases={6 + k: 2 + k for k in range(KEPT)},
        scratch_shapes=[vmem((ROWS, 128), f32)],
        compiler_params=params(5),
        name="row_last",
    )(*parts, in_vmem(z0), in_vmem(z1), *map(in_vmem, keep))
    terms = row_terms(rzp)
    pt, cb, token = pl.pallas_call(
        prep_kernel,
        out_shape=(vmem((OWN, D), bf16), vmem((OWN, 128), f32), vmem((8, 128), f32)),
        in_specs=[whole()] * 3,
        out_specs=(whole(),) * 3,
        compiler_params=params(5),
        name="prep",
    )(terms[0], in_vmem(colsc), in_vmem(keep[1]))
    rz = pl.pallas_call(
        rz_kernel,
        out_shape=vmem((2, ROWS), f32),
        in_specs=[whole()] * 5,
        out_specs=whole(),
        compiler_params=params(5),
        name="rz",
    )(*terms, token)
    rz_y = around(rz, "y")

    half = ROWS // 2
    mine, other = pl.pallas_call(
        dz_kernel,
        out_shape=(vmem((half, D), f32), vmem((half, D), f32)),
        in_specs=[whole()] * 5,
        out_specs=(whole(), whole()),
        scratch_shapes=[vmem((ROWS, 128), f32)] * 2 + [vmem((ROWS, D), f32)],
        compiler_params=params(5),
        name="dz",
    )(in_vmem(rz), in_vmem(colsc), in_vmem(feats), *map(in_vmem, keep))

    rz_rows, other = pl.pallas_call(
        stack_kernel,
        out_shape=(vmem((4, 2, ROWS), f32), vmem((half, D), f32)),
        in_specs=[whole()] * 5,
        out_specs=(whole(), whole()),
        input_output_aliases={4: 1},
        compiler_params=params(5),
        name="stack",
    )(*rz_y, other)
    rz_all = around(rz_rows, "x")

    got = lax.ppermute(other, "c", [(0, 1), (1, 0)])
    parts = around(mine + got, "z")

    proto_grad = pl.pallas_call(
        pg_kernel,
        grid=(NB * ROWS // PG_ROWS,),
        out_shape=sds((D, OWN), f32),
        in_specs=[whole()] * 6 + [pl.BlockSpec((PG_ROWS, 2 * D), lambda i: (i, 0))],
        out_specs=pl.BlockSpec((D, OWN), lambda i: (0, 0)),
        scratch_shapes=[
            vmem((OWN, D), f32),
            vmem((OWN, PG_ROWS), bf16),
            vmem((NB, 2, ROWS), f32),
        ],
        compiler_params=params(30),
        cost_estimate=pl.CostEstimate(flops=9700000000, bytes_accessed=8000000, transcendentals=12600000),
        name="pg",
    )(*rz_all, in_vmem(pt), in_vmem(cb), in_hbm(feats_all))

    parts, proto_grad, student_feats = lax.optimization_barrier(
        (parts, proto_grad, student_feats)
    )
    dz = (parts[0] + parts[2]) + (parts[1] + parts[3])
    feats = lax.dynamic_slice(student_feats, (core * half, 0), (half, D)).astype(f32)
    rnorm = row_norm(feats)
    stud_f = feats * rnorm
    grad = (dz - stud_f * jnp.sum(stud_f * dz, axis=1, keepdims=True)) * rnorm
    sibling = lax.ppermute(grad, "c", [(0, 1), (1, 0)])
    feat_grad = jnp.where(
        core == 0,
        jnp.concatenate([grad, sibling], axis=0),
        jnp.concatenate([sibling, grad], axis=0),
    )
    return (feat_grad, proto_grad)


def solution(mesh):
    grid = Mesh(mesh.devices.reshape(4, 4, 4, 2), ("x", "y", "z", "c"))
    in_specs = (P(XY, None), P(XY, None), P(None, ZC))
    out_specs = (P(XY, None), P(None, ZC + XY))
    return jax.shard_map(shards, mesh=grid, in_specs=in_specs, out_specs=out_specs, check_vma=False)
```

time: 161 us -> 156 us (0.969)
  Pallas kernels: 59.9 us -> 53.5 us
    pallas_call x10 -> x11, Pallas kernels: 58 us -> 51.6 us  [the longest x1 16.1 us: shards(): pl.pallas_call(pg_kernel, grid=(NB * ROWS // PG_ROWS,), out_shape=sds((D,...]
  transfers between devices with their start and end apart: 42 -> 42, of which waited for: 22 -> 24; matrix products, arithmetic and copies ran while one was open for 0% -> 0% of each run, Pallas kernels for 36% -> 33%
where the time goes in v4:
time: 156 us
  starting transfers between devices  64.7 us (41%)
  Pallas kernels  53.5 us (34%)
  waiting for transfers between devices  21.9 us (14%)
  between operations  14.2 us (9%)
    ppermute x36, starting transfers between devices, around(): parts.append(lax.ppermute(x, axis, [(i, (i + d) % 4) for i in range(4)]))  46.7 us
    ppermute x36, waiting for transfers between devices, around(): parts.append(lax.ppermute(x, axis, [(i, (i + d) % 4) for i in range(4)]))  18.4 us
    pallas_call x1, Pallas kernels, shards(): pl.pallas_call(pg_kernel, grid=(NB * ROWS // PG_ROWS,), out_shape=sds((D,...  16.1 us
    ppermute x3, starting transfers between devices, row_terms(): lax.ppermute(rowp, 'c', [(0, 1), (1, 0)])  13.9 us
    pallas_call x1, Pallas kernels, shards(): pl.pallas_call(first_kernel, out_shape=(packed, kept, vmem((GROUPS, 128),...  9.24 us
    pallas_call x1, Pallas kernels, shards(): pl.pallas_call(dz_kernel, out_shape=(vmem((half, D), f32), vmem((half, D)...  8.94 us
    pallas_call x2, Pallas kernels, z_call(): pl.pallas_call(functools.partial(z_kernel, half), out_shape=pltpu.VMEM((1...  4.34 us
    pallas_call x2, Pallas kernels, shards(): pl.pallas_call(col_kernel, out_shape=[vmem((GROUPS, 128), f32)] + shapes,...  4.3 us
  transfers between devices with their start and end apart: 42, of which 24 were waited for; matrix products, arithmetic and copies ran while one was open for 0% of the time, Pallas kernels for 33%

profile of v4, /device:TPU:1, one launch (start us, length us, event | category | flops | bytes accessed | tf_op | source)
XLA Modules:
  0.0 155.6 jit_solution(13395920303770390199)
XLA Ops:
  9.1 9.2 %first.1 = (bf16[8,256,2048]{2,1,0:T(8,128)(2,1)S(1)}, f32[384,16384]{1,0:T(8,128)S(1)}, f32[128,128]{1,0:T(8,128)S(1)}) custom-call(bf16[256,16384]{1,0:T(8,128)(2,1)} %w_ref.1, bf16[768,256]{1,0:T(8,128)(2,1)S(1)} %get-tuple-element.39.f_ref), custom_call_target="tpu_custom_call" | custom-call | tf_op jit(solution)/shard_map/first/pallas_call | solution.py:330
  18.3 2.2 %collective-permute-start = (f32[128,128]{1,0:T(8,128)S(1)}, f32[128,128]{1,0:T(8,128)S(1)}, u32[]{:S(2)}, u32[]{:S(2)}) collective-permute-start(f32[128,128]{1,0:T(8,128)S(1)} %get-tuple-element.40.a_ref), channel_id=1, source_target_pairs={{0,8},{8,16},{16,24},{24,0},{1,9},{9,17},{17,25},{25,1},{2,10},{10... | collective-permute-start | bytes 196616 | tf_op jit(solution)/shard_map/ppermute | solution.py:285
  20.5 2.6 %collective-permute-start.1 = (f32[128,128]{1,0:T(8,128)S(1)}, f32[128,128]{1,0:T(8,128)S(1)}, u32[]{:S(2)}, u32[]{:S(2)}) collective-permute-start(f32[128,128]{1,0:T(8,128)S(1)} %get-tuple-element.40.a_ref), channel_id=1, source_target_pairs={{0,16},{8,24},{16,0},{24,8},{1,17},{9,25},{17,1},{25,9},{2,18},{10... | collective-permute-start | bytes 196616 | tf_op jit(solution)/shard_map/ppermute | solution.py:285
  27.9 2.4 %collective-permute-start.4 = (f32[128,128]{1,0:T(8,128)S(1)}, f32[128,128]{1,0:T(8,128)S(1)}, u32[]{:S(2)}, u32[]{:S(2)}) collective-permute-start(f32[128,128]{1,0:T(8,128)S(1)} %sum.2.c0), channel_id=1, source_target_pairs={{0,64},{32,96},{64,0},{96,32},{1,65},{33,97},{65,1},{97,33},{2,66}... | collective-permute-start | bytes 196616 | tf_op jit(solution)/shard_map/ppermute | solution.py:285
  33.9 2.9 %row.2 = (f32[128,128]{1,0:T(8,128)}, f32[1,384]{1,0:T(1,128)S(1)}, f32[384,16384]{1,0:T(8,128)S(1)}, bf16[8,256,2048]{2,1,0:T(8,128)(2,1)S(1)}) custom-call(f32[128,128]{1,0:T(8,128)S(1)} %sum.2.c0, f32[128,128]{1,0:T(8,128)S(1)} %collective-permute-done.3.c1, ...), custom_call_target="tpu_custom_call", output_to_operand_aliasing={{2}: (4, {}), {3}: (5, {})} | custom-call | tf_op jit(solution)/shard_map/row/pallas_call | solution.py:367
  36.8 3.4 %collective-permute-start.6 = (f32[1,384]{1,0:T(1,128)S(1)}, f32[1,384]{1,0:T(1,128)S(1)}, u32[]{:S(2)}, u32[]{:S(2)}) collective-permute-start(f32[1,384]{1,0:T(1,128)S(1)} %get-tuple-element.43.a_ref), channel_id=1, source_target_pairs={{0,1},{1,0},{2,3},{3,2},{4,5},{5,4},{6,7},{7,6},{8,9},{9,8},{10,11... | collective-permute-start | bytes 4616 | tf_op jit(solution)/shard_map/ppermute | solution.py:297
  42.8 3.2 %collective-permute-start.8 = (f32[1,384]{1,0:T(1,128)S(1)}, f32[1,384]{1,0:T(1,128)S(1)}, u32[]{:S(2)}, u32[]{:S(2)}) collective-permute-start(f32[1,384]{1,0:T(1,128)S(1)} %pair.3.r0), channel_id=1, source_target_pairs={{0,4},{2,6},{4,0},{6,2},{1,5},{3,7},{5,1},{7,3},{8,12},{10,14},{12... | collective-permute-start | bytes 4616 | tf_op jit(solution)/shard_map/ppermute | solution.py:285
  48.8 2.1 %col.2 = (f32[128,128]{1,0:T(8,128)S(1)}, f32[384,16384]{1,0:T(8,128)S(1)}, bf16[8,256,2048]{2,1,0:T(8,128)(2,1)S(1)}) custom-call(f32[1,384]{1,0:T(1,128)S(1)} %pair.3.r0, f32[1,384]{1,0:T(1,128)S(1)} %collective-permute-done.7.r1, f32[1,384]{1,0:T(1,128)S(1)} %collective-permute-done.8.r2, ...), custom_call_target="tpu_custom_call", output_to_operand_aliasing={{1}: (4, {}), {2}: (5, {})} | custom-call | tf_op jit(solution)/shard_map/col/pallas_call | solution.py:391
  51.1 3.3 %collective-permute-start.11 = (f32[128,128]{1,0:T(8,128)S(1)}, f32[128,128]{1,0:T(8,128)S(1)}, u32[]{:S(2)}, u32[]{:S(2)}) collective-permute-start(f32[128,128]{1,0:T(8,128)S(1)} %get-tuple-element.46.a_ref), channel_id=1, source_target_pairs={{0,16},{8,24},{16,0},{24,8},{1,17},{9,25},{17,1},{25,9},{2,18},{10... | collective-permute-start | bytes 196616 | tf_op jit(solution)/shard_map/ppermute | solution.py:285
  58.9 2.7 %collective-permute-start.14 = (f32[128,128]{1,0:T(8,128)S(1)}, f32[128,128]{1,0:T(8,128)S(1)}, u32[]{:S(2)}, u32[]{:S(2)}) collective-permute-start(f32[128,128]{1,0:T(8,128)S(1)} %sum.3.after_ref.c0), channel_id=1, source_target_pairs={{0,64},{32,96},{64,0},{96,32},{1,65},{33,97},{65,1},{97,33},{2,66}... | collective-permute-start | bytes 196616 | tf_op jit(solution)/shard_map/ppermute | solution.py:285
  61.9 2.2 %zden.2.z_ref = f32[1,384]{1,0:T(1,128)S(1)} custom-call(f32[128,128]{1,0:T(8,128)S(1)} %sum.3.after_ref.c0, bf16[768,256]{1,0:T(8,128)(2,1)S(1)} %get-tuple-element.39.f_ref, bf16[8,256,2048]{2,1,0:T(8,128)(2,1)S(1)} %get-tuple-element.47.p_ref.refs_1_), custom_call_target="tpu_custom_call" | custom-call | tf_op jit(solution)/shard_map/zden/pallas_call | solution.py:302
  64.7 2.9 %row.3 = (f32[128,128]{1,0:T(8,128)}, f32[1,384]{1,0:T(1,128)S(1)}, f32[1,384]{1,0:T(1,128)S(1)}, f32[384,16384]{1,0:T(8,128)S(1)}, bf16[8,256,2048]{2,1,0:T(8,128)(2,1)S(1)}) custom-call(f32[128,128]{1,0:T(8,128)S(1)} %sum.3.after_ref.c0, f32[128,128]{1,0:T(8,128)S(1)} %collective-permute-done.13.c1, ...), custom_call_target="tpu_custom_call", output_to_operand_aliasing={{3}: (5, {}), {4}: (6, {})} | custom-call | tf_op jit(solution)/shard_map/row/pallas_call | solution.py:379
  67.6 5.8 %collective-permute-start.16 = (f32[1,384]{1,0:T(1,128)S(1)}, f32[1,384]{1,0:T(1,128)S(1)}, u32[]{:S(2)}, u32[]{:S(2)}) collective-permute-start(f32[1,384]{1,0:T(1,128)S(1)} %get-tuple-element.49.a_ref), channel_id=1, source_target_pairs={{0,1},{1,0},{2,3},{3,2},{4,5},{5,4},{6,7},{7,6},{8,9},{9,8},{10,11... | collective-permute-start | bytes 4616 | tf_op jit(solution)/shard_map/ppermute | solution.py:297
  74.2 3.2 %collective-permute-start.18 = (f32[1,384]{1,0:T(1,128)S(1)}, f32[1,384]{1,0:T(1,128)S(1)}, u32[]{:S(2)}, u32[]{:S(2)}) collective-permute-start(f32[1,384]{1,0:T(1,128)S(1)} %pair.4.r0), channel_id=1, source_target_pairs={{0,4},{2,6},{4,0},{6,2},{1,5},{3,7},{5,1},{7,3},{8,12},{10,14},{12... | collective-permute-start | bytes 4616 | tf_op jit(solution)/shard_map/ppermute | solution.py:285
  85.1 2.2 %zden.3.z_ref = f32[1,384]{1,0:T(1,128)S(1)} custom-call(f32[128,128]{1,0:T(8,128)S(1)} %get-tuple-element.52.after_ref.a_ref, bf16[768,256]{1,0:T(8,128)(2,1)S(1)} %get-tuple-element.39.f_ref, bf16[8,256,2048]{2,1,0:T(8,128)(2,1)S(1)} %get-tuple-element.53.p_ref.refs_1_), custom_call_target="tpu_custom_call" | custom-call | tf_op jit(solution)/shard_map/zden/pallas_call | solution.py:302
  88.2 2.4 %collective-permute-start.24 = (f32[128,128]{1,0:T(8,128)S(1)}, f32[128,128]{1,0:T(8,128)S(1)}, u32[]{:S(2)}, u32[]{:S(2)}) collective-permute-start(f32[128,128]{1,0:T(8,128)S(1)} %get-tuple-element.54.c0), channel_id=1, source_target_pairs={{0,64},{32,96},{64,0},{96,32},{1,65},{33,97},{65,1},{97,33},{2,66}... | collective-permute-start | bytes 196616 | tf_op jit(solution)/shard_map/ppermute | solution.py:285
  93.8 2.4 %row_last.1 = (f32[128,128]{1,0:T(8,128)S(1)}, f32[2,384]{1,0:T(2,128)S(1)}, f32[384,16384]{1,0:T(8,128)S(1)}, bf16[8,256,2048]{2,1,0:T(8,128)(2,1)S(1)}) custom-call(f32[128,128]{1,0:T(8,128)S(1)} %get-tuple-element.54.c0, f32[128,128]{1,0:T(8,128)S(1)} %collective-permute-done.23.c1, ...), custom_call_target="tpu_custom_call", output_to_operand_aliasing={{2}: (6, {}), {3}: (7, {})} | custom-call | tf_op jit(solution)/shard_map/row_last/pallas_call | solution.py:402
  96.2 4.8 %collective-permute-start.26 = (f32[2,384]{1,0:T(2,128)S(1)}, f32[2,384]{1,0:T(2,128)S(1)}, u32[]{:S(2)}, u32[]{:S(2)}) collective-permute-start(f32[2,384]{1,0:T(2,128)S(1)} %get-tuple-element.58.a_ref), channel_id=1, source_target_pairs={{0,1},{1,0},{2,3},{3,2},{4,5},{5,4},{6,7},{7,6},{8,9},{9,8},{10,11... | collective-permute-start | bytes 9224 | tf_op jit(solution)/shard_map/ppermute | solution.py:297
  107.7 2.3 %collective-permute-start.31 = (f32[2,384]{1,0:T(2,128)S(1)}, f32[2,384]{1,0:T(2,128)S(1)}, u32[]{:S(2)}, u32[]{:S(2)}) collective-permute-start(f32[2,384]{1,0:T(2,128)S(1)} %rz.1.rz_ref.a_ref), channel_id=1, source_target_pairs={{0,16},{8,24},{16,0},{24,8},{1,17},{9,25},{17,1},{25,9},{2,18},{10... | collective-permute-start | bytes 9224 | tf_op jit(solution)/shard_map/ppermute | solution.py:285
  110.2 8.9 %dz.1 = (f32[192,256]{1,0:T(8,128)S(1)}, f32[192,256]{1,0:T(8,128)S(1)}) custom-call(f32[2,384]{1,0:T(2,128)S(1)} %rz.1.rz_ref.a_ref, f32[128,128]{1,0:T(8,128)S(1)} %get-tuple-element.59.c_ref, bf16[768,256]{1,0:T(8,128)(2,1)S(1)} %get-tuple-element.39.f_ref, f32[384,16384]{1,0:T(8,128)S(1)} %get-tuple-element.62.e_ref, ...), custom_call_target="tpu_custom_call" | custom-call | tf_op jit(solution)/shard_map/dz/pallas_call | solution.py:432
  119.2 2.4 %collective-permute-start.33 = (f32[192,256]{1,0:T(8,128)S(1)}, f32[192,256]{1,0:T(8,128)S(1)}, u32[]{:S(2)}, u32[]{:S(2)}) collective-permute-start(f32[192,256]{1,0:T(8,128)S(1)} %get-tuple-element.65), channel_id=1, source_target_pairs={{0,1},{1,0},{2,3},{3,2},{4,5},{5,4},{6,7},{7,6},{8,9},{9,8},{10,11... | collective-permute-start | bytes 589832 | tf_op jit(solution)/shard_map/ppermute | solution.py:453
  122.5 2.5 %collective-permute-start.38 = (f32[4,2,384]{2,1,0:T(2,128)S(1)}, f32[4,2,384]{2,1,0:T(2,128)S(1)}, u32[]{:S(2)}, u32[]{:S(2)}) collective-permute-start(f32[4,2,384]{2,1,0:T(2,128)S(1)} %get-tuple-element.66.r0), channel_id=1, source_target_pairs={{0,64},{32,96},{64,0},{96,32},{1,65},{33,97},{65,1},{97,33},{2,66}... | collective-permute-start | bytes 36872 | tf_op jit(solution)/shard_map/ppermute | solution.py:285
  126.2 2.4 %collective-permute-start.35 = (f32[192,256]{1,0:T(8,128)S(1)}, f32[192,256]{1,0:T(8,128)S(1)}, u32[]{:S(2)}, u32[]{:S(2)}) collective-permute-start(f32[192,256]{1,0:T(8,128)S(1)} %add.26), channel_id=1, source_target_pairs={{0,4},{2,6},{4,0},{6,2},{1,5},{3,7},{5,1},{7,3},{8,12},{10,14},{12... | collective-permute-start | bytes 589832 | tf_op jit(solution)/shard_map/ppermute | solution.py:285
  128.7 16.1 %pg.1 = f32[256,1024]{1,0:T(8,128)} custom-call(f32[4,2,384]{2,1,0:T(2,128)S(1)} %get-tuple-element.66.r0, f32[4,2,384]{2,1,0:T(2,128)S(1)} %collective-permute-done.37.r1, f32[4,2,384]{2,1,0:T(2,128)S(1)} %collective-permute-done.38.r2, f32[4,2,384]{2,1,0:T(2,128)S(1)} %collective-permute-done.39.r3, bf16[1024,256]{1,0:T(8,128)(2,1)S(1)} %get-tuple-element.67.pt, ...), custom_call_target="tpu_custom_call" | custom-call | flops 9699999744 | bytes 8000000 | tf_op jit(solution)/shard_map/pg/pallas_call | solution.py:456
  (89 shorter events, 46.5 us)
Async XLA Ops:
  7.2 121.6 %all-gather.2.cloned.1.call-start = ((), (), s32[]{:S(2)}) async-start(), calls=%async_computation | async-start | bytes 6340608 | tf_op jit(solution)/shard_map/all_gather | solution.py:327
  18.3 5.9 %collective-permute-start = (f32[128,128]{1,0:T(8,128)S(1)}, f32[128,128]{1,0:T(8,128)S(1)}, u32[]{:S(2)}, u32[]{:S(2)}) collective-permute-start(f32[128,128]{1,0:T(8,128)S(1)} %get-tuple-element.40.a_ref), channel_id=1, source_target_pairs={{0,8},{8,16},{16,24},{24,0},{1,9},{9,17},{17,25},{25,1},{2,10},{10... | collective-permute-start | bytes 196616 | tf_op jit(solution)/shard_map/ppermute | solution.py:285
  20.5 5.2 %collective-permute-start.1 = (f32[128,128]{1,0:T(8,128)S(1)}, f32[128,128]{1,0:T(8,128)S(1)}, u32[]{:S(2)}, u32[]{:S(2)}) collective-permute-start(f32[128,128]{1,0:T(8,128)S(1)} %get-tuple-element.40.a_ref), channel_id=1, source_target_pairs={{0,16},{8,24},{16,0},{24,8},{1,17},{9,25},{17,1},{25,9},{2,18},{10... | collective-permute-start | bytes 196616 | tf_op jit(solution)/shard_map/ppermute | solution.py:285
  26.6 4.9 %collective-permute-start.3 = (f32[128,128]{1,0:T(8,128)S(1)}, f32[128,128]{1,0:T(8,128)S(1)}, u32[]{:S(2)}, u32[]{:S(2)}) collective-permute-start(f32[128,128]{1,0:T(8,128)S(1)} %sum.2.c0), channel_id=1, source_target_pairs={{0,32},{32,64},{64,96},{96,0},{1,33},{33,65},{65,97},{97,1},{2,34}... | collective-permute-start | bytes 196616 | tf_op jit(solution)/shard_map/ppermute | solution.py:285
  27.9 4.8 %collective-permute-start.4 = (f32[128,128]{1,0:T(8,128)S(1)}, f32[128,128]{1,0:T(8,128)S(1)}, u32[]{:S(2)}, u32[]{:S(2)}) collective-permute-start(f32[128,128]{1,0:T(8,128)S(1)} %sum.2.c0), channel_id=1, source_target_pairs={{0,64},{32,96},{64,0},{96,32},{1,65},{33,97},{65,1},{97,33},{2,66}... | collective-permute-start | bytes 196616 | tf_op jit(solution)/shard_map/ppermute | solution.py:285
  41.0 5.8 %collective-permute-start.7 = (f32[1,384]{1,0:T(1,128)S(1)}, f32[1,384]{1,0:T(1,128)S(1)}, u32[]{:S(2)}, u32[]{:S(2)}) collective-permute-start(f32[1,384]{1,0:T(1,128)S(1)} %pair.3.r0), channel_id=1, source_target_pairs={{0,2},{2,4},{4,6},{6,0},{1,3},{3,5},{5,7},{7,1},{8,10},{10,12},{12... | collective-permute-start | bytes 4616 | tf_op jit(solution)/shard_map/ppermute | solution.py:285
  51.1 5.7 %collective-permute-start.11 = (f32[128,128]{1,0:T(8,128)S(1)}, f32[128,128]{1,0:T(8,128)S(1)}, u32[]{:S(2)}, u32[]{:S(2)}) collective-permute-start(f32[128,128]{1,0:T(8,128)S(1)} %get-tuple-element.46.a_ref), channel_id=1, source_target_pairs={{0,16},{8,24},{16,0},{24,8},{1,17},{9,25},{17,1},{25,9},{2,18},{10... | collective-permute-start | bytes 196616 | tf_op jit(solution)/shard_map/ppermute | solution.py:285
  58.3 5.8 %collective-permute-start.13 = (f32[128,128]{1,0:T(8,128)S(1)}, f32[128,128]{1,0:T(8,128)S(1)}, u32[]{:S(2)}, u32[]{:S(2)}) collective-permute-start(f32[128,128]{1,0:T(8,128)S(1)} %sum.3.after_ref.c0), channel_id=1, source_target_pairs={{0,32},{32,64},{64,96},{96,0},{1,33},{33,65},{65,97},{97,1},{2,34}... | collective-permute-start | bytes 196616 | tf_op jit(solution)/shard_map/ppermute | solution.py:285
  58.9 5.2 %collective-permute-start.14 = (f32[128,128]{1,0:T(8,128)S(1)}, f32[128,128]{1,0:T(8,128)S(1)}, u32[]{:S(2)}, u32[]{:S(2)}) collective-permute-start(f32[128,128]{1,0:T(8,128)S(1)} %sum.3.after_ref.c0), channel_id=1, source_target_pairs={{0,64},{32,96},{64,0},{96,32},{1,65},{33,97},{65,1},{97,33},{2,66}... | collective-permute-start | bytes 196616 | tf_op jit(solution)/shard_map/ppermute | solution.py:285
  67.6 6.6 %collective-permute-start.16 = (f32[1,384]{1,0:T(1,128)S(1)}, f32[1,384]{1,0:T(1,128)S(1)}, u32[]{:S(2)}, u32[]{:S(2)}) collective-permute-start(f32[1,384]{1,0:T(1,128)S(1)} %get-tuple-element.49.a_ref), channel_id=1, source_target_pairs={{0,1},{1,0},{2,3},{3,2},{4,5},{5,4},{6,7},{7,6},{8,9},{9,8},{10,11... | collective-permute-start | bytes 4616 | tf_op jit(solution)/shard_map/ppermute | solution.py:297
  82.4 5.0 %collective-permute-start.20 = (f32[128,128]{1,0:T(8,128)S(1)}, f32[128,128]{1,0:T(8,128)S(1)}, u32[]{:S(2)}, u32[]{:S(2)}) collective-permute-start(f32[128,128]{1,0:T(8,128)S(1)} %get-tuple-element.52.after_ref.a_ref), channel_id=1, source_target_pairs={{0,8},{8,16},{16,24},{24,0},{1,9},{9,17},{17,25},{25,1},{2,10},{10... | collective-permute-start | bytes 196616 | tf_op jit(solution)/shard_map/ppermute | solution.py:285
  82.5 5.1 %collective-permute-start.21 = (f32[128,128]{1,0:T(8,128)S(1)}, f32[128,128]{1,0:T(8,128)S(1)}, u32[]{:S(2)}, u32[]{:S(2)}) collective-permute-start(f32[128,128]{1,0:T(8,128)S(1)} %get-tuple-element.52.after_ref.a_ref), channel_id=1, source_target_pairs={{0,16},{8,24},{16,0},{24,8},{1,17},{9,25},{17,1},{25,9},{2,18},{10... | collective-permute-start | bytes 196616 | tf_op jit(solution)/shard_map/ppermute | solution.py:285
  88.1 5.1 %collective-permute-start.23 = (f32[128,128]{1,0:T(8,128)S(1)}, f32[128,128]{1,0:T(8,128)S(1)}, u32[]{:S(2)}, u32[]{:S(2)}) collective-permute-start(f32[128,128]{1,0:T(8,128)S(1)} %get-tuple-element.54.c0), channel_id=1, source_target_pairs={{0,32},{32,64},{64,96},{96,0},{1,33},{33,65},{65,97},{97,1},{2,34}... | collective-permute-start | bytes 196616 | tf_op jit(solution)/shard_map/ppermute | solution.py:285
  88.2 5.0 %collective-permute-start.24 = (f32[128,128]{1,0:T(8,128)S(1)}, f32[128,128]{1,0:T(8,128)S(1)}, u32[]{:S(2)}, u32[]{:S(2)}) collective-permute-start(f32[128,128]{1,0:T(8,128)S(1)} %get-tuple-element.54.c0), channel_id=1, source_target_pairs={{0,64},{32,96},{64,0},{96,32},{1,65},{33,97},{65,1},{97,33},{2,66}... | collective-permute-start | bytes 196616 | tf_op jit(solution)/shard_map/ppermute | solution.py:285
  96.2 5.6 %collective-permute-start.26 = (f32[2,384]{1,0:T(2,128)S(1)}, f32[2,384]{1,0:T(2,128)S(1)}, u32[]{:S(2)}, u32[]{:S(2)}) collective-permute-start(f32[2,384]{1,0:T(2,128)S(1)} %get-tuple-element.58.a_ref), channel_id=1, source_target_pairs={{0,1},{1,0},{2,3},{3,2},{4,5},{5,4},{6,7},{7,6},{8,9},{9,8},{10,11... | collective-permute-start | bytes 9224 | tf_op jit(solution)/shard_map/ppermute | solution.py:297
  106.7 12.5 %collective-permute-start.30 = (f32[2,384]{1,0:T(2,128)S(1)}, f32[2,384]{1,0:T(2,128)S(1)}, u32[]{:S(2)}, u32[]{:S(2)}) collective-permute-start(f32[2,384]{1,0:T(2,128)S(1)} %rz.1.rz_ref.a_ref), channel_id=1, source_target_pairs={{0,8},{8,16},{16,24},{24,0},{1,9},{9,17},{17,25},{25,1},{2,10},{10... | collective-permute-start | bytes 9224 | tf_op jit(solution)/shard_map/ppermute | solution.py:285
  107.7 11.4 %collective-permute-start.31 = (f32[2,384]{1,0:T(2,128)S(1)}, f32[2,384]{1,0:T(2,128)S(1)}, u32[]{:S(2)}, u32[]{:S(2)}) collective-permute-start(f32[2,384]{1,0:T(2,128)S(1)} %rz.1.rz_ref.a_ref), channel_id=1, source_target_pairs={{0,16},{8,24},{16,0},{24,8},{1,17},{9,25},{17,1},{25,9},{2,18},{10... | collective-permute-start | bytes 9224 | tf_op jit(solution)/shard_map/ppermute | solution.py:285
  110.0 9.1 %collective-permute-start.32 = (f32[2,384]{1,0:T(2,128)S(1)}, f32[2,384]{1,0:T(2,128)S(1)}, u32[]{:S(2)}, u32[]{:S(2)}) collective-permute-start(f32[2,384]{1,0:T(2,128)S(1)} %rz.1.rz_ref.a_ref), channel_id=1, source_target_pairs={{0,24},{8,0},{16,8},{24,16},{1,25},{9,1},{17,9},{25,17},{2,26},{10... | collective-permute-start | bytes 9224 | tf_op jit(solution)/shard_map/ppermute | solution.py:285
  119.2 5.9 %collective-permute-start.33 = (f32[192,256]{1,0:T(8,128)S(1)}, f32[192,256]{1,0:T(8,128)S(1)}, u32[]{:S(2)}, u32[]{:S(2)}) collective-permute-start(f32[192,256]{1,0:T(8,128)S(1)} %get-tuple-element.65), channel_id=1, source_target_pairs={{0,1},{1,0},{2,3},{3,2},{4,5},{5,4},{6,7},{7,6},{8,9},{9,8},{10,11... | collective-permute-start | bytes 589832 | tf_op jit(solution)/shard_map/ppermute | solution.py:453
  121.6 7.0 %collective-permute-start.37 = (f32[4,2,384]{2,1,0:T(2,128)S(1)}, f32[4,2,384]{2,1,0:T(2,128)S(1)}, u32[]{:S(2)}, u32[]{:S(2)}) collective-permute-start(f32[4,2,384]{2,1,0:T(2,128)S(1)} %get-tuple-element.66.r0), channel_id=1, source_target_pairs={{0,32},{32,64},{64,96},{96,0},{1,33},{33,65},{65,97},{97,1},{2,34}... | collective-permute-start | bytes 36872 | tf_op jit(solution)/shard_map/ppermute | solution.py:285
  122.5 6.2 %collective-permute-start.38 = (f32[4,2,384]{2,1,0:T(2,128)S(1)}, f32[4,2,384]{2,1,0:T(2,128)S(1)}, u32[]{:S(2)}, u32[]{:S(2)}) collective-permute-start(f32[4,2,384]{2,1,0:T(2,128)S(1)} %get-tuple-element.66.r0), channel_id=1, source_target_pairs={{0,64},{32,96},{64,0},{96,32},{1,65},{33,97},{65,1},{97,33},{2,66}... | collective-permute-start | bytes 36872 | tf_op jit(solution)/shard_map/ppermute | solution.py:285
  125.1 19.8 %collective-permute-start.34 = (f32[192,256]{1,0:T(8,128)S(1)}, f32[192,256]{1,0:T(8,128)S(1)}, u32[]{:S(2)}, u32[]{:S(2)}) collective-permute-start(f32[192,256]{1,0:T(8,128)S(1)} %add.26), channel_id=1, source_target_pairs={{0,2},{2,4},{4,6},{6,0},{1,3},{3,5},{5,7},{7,1},{8,10},{10,12},{12... | collective-permute-start | bytes 589832 | tf_op jit(solution)/shard_map/ppermute | solution.py:285
  126.2 18.7 %collective-permute-start.35 = (f32[192,256]{1,0:T(8,128)S(1)}, f32[192,256]{1,0:T(8,128)S(1)}, u32[]{:S(2)}, u32[]{:S(2)}) collective-permute-start(f32[192,256]{1,0:T(8,128)S(1)} %add.26), channel_id=1, source_target_pairs={{0,4},{2,6},{4,0},{6,2},{1,5},{3,7},{5,1},{7,3},{8,12},{10,14},{12... | collective-permute-start | bytes 589832 | tf_op jit(solution)/shard_map/ppermute | solution.py:285
  128.7 16.2 %collective-permute-start.36 = (f32[192,256]{1,0:T(8,128)S(1)}, f32[192,256]{1,0:T(8,128)S(1)}, u32[]{:S(2)}, u32[]{:S(2)}) collective-permute-start(f32[192,256]{1,0:T(8,128)S(1)} %add.26), channel_id=1, source_target_pairs={{0,6},{2,0},{4,2},{6,4},{1,7},{3,1},{5,3},{7,5},{8,14},{10,8},{12,... | collective-permute-start | bytes 589832 | tf_op jit(solution)/shard_map/ppermute | solution.py:285
  (19 other events, 80.9 us)
Sparse Core Ops, SparseCore 0:
  11.6 71.8 all-gather.1

commit v5 on v4

--- a/solution.py
+++ b/solution.py
@@ -15,7 +15,7 @@
 COLS = 16384
 OWN = 1024
 SHARE = 48
-BLOCK = 4096
+BLOCK = 8192
 PG_ROWS = 3072
 CHUNK = 2048
 KEPT = 2
@@ -117,9 +117,10 @@
 def prep_kernel(after_ref, c_ref, p_ref, pt_ref, cb_ref, done_ref):
     x = lax.axis_index("x")
     y = lax.axis_index("y")
-    lanes = pl.ds(pl.multiple_of(lax.rem(y, 2) * OWN, OWN), OWN)
-    pt_ref[...] = jnp.transpose(p_ref[x * 2 + lax.div(y, 2), :, lanes].astype(f32)).astype(bf16)
-    own = c_ref[pl.ds(pl.multiple_of((x * 4 + y) * 8, 8), 8), :]
+    block, per = x * 4 + y, CHUNK // OWN
+    lanes = pl.ds(pl.multiple_of(lax.rem(block, per) * OWN, OWN), OWN)
+    pt_ref[...] = jnp.transpose(p_ref[lax.div(block, per), :, lanes].astype(f32)).astype(bf16)
+    own = c_ref[pl.ds(pl.multiple_of(block * 8, 8), 8), :]
     for q in range(8):
         cb_ref[q * 128 : (q + 1) * 128, :] = lanes_to_rows(own[q : q + 1, :], 128)
     done_ref[...] = jnp.zeros_like(done_ref)
@@ -177,12 +178,12 @@
 
 
 def row_kernel(c0, c1, c2, c3, *refs):
-    e_ref, (c_ref, row_ref), acc = refs[0], refs[KEPT : KEPT + 2], refs[-1]
+    e_ref, row_ref, (c_ref, acc) = refs[0], refs[KEPT], refs[-2:]
     row_ref[...] = row_pass((c0, c1, c2, c3), e_ref, c_ref, acc)
 
 
 def row_z_kernel(c0, c1, c2, c3, z_ref, *refs):
-    e_ref, (c_ref, row_ref, z_out), acc = refs[0], refs[KEPT : KEPT + 3], refs[-1]
+    e_ref, (row_ref, z_out), (c_ref, acc) = refs[0], refs[KEPT : KEPT + 2], refs[-2:]
     row_ref[...] = row_pass((c0, c1, c2, c3), e_ref, c_ref, acc)
     z_out[...] = z_ref[...]
 
@@ -271,6 +272,23 @@
         out_ref[...] = jnp.transpose(acc[...])
 
 
+def end_kernel(a_ref, b_ref, c_ref, d_ref, s_ref, out_ref):
+    half = ROWS // 2
+    start = lax.axis_index("c") * half
+    feats = s_ref[pl.ds(pl.multiple_of(start, half), half), :].astype(f32)
+    rnorm = row_norm(feats)
+    stud_f = feats * rnorm
+    dz = (a_ref[...] + c_ref[...]) + (b_ref[...] + d_ref[...])
+    out_ref[...] = (dz - stud_f * jnp.sum(stud_f * dz, axis=1, keepdims=True)) * rnorm
+
+
+def place_kernel(own_ref, sibling_ref, out_ref):
+    half = ROWS // 2
+    core = lax.axis_index("c")
+    out_ref[pl.ds(pl.multiple_of(core * half, half), half), :] = own_ref[...]
+    out_ref[pl.ds(pl.multiple_of((1 - core) * half, half), half), :] = sibling_ref[...]
+
+
 def in_vmem(x):
     return pltpu.with_memory_space_constraint(x, pltpu.VMEM)
 
@@ -310,7 +328,6 @@
 
 
 def shards(teacher_feats, student_feats, proto_weight):
-    core = lax.axis_index("c")
     sds = jax.ShapeDtypeStruct
     vmem = pltpu.VMEM
     kept = vmem((ROWS, COLS), f32)
@@ -364,26 +381,25 @@
         if step == 2:
             break
         if step == 0:
-            unused, rowp, *keep = pl.pallas_call(
+            rowp, *keep = pl.pallas_call(
                 row_kernel,
-                out_shape=[vmem((GROUPS, 128), f32), vmem((1, ROWS), f32)] + shapes,
+                out_shape=[vmem((1, ROWS), f32)] + shapes,
                 in_specs=[whole()] * (4 + KEPT),
-                out_specs=[whole()] * (2 + KEPT),
-                input_output_aliases={4 + k: 2 + k for k in range(KEPT)},
-                scratch_shapes=[vmem((ROWS, 128), f32)],
+                out_specs=[whole()] * (1 + KEPT),
+                input_output_aliases={4 + k: 1 + k for k in range(KEPT)},
+                scratch_shapes=[vmem((GROUPS, 128), f32), vmem((ROWS, 128), f32)],
                 compiler_params=params(5),
                 name="row",
             )(*parts, *map(in_vmem, keep))
         else:
             z0 = z_call(0, colp, feats, keep[1])
-            unused, rowp, z0, *keep = pl.pallas_call(
+            rowp, z0, *keep = pl.pallas_call(
                 row_z_kernel,
-                out_shape=[vmem((GROUPS, 128), f32), vmem((1, ROWS), f32), vmem((1, ROWS), f32)]
-                + shapes,
+                out_shape=[vmem((1, ROWS), f32)] * 2 + shapes,
                 in_specs=[whole()] * (5 + KEPT),
-                out_specs=[whole()] * (3 + KEPT),
-                input_output_aliases={5 + k: 3 + k for k in range(KEPT)},
-                scratch_shapes=[vmem((ROWS, 128), f32)],
+                out_specs=[whole()] * (2 + KEPT),
+                input_output_aliases={5 + k: 2 + k for k in range(KEPT)},
+                scratch_shapes=[vmem((GROUPS, 128), f32), vmem((ROWS, 128), f32)],
                 compiler_params=params(5),
                 name="row",
             )(*parts, in_vmem(z0), *map(in_vmem, keep))
@@ -472,17 +488,22 @@
     parts, proto_grad, student_feats = lax.optimization_barrier(
         (parts, proto_grad, student_feats)
     )
-    dz = (parts[0] + parts[2]) + (parts[1] + parts[3])
-    feats = lax.dynamic_slice(student_feats, (core * half, 0), (half, D)).astype(f32)
-    rnorm = row_norm(feats)
-    stud_f = feats * rnorm
-    grad = (dz - stud_f * jnp.sum(stud_f * dz, axis=1, keepdims=True)) * rnorm
-    sibling = lax.ppermute(grad, "c", [(0, 1), (1, 0)])
-    feat_grad = jnp.where(
-        core == 0,
-        jnp.concatenate([grad, sibling], axis=0),
-        jnp.concatenate([sibling, grad], axis=0),
-    )
+    grad = pl.pallas_call(
+        end_kernel,
+        out_shape=vmem((half, D), f32),
+        in_specs=[whole()] * 5,
+        out_specs=whole(),
+        compiler_params=params(5),
+        name="feat_end",
+    )(*parts, student_feats)
+    feat_grad = pl.pallas_call(
+        place_kernel,
+        out_shape=sds((ROWS, D), f32),
+        in_specs=[whole()] * 2,
+        out_specs=whole(),
+        compiler_params=params(5),
+        name="feat_place",
+    )(grad, lax.ppermute(grad, "c", [(0, 1), (1, 0)]))
     return (feat_grad, proto_grad)
 
 

time: 156 us -> 154 us (0.987)
    pallas_call x2 -> x4, Pallas kernels: 5.84 us -> 5.86 us  [the longest x1 2.44 us: shards(): pl.pallas_call(row_kernel, out_shape=[vmem((1, ROWS), f32)] + shapes, in_...]
  transfers between devices with their start and end apart: 42 -> 42, of which waited for: 24 -> 25; matrix products, arithmetic and copies ran while one was open for 0% -> 0% of each run, Pallas kernels for 33% -> 33%
where the time goes in v5:
time: 154 us
  starting transfers between devices  64.1 us (42%)
  Pallas kernels  53 us (34%)
  waiting for transfers between devices  22.5 us (15%)
  between operations  14.2 us (9%)
    ppermute x36, starting transfers between devices, around(): parts.append(lax.ppermute(x, axis, [(i, (i + d) % 4) for i in range(4)]))  46.3 us
    ppermute x36, waiting for transfers between devices, around(): parts.append(lax.ppermute(x, axis, [(i, (i + d) % 4) for i in range(4)]))  19 us
    pallas_call x1, Pallas kernels, shards(): pl.pallas_call(pg_kernel, grid=(NB * ROWS // PG_ROWS,), out_shape=sds((D,...  16.1 us
    ppermute x3, starting transfers between devices, row_terms(): lax.ppermute(rowp, 'c', [(0, 1), (1, 0)])  13.8 us
    pallas_call x1, Pallas kernels, shards(): pl.pallas_call(first_kernel, out_shape=(packed, kept, vmem((GROUPS, 128),...  9.24 us
    pallas_call x1, Pallas kernels, shards(): pl.pallas_call(dz_kernel, out_shape=(vmem((half, D), f32), vmem((half, D)...  8.46 us
    pallas_call x2, Pallas kernels, z_call(): pl.pallas_call(functools.partial(z_kernel, half), out_shape=pltpu.VMEM((1...  4.34 us
    pallas_call x2, Pallas kernels, shards(): pl.pallas_call(col_kernel, out_shape=[vmem((GROUPS, 128), f32)] + shapes,...  4.29 us
  transfers between devices with their start and end apart: 42, of which 25 were waited for; matrix products, arithmetic and copies ran while one was open for 0% of the time, Pallas kernels for 33%

profile of v5, /device:TPU:1, one launch (start us, length us, event | category | flops | bytes accessed | tf_op | source)
XLA Modules:
  0.0 153.9 jit_solution(7609073020862256647)
XLA Ops:
  9.1 9.2 %first.1 = (bf16[8,256,2048]{2,1,0:T(8,128)(2,1)S(1)}, f32[384,16384]{1,0:T(8,128)S(1)}, f32[128,128]{1,0:T(8,128)S(1)}) custom-call(bf16[256,16384]{1,0:T(8,128)(2,1)} %w_ref.1, bf16[768,256]{1,0:T(8,128)(2,1)S(1)} %get-tuple-element.39.f_ref), custom_call_target="tpu_custom_call" | custom-call | tf_op jit(solution)/shard_map/first/pallas_call | solution.py:347
  18.3 2.2 %collective-permute-start = (f32[128,128]{1,0:T(8,128)S(1)}, f32[128,128]{1,0:T(8,128)S(1)}, u32[]{:S(2)}, u32[]{:S(2)}) collective-permute-start(f32[128,128]{1,0:T(8,128)S(1)} %get-tuple-element.40.a_ref), channel_id=1, source_target_pairs={{0,8},{8,16},{16,24},{24,0},{1,9},{9,17},{17,25},{25,1},{2,10},{10... | collective-permute-start | bytes 196616 | tf_op jit(solution)/shard_map/ppermute | solution.py:303
  20.5 2.6 %collective-permute-start.1 = (f32[128,128]{1,0:T(8,128)S(1)}, f32[128,128]{1,0:T(8,128)S(1)}, u32[]{:S(2)}, u32[]{:S(2)}) collective-permute-start(f32[128,128]{1,0:T(8,128)S(1)} %get-tuple-element.40.a_ref), channel_id=1, source_target_pairs={{0,16},{8,24},{16,0},{24,8},{1,17},{9,25},{17,1},{25,9},{2,18},{10... | collective-permute-start | bytes 196616 | tf_op jit(solution)/shard_map/ppermute | solution.py:303
  27.9 2.4 %collective-permute-start.4 = (f32[128,128]{1,0:T(8,128)S(1)}, f32[128,128]{1,0:T(8,128)S(1)}, u32[]{:S(2)}, u32[]{:S(2)}) collective-permute-start(f32[128,128]{1,0:T(8,128)S(1)} %sum.2.c0), channel_id=1, source_target_pairs={{0,64},{32,96},{64,0},{96,32},{1,65},{33,97},{65,1},{97,33},{2,66}... | collective-permute-start | bytes 196616 | tf_op jit(solution)/shard_map/ppermute | solution.py:303
  33.9 2.4 %row.2 = (f32[1,384]{1,0:T(1,128)S(1)}, f32[384,16384]{1,0:T(8,128)S(1)}, bf16[8,256,2048]{2,1,0:T(8,128)(2,1)S(1)}) custom-call(f32[128,128]{1,0:T(8,128)S(1)} %sum.2.c0, f32[128,128]{1,0:T(8,128)S(1)} %collective-permute-done.3.c1, f32[128,128]{1,0:T(8,128)S(1)} %collective-permute-done.4.c2, ...), custom_call_target="tpu_custom_call", output_to_operand_aliasing={{1}: (4, {}), {2}: (5, {})} | custom-call | tf_op jit(solution)/shard_map/row/pallas_call | solution.py:384
  36.3 3.4 %collective-permute-start.6 = (f32[1,384]{1,0:T(1,128)S(1)}, f32[1,384]{1,0:T(1,128)S(1)}, u32[]{:S(2)}, u32[]{:S(2)}) collective-permute-start(f32[1,384]{1,0:T(1,128)S(1)} %get-tuple-element.43.a_ref), channel_id=1, source_target_pairs={{0,1},{1,0},{2,3},{3,2},{4,5},{5,4},{6,7},{7,6},{8,9},{9,8},{10,11... | collective-permute-start | bytes 4616 | tf_op jit(solution)/shard_map/ppermute | solution.py:315
  42.4 3.2 %collective-permute-start.8 = (f32[1,384]{1,0:T(1,128)S(1)}, f32[1,384]{1,0:T(1,128)S(1)}, u32[]{:S(2)}, u32[]{:S(2)}) collective-permute-start(f32[1,384]{1,0:T(1,128)S(1)} %pair.3.r0), channel_id=1, source_target_pairs={{0,4},{2,6},{4,0},{6,2},{1,5},{3,7},{5,1},{7,3},{8,12},{10,14},{12... | collective-permute-start | bytes 4616 | tf_op jit(solution)/shard_map/ppermute | solution.py:303
  48.4 2.1 %col.2 = (f32[128,128]{1,0:T(8,128)S(1)}, f32[384,16384]{1,0:T(8,128)S(1)}, bf16[8,256,2048]{2,1,0:T(8,128)(2,1)S(1)}) custom-call(f32[1,384]{1,0:T(1,128)S(1)} %pair.3.r0, f32[1,384]{1,0:T(1,128)S(1)} %collective-permute-done.7.r1, f32[1,384]{1,0:T(1,128)S(1)} %collective-permute-done.8.r2, ...), custom_call_target="tpu_custom_call", output_to_operand_aliasing={{1}: (4, {}), {2}: (5, {})} | custom-call | tf_op jit(solution)/shard_map/col/pallas_call | solution.py:407
  50.7 3.4 %collective-permute-start.11 = (f32[128,128]{1,0:T(8,128)S(1)}, f32[128,128]{1,0:T(8,128)S(1)}, u32[]{:S(2)}, u32[]{:S(2)}) collective-permute-start(f32[128,128]{1,0:T(8,128)S(1)} %get-tuple-element.46.a_ref), channel_id=1, source_target_pairs={{0,16},{8,24},{16,0},{24,8},{1,17},{9,25},{17,1},{25,9},{2,18},{10... | collective-permute-start | bytes 196616 | tf_op jit(solution)/shard_map/ppermute | solution.py:303
  58.4 2.6 %collective-permute-start.14 = (f32[128,128]{1,0:T(8,128)S(1)}, f32[128,128]{1,0:T(8,128)S(1)}, u32[]{:S(2)}, u32[]{:S(2)}) collective-permute-start(f32[128,128]{1,0:T(8,128)S(1)} %sum.3.after_ref.c0), channel_id=1, source_target_pairs={{0,64},{32,96},{64,0},{96,32},{1,65},{33,97},{65,1},{97,33},{2,66}... | collective-permute-start | bytes 196616 | tf_op jit(solution)/shard_map/ppermute | solution.py:303
  61.1 2.2 %zden.2.z_ref = f32[1,384]{1,0:T(1,128)S(1)} custom-call(f32[128,128]{1,0:T(8,128)S(1)} %sum.3.after_ref.c0, bf16[768,256]{1,0:T(8,128)(2,1)S(1)} %get-tuple-element.39.f_ref, bf16[8,256,2048]{2,1,0:T(8,128)(2,1)S(1)} %get-tuple-element.47.p_ref.refs_1_), custom_call_target="tpu_custom_call" | custom-call | tf_op jit(solution)/shard_map/zden/pallas_call | solution.py:320
  64.2 2.4 %row.3 = (f32[1,384]{1,0:T(1,128)S(1)}, f32[1,384]{1,0:T(1,128)S(1)}, f32[384,16384]{1,0:T(8,128)S(1)}, bf16[8,256,2048]{2,1,0:T(8,128)(2,1)S(1)}) custom-call(f32[128,128]{1,0:T(8,128)S(1)} %sum.3.after_ref.c0, f32[128,128]{1,0:T(8,128)S(1)} %collective-permute-done.13.c1, ...), custom_call_target="tpu_custom_call", output_to_operand_aliasing={{2}: (5, {}), {3}: (6, {})} | custom-call | tf_op jit(solution)/shard_map/row/pallas_call | solution.py:396
  66.6 5.8 %collective-permute-start.16 = (f32[1,384]{1,0:T(1,128)S(1)}, f32[1,384]{1,0:T(1,128)S(1)}, u32[]{:S(2)}, u32[]{:S(2)}) collective-permute-start(f32[1,384]{1,0:T(1,128)S(1)} %get-tuple-element.49.a_ref), channel_id=1, source_target_pairs={{0,1},{1,0},{2,3},{3,2},{4,5},{5,4},{6,7},{7,6},{8,9},{9,8},{10,11... | collective-permute-start | bytes 4616 | tf_op jit(solution)/shard_map/ppermute | solution.py:315
  73.3 3.3 %collective-permute-start.18 = (f32[1,384]{1,0:T(1,128)S(1)}, f32[1,384]{1,0:T(1,128)S(1)}, u32[]{:S(2)}, u32[]{:S(2)}) collective-permute-start(f32[1,384]{1,0:T(1,128)S(1)} %pair.4.r0), channel_id=1, source_target_pairs={{0,4},{2,6},{4,0},{6,2},{1,5},{3,7},{5,1},{7,3},{8,12},{10,14},{12... | collective-permute-start | bytes 4616 | tf_op jit(solution)/shard_map/ppermute | solution.py:303
  84.3 2.2 %zden.3.z_ref = f32[1,384]{1,0:T(1,128)S(1)} custom-call(f32[128,128]{1,0:T(8,128)S(1)} %get-tuple-element.52.after_ref.a_ref, bf16[768,256]{1,0:T(8,128)(2,1)S(1)} %get-tuple-element.39.f_ref, bf16[8,256,2048]{2,1,0:T(8,128)(2,1)S(1)} %get-tuple-element.53.p_ref.refs_1_), custom_call_target="tpu_custom_call" | custom-call | tf_op jit(solution)/shard_map/zden/pallas_call | solution.py:320
  90.0 2.3 %collective-permute-done.23.c1 = f32[128,128]{1,0:T(8,128)S(1)} collective-permute-done((f32[128,128]{1,0:T(8,128)S(1)}, f32[128,128]{1,0:T(8,128)S(1)}, u32[]{:S(2)}, u32[]{:S(2)}) %collective-permute-start.23) | collective-permute-done | bytes 65568 | tf_op jit(solution)/shard_map/ppermute | solution.py:303
  93.0 2.4 %row_last.1 = (f32[128,128]{1,0:T(8,128)S(1)}, f32[2,384]{1,0:T(2,128)S(1)}, f32[384,16384]{1,0:T(8,128)S(1)}, bf16[8,256,2048]{2,1,0:T(8,128)(2,1)S(1)}) custom-call(f32[128,128]{1,0:T(8,128)S(1)} %get-tuple-element.54.c0, f32[128,128]{1,0:T(8,128)S(1)} %collective-permute-done.23.c1, ...), custom_call_target="tpu_custom_call", output_to_operand_aliasing={{2}: (6, {}), {3}: (7, {})} | custom-call | tf_op jit(solution)/shard_map/row_last/pallas_call | solution.py:418
  95.4 4.6 %collective-permute-start.26 = (f32[2,384]{1,0:T(2,128)S(1)}, f32[2,384]{1,0:T(2,128)S(1)}, u32[]{:S(2)}, u32[]{:S(2)}) collective-permute-start(f32[2,384]{1,0:T(2,128)S(1)} %get-tuple-element.58.a_ref), channel_id=1, source_target_pairs={{0,1},{1,0},{2,3},{3,2},{4,5},{5,4},{6,7},{7,6},{8,9},{9,8},{10,11... | collective-permute-start | bytes 9224 | tf_op jit(solution)/shard_map/ppermute | solution.py:315
  106.8 2.5 %collective-permute-start.31 = (f32[2,384]{1,0:T(2,128)S(1)}, f32[2,384]{1,0:T(2,128)S(1)}, u32[]{:S(2)}, u32[]{:S(2)}) collective-permute-start(f32[2,384]{1,0:T(2,128)S(1)} %rz.1.rz_ref.a_ref), channel_id=1, source_target_pairs={{0,16},{8,24},{16,0},{24,8},{1,17},{9,25},{17,1},{25,9},{2,18},{10... | collective-permute-start | bytes 9224 | tf_op jit(solution)/shard_map/ppermute | solution.py:303
  109.3 8.5 %dz.1 = (f32[192,256]{1,0:T(8,128)S(1)}, f32[192,256]{1,0:T(8,128)S(1)}) custom-call(f32[2,384]{1,0:T(2,128)S(1)} %rz.1.rz_ref.a_ref, f32[128,128]{1,0:T(8,128)S(1)} %get-tuple-element.59.c_ref, bf16[768,256]{1,0:T(8,128)(2,1)S(1)} %get-tuple-element.39.f_ref, f32[384,16384]{1,0:T(8,128)S(1)} %get-tuple-element.62.e_ref, ...), custom_call_target="tpu_custom_call" | custom-call | tf_op jit(solution)/shard_map/dz/pallas_call | solution.py:448
  117.8 2.4 %collective-permute-start.33 = (f32[192,256]{1,0:T(8,128)S(1)}, f32[192,256]{1,0:T(8,128)S(1)}, u32[]{:S(2)}, u32[]{:S(2)}) collective-permute-start(f32[192,256]{1,0:T(8,128)S(1)} %get-tuple-element.65), channel_id=1, source_target_pairs={{0,1},{1,0},{2,3},{3,2},{4,5},{5,4},{6,7},{7,6},{8,9},{9,8},{10,11... | collective-permute-start | bytes 589832 | tf_op jit(solution)/shard_map/ppermute | solution.py:469
  121.1 2.5 %collective-permute-start.38 = (f32[4,2,384]{2,1,0:T(2,128)S(1)}, f32[4,2,384]{2,1,0:T(2,128)S(1)}, u32[]{:S(2)}, u32[]{:S(2)}) collective-permute-start(f32[4,2,384]{2,1,0:T(2,128)S(1)} %get-tuple-element.66.r0), channel_id=1, source_target_pairs={{0,64},{32,96},{64,0},{96,32},{1,65},{33,97},{65,1},{97,33},{2,66}... | collective-permute-start | bytes 36872 | tf_op jit(solution)/shard_map/ppermute | solution.py:303
  124.8 2.5 %collective-permute-start.35 = (f32[192,256]{1,0:T(8,128)S(1)}, f32[192,256]{1,0:T(8,128)S(1)}, u32[]{:S(2)}, u32[]{:S(2)}) collective-permute-start(f32[192,256]{1,0:T(8,128)S(1)} %add.3.a_ref), channel_id=1, source_target_pairs={{0,4},{2,6},{4,0},{6,2},{1,5},{3,7},{5,1},{7,3},{8,12},{10,14},{12... | collective-permute-start | bytes 589832 | tf_op jit(solution)/shard_map/ppermute | solution.py:303
  127.3 16.1 %pg.1 = f32[256,1024]{1,0:T(8,128)} custom-call(f32[4,2,384]{2,1,0:T(2,128)S(1)} %get-tuple-element.66.r0, f32[4,2,384]{2,1,0:T(2,128)S(1)} %collective-permute-done.37.r1, f32[4,2,384]{2,1,0:T(2,128)S(1)} %collective-permute-done.38.r2, f32[4,2,384]{2,1,0:T(2,128)S(1)} %collective-permute-done.39.r3, bf16[1024,256]{1,0:T(8,128)(2,1)S(1)} %get-tuple-element.67.pt, ...), custom_call_target="tpu_custom_call" | custom-call | flops 9699999744 | bytes 8000000 | tf_op jit(solution)/shard_map/pg/pallas_call | solution.py:472
  (86 shorter events, 46.2 us)
Async XLA Ops:
  7.2 120.1 %all-gather.2.cloned.1.call-start = ((), (), s32[]{:S(2)}) async-start(), calls=%async_computation | async-start | bytes 6340608 | tf_op jit(solution)/shard_map/all_gather | solution.py:344
  18.3 5.9 %collective-permute-start = (f32[128,128]{1,0:T(8,128)S(1)}, f32[128,128]{1,0:T(8,128)S(1)}, u32[]{:S(2)}, u32[]{:S(2)}) collective-permute-start(f32[128,128]{1,0:T(8,128)S(1)} %get-tuple-element.40.a_ref), channel_id=1, source_target_pairs={{0,8},{8,16},{16,24},{24,0},{1,9},{9,17},{17,25},{25,1},{2,10},{10... | collective-permute-start | bytes 196616 | tf_op jit(solution)/shard_map/ppermute | solution.py:303
  20.5 5.2 %collective-permute-start.1 = (f32[128,128]{1,0:T(8,128)S(1)}, f32[128,128]{1,0:T(8,128)S(1)}, u32[]{:S(2)}, u32[]{:S(2)}) collective-permute-start(f32[128,128]{1,0:T(8,128)S(1)} %get-tuple-element.40.a_ref), channel_id=1, source_target_pairs={{0,16},{8,24},{16,0},{24,8},{1,17},{9,25},{17,1},{25,9},{2,18},{10... | collective-permute-start | bytes 196616 | tf_op jit(solution)/shard_map/ppermute | solution.py:303
  26.6 4.9 %collective-permute-start.3 = (f32[128,128]{1,0:T(8,128)S(1)}, f32[128,128]{1,0:T(8,128)S(1)}, u32[]{:S(2)}, u32[]{:S(2)}) collective-permute-start(f32[128,128]{1,0:T(8,128)S(1)} %sum.2.c0), channel_id=1, source_target_pairs={{0,32},{32,64},{64,96},{96,0},{1,33},{33,65},{65,97},{97,1},{2,34}... | collective-permute-start | bytes 196616 | tf_op jit(solution)/shard_map/ppermute | solution.py:303
  27.9 4.8 %collective-permute-start.4 = (f32[128,128]{1,0:T(8,128)S(1)}, f32[128,128]{1,0:T(8,128)S(1)}, u32[]{:S(2)}, u32[]{:S(2)}) collective-permute-start(f32[128,128]{1,0:T(8,128)S(1)} %sum.2.c0), channel_id=1, source_target_pairs={{0,64},{32,96},{64,0},{96,32},{1,65},{33,97},{65,1},{97,33},{2,66}... | collective-permute-start | bytes 196616 | tf_op jit(solution)/shard_map/ppermute | solution.py:303
  40.6 5.8 %collective-permute-start.7 = (f32[1,384]{1,0:T(1,128)S(1)}, f32[1,384]{1,0:T(1,128)S(1)}, u32[]{:S(2)}, u32[]{:S(2)}) collective-permute-start(f32[1,384]{1,0:T(1,128)S(1)} %pair.3.r0), channel_id=1, source_target_pairs={{0,2},{2,4},{4,6},{6,0},{1,3},{3,5},{5,7},{7,1},{8,10},{10,12},{12... | collective-permute-start | bytes 4616 | tf_op jit(solution)/shard_map/ppermute | solution.py:303
  50.7 5.7 %collective-permute-start.11 = (f32[128,128]{1,0:T(8,128)S(1)}, f32[128,128]{1,0:T(8,128)S(1)}, u32[]{:S(2)}, u32[]{:S(2)}) collective-permute-start(f32[128,128]{1,0:T(8,128)S(1)} %get-tuple-element.46.a_ref), channel_id=1, source_target_pairs={{0,16},{8,24},{16,0},{24,8},{1,17},{9,25},{17,1},{25,9},{2,18},{10... | collective-permute-start | bytes 196616 | tf_op jit(solution)/shard_map/ppermute | solution.py:303
  57.4 5.8 %collective-permute-start.13 = (f32[128,128]{1,0:T(8,128)S(1)}, f32[128,128]{1,0:T(8,128)S(1)}, u32[]{:S(2)}, u32[]{:S(2)}) collective-permute-start(f32[128,128]{1,0:T(8,128)S(1)} %sum.3.after_ref.c0), channel_id=1, source_target_pairs={{0,32},{32,64},{64,96},{96,0},{1,33},{33,65},{65,97},{97,1},{2,34}... | collective-permute-start | bytes 196616 | tf_op jit(solution)/shard_map/ppermute | solution.py:303
  58.4 5.0 %collective-permute-start.14 = (f32[128,128]{1,0:T(8,128)S(1)}, f32[128,128]{1,0:T(8,128)S(1)}, u32[]{:S(2)}, u32[]{:S(2)}) collective-permute-start(f32[128,128]{1,0:T(8,128)S(1)} %sum.3.after_ref.c0), channel_id=1, source_target_pairs={{0,64},{32,96},{64,0},{96,32},{1,65},{33,97},{65,1},{97,33},{2,66}... | collective-permute-start | bytes 196616 | tf_op jit(solution)/shard_map/ppermute | solution.py:303
  66.6 6.6 %collective-permute-start.16 = (f32[1,384]{1,0:T(1,128)S(1)}, f32[1,384]{1,0:T(1,128)S(1)}, u32[]{:S(2)}, u32[]{:S(2)}) collective-permute-start(f32[1,384]{1,0:T(1,128)S(1)} %get-tuple-element.49.a_ref), channel_id=1, source_target_pairs={{0,1},{1,0},{2,3},{3,2},{4,5},{5,4},{6,7},{7,6},{8,9},{9,8},{10,11... | collective-permute-start | bytes 4616 | tf_op jit(solution)/shard_map/ppermute | solution.py:315
  81.6 5.0 %collective-permute-start.20 = (f32[128,128]{1,0:T(8,128)S(1)}, f32[128,128]{1,0:T(8,128)S(1)}, u32[]{:S(2)}, u32[]{:S(2)}) collective-permute-start(f32[128,128]{1,0:T(8,128)S(1)} %get-tuple-element.52.after_ref.a_ref), channel_id=1, source_target_pairs={{0,8},{8,16},{16,24},{24,0},{1,9},{9,17},{17,25},{25,1},{2,10},{10... | collective-permute-start | bytes 196616 | tf_op jit(solution)/shard_map/ppermute | solution.py:303
  81.7 5.1 %collective-permute-start.21 = (f32[128,128]{1,0:T(8,128)S(1)}, f32[128,128]{1,0:T(8,128)S(1)}, u32[]{:S(2)}, u32[]{:S(2)}) collective-permute-start(f32[128,128]{1,0:T(8,128)S(1)} %get-tuple-element.52.after_ref.a_ref), channel_id=1, source_target_pairs={{0,16},{8,24},{16,0},{24,8},{1,17},{9,25},{17,1},{25,9},{2,18},{10... | collective-permute-start | bytes 196616 | tf_op jit(solution)/shard_map/ppermute | solution.py:303
  87.3 5.1 %collective-permute-start.23 = (f32[128,128]{1,0:T(8,128)S(1)}, f32[128,128]{1,0:T(8,128)S(1)}, u32[]{:S(2)}, u32[]{:S(2)}) collective-permute-start(f32[128,128]{1,0:T(8,128)S(1)} %get-tuple-element.54.c0), channel_id=1, source_target_pairs={{0,32},{32,64},{64,96},{96,0},{1,33},{33,65},{65,97},{97,1},{2,34}... | collective-permute-start | bytes 196616 | tf_op jit(solution)/shard_map/ppermute | solution.py:303
  87.4 5.0 %collective-permute-start.24 = (f32[128,128]{1,0:T(8,128)S(1)}, f32[128,128]{1,0:T(8,128)S(1)}, u32[]{:S(2)}, u32[]{:S(2)}) collective-permute-start(f32[128,128]{1,0:T(8,128)S(1)} %get-tuple-element.54.c0), channel_id=1, source_target_pairs={{0,64},{32,96},{64,0},{96,32},{1,65},{33,97},{65,1},{97,33},{2,66}... | collective-permute-start | bytes 196616 | tf_op jit(solution)/shard_map/ppermute | solution.py:303
  95.4 5.4 %collective-permute-start.26 = (f32[2,384]{1,0:T(2,128)S(1)}, f32[2,384]{1,0:T(2,128)S(1)}, u32[]{:S(2)}, u32[]{:S(2)}) collective-permute-start(f32[2,384]{1,0:T(2,128)S(1)} %get-tuple-element.58.a_ref), channel_id=1, source_target_pairs={{0,1},{1,0},{2,3},{3,2},{4,5},{5,4},{6,7},{7,6},{8,9},{9,8},{10,11... | collective-permute-start | bytes 9224 | tf_op jit(solution)/shard_map/ppermute | solution.py:315
  105.7 12.1 %collective-permute-start.30 = (f32[2,384]{1,0:T(2,128)S(1)}, f32[2,384]{1,0:T(2,128)S(1)}, u32[]{:S(2)}, u32[]{:S(2)}) collective-permute-start(f32[2,384]{1,0:T(2,128)S(1)} %rz.1.rz_ref.a_ref), channel_id=1, source_target_pairs={{0,8},{8,16},{16,24},{24,0},{1,9},{9,17},{17,25},{25,1},{2,10},{10... | collective-permute-start | bytes 9224 | tf_op jit(solution)/shard_map/ppermute | solution.py:303
  106.8 11.0 %collective-permute-start.31 = (f32[2,384]{1,0:T(2,128)S(1)}, f32[2,384]{1,0:T(2,128)S(1)}, u32[]{:S(2)}, u32[]{:S(2)}) collective-permute-start(f32[2,384]{1,0:T(2,128)S(1)} %rz.1.rz_ref.a_ref), channel_id=1, source_target_pairs={{0,16},{8,24},{16,0},{24,8},{1,17},{9,25},{17,1},{25,9},{2,18},{10... | collective-permute-start | bytes 9224 | tf_op jit(solution)/shard_map/ppermute | solution.py:303
  109.3 8.5 %collective-permute-start.32 = (f32[2,384]{1,0:T(2,128)S(1)}, f32[2,384]{1,0:T(2,128)S(1)}, u32[]{:S(2)}, u32[]{:S(2)}) collective-permute-start(f32[2,384]{1,0:T(2,128)S(1)} %rz.1.rz_ref.a_ref), channel_id=1, source_target_pairs={{0,24},{8,0},{16,8},{24,16},{1,25},{9,1},{17,9},{25,17},{2,26},{10... | collective-permute-start | bytes 9224 | tf_op jit(solution)/shard_map/ppermute | solution.py:303
  117.8 5.8 %collective-permute-start.33 = (f32[192,256]{1,0:T(8,128)S(1)}, f32[192,256]{1,0:T(8,128)S(1)}, u32[]{:S(2)}, u32[]{:S(2)}) collective-permute-start(f32[192,256]{1,0:T(8,128)S(1)} %get-tuple-element.65), channel_id=1, source_target_pairs={{0,1},{1,0},{2,3},{3,2},{4,5},{5,4},{6,7},{7,6},{8,9},{9,8},{10,11... | collective-permute-start | bytes 589832 | tf_op jit(solution)/shard_map/ppermute | solution.py:469
  120.2 7.0 %collective-permute-start.37 = (f32[4,2,384]{2,1,0:T(2,128)S(1)}, f32[4,2,384]{2,1,0:T(2,128)S(1)}, u32[]{:S(2)}, u32[]{:S(2)}) collective-permute-start(f32[4,2,384]{2,1,0:T(2,128)S(1)} %get-tuple-element.66.r0), channel_id=1, source_target_pairs={{0,32},{32,64},{64,96},{96,0},{1,33},{33,65},{65,97},{97,1},{2,34}... | collective-permute-start | bytes 36872 | tf_op jit(solution)/shard_map/ppermute | solution.py:303
  121.1 6.1 %collective-permute-start.38 = (f32[4,2,384]{2,1,0:T(2,128)S(1)}, f32[4,2,384]{2,1,0:T(2,128)S(1)}, u32[]{:S(2)}, u32[]{:S(2)}) collective-permute-start(f32[4,2,384]{2,1,0:T(2,128)S(1)} %get-tuple-element.66.r0), channel_id=1, source_target_pairs={{0,64},{32,96},{64,0},{96,32},{1,65},{33,97},{65,1},{97,33},{2,66}... | collective-permute-start | bytes 36872 | tf_op jit(solution)/shard_map/ppermute | solution.py:303
  123.7 19.7 %collective-permute-start.34 = (f32[192,256]{1,0:T(8,128)S(1)}, f32[192,256]{1,0:T(8,128)S(1)}, u32[]{:S(2)}, u32[]{:S(2)}) collective-permute-start(f32[192,256]{1,0:T(8,128)S(1)} %add.3.a_ref), channel_id=1, source_target_pairs={{0,2},{2,4},{4,6},{6,0},{1,3},{3,5},{5,7},{7,1},{8,10},{10,12},{12... | collective-permute-start | bytes 589832 | tf_op jit(solution)/shard_map/ppermute | solution.py:303
  124.8 18.7 %collective-permute-start.35 = (f32[192,256]{1,0:T(8,128)S(1)}, f32[192,256]{1,0:T(8,128)S(1)}, u32[]{:S(2)}, u32[]{:S(2)}) collective-permute-start(f32[192,256]{1,0:T(8,128)S(1)} %add.3.a_ref), channel_id=1, source_target_pairs={{0,4},{2,6},{4,0},{6,2},{1,5},{3,7},{5,1},{7,3},{8,12},{10,14},{12... | collective-permute-start | bytes 589832 | tf_op jit(solution)/shard_map/ppermute | solution.py:303
  127.3 16.2 %collective-permute-start.36 = (f32[192,256]{1,0:T(8,128)S(1)}, f32[192,256]{1,0:T(8,128)S(1)}, u32[]{:S(2)}, u32[]{:S(2)}) collective-permute-start(f32[192,256]{1,0:T(8,128)S(1)} %add.3.a_ref), channel_id=1, source_target_pairs={{0,6},{2,0},{4,2},{6,4},{1,7},{3,1},{5,3},{7,5},{8,14},{10,8},{12,... | collective-permute-start | bytes 589832 | tf_op jit(solution)/shard_map/ppermute | solution.py:303
  (19 other events, 81.1 us)
Sparse Core Ops, SparseCore 0:
  11.6 71.9 all-gather.1

commit v6 on v5

--- a/solution.py
+++ b/solution.py
@@ -238,22 +238,22 @@
     other_ref[...] = dz_ref[pl.ds(pl.multiple_of((1 - core) * half, half), half), :]
 
 
-def pg_kernel(r0, r1, r2, r3, pt, cb, f_ref, out_ref, acc, g, rz):
-    step = pl.program_id(0)
-
-    @pl.when(step == 0)
-    def _():
-        acc[...] = jnp.zeros_like(acc)
-        x = lax.axis_index("x")
-        y = lax.axis_index("y")
-        for dx, ref in enumerate((r0, r1, r2, r3)):
-            for dy in range(4):
-                rz[lax.rem(x - dx + 4, 4) * 4 + lax.rem(y - dy + 4, 4)] = ref[dy]
+def joined_kernel(a_ref, b_ref, acc_ref, out_ref, kept_ref):
+    out_ref[...] = a_ref[...] + b_ref[...]
+
+
+def pg_kernel(part, r0, r1, r2, r3, pt, cb, f_ref, *refs):
+    out_ref, g, rz = refs[-3:]
+    x = lax.axis_index("x")
+    y = lax.axis_index("y")
+    for dx, ref in enumerate((r0, r1, r2, r3)):
+        for dy in range(4):
+            rz[lax.rem(x - dx + 4, 4) * 4 + lax.rem(y - dy + 4, 4)] = ref[dy]
 
     t = f_ref[:, :D]
     s = f_ref[:, D:]
     blocks = range(PG_ROWS // ROWS)
-    rzs = [rz[step * len(blocks) + b] for b in blocks]
+    rzs = [rz[part * len(blocks) + b] for b in blocks]
     r = jnp.concatenate([v[0:1, :] for v in rzs], axis=1)
     z = jnp.concatenate([v[1:2, :] for v in rzs], axis=1)
     nt = (((1,), (1,)), ((), ()))
@@ -265,20 +265,20 @@
             lane = slice(h * 128, (h + 1) * 128)
             to = slice(n * 256 + h * 128, n * 256 + (h + 1) * 128)
             g[:, to] = (es[:, lane] * z[:, to] - et[:, lane] * r[:, to] * cb[...]).astype(bf16)
-    acc[...] += jnp.dot(g[...], s, preferred_element_type=f32)
-
-    @pl.when(step == pl.num_programs(0) - 1)
-    def _():
-        out_ref[...] = jnp.transpose(acc[...])
-
-
-def end_kernel(a_ref, b_ref, c_ref, d_ref, s_ref, out_ref):
+    term = jnp.dot(g[...], s, preferred_element_type=f32)
+    if part == 0:
+        out_ref[...] = term
+    else:
+        out_ref[...] = jnp.transpose(refs[0][...] + term)
+
+
+def end_kernel(a_ref, b_ref, s_ref, out_ref):
     half = ROWS // 2
     start = lax.axis_index("c") * half
     feats = s_ref[pl.ds(pl.multiple_of(start, half), half), :].astype(f32)
     rnorm = row_norm(feats)
     stud_f = feats * rnorm
-    dz = (a_ref[...] + c_ref[...]) + (b_ref[...] + d_ref[...])
+    dz = a_ref[...] + b_ref[...]
     out_ref[...] = (dz - stud_f * jnp.sum(stud_f * dz, axis=1, keepdims=True)) * rnorm
 
 
@@ -467,23 +467,38 @@
     rz_all = around(rz_rows, "x")
 
     got = lax.ppermute(other, "c", [(0, 1), (1, 0)])
-    parts = around(mine + got, "z")
-
-    proto_grad = pl.pallas_call(
-        pg_kernel,
-        grid=(NB * ROWS // PG_ROWS,),
-        out_shape=sds((D, OWN), f32),
-        in_specs=[whole()] * 6 + [pl.BlockSpec((PG_ROWS, 2 * D), lambda i: (i, 0))],
-        out_specs=pl.BlockSpec((D, OWN), lambda i: (0, 0)),
-        scratch_shapes=[
-            vmem((OWN, D), f32),
-            vmem((OWN, PG_ROWS), bf16),
-            vmem((NB, 2, ROWS), f32),
-        ],
-        compiler_params=params(30),
-        cost_estimate=pl.CostEstimate(flops=9700000000, bytes_accessed=8000000, transcendentals=12600000),
-        name="pg",
-    )(*rz_all, in_vmem(pt), in_vmem(cb), in_hbm(feats_all))
+    dz = mine + got
+    beside = lax.ppermute(dz, "z", [(i, i ^ 1) for i in range(4)])
+
+    def pg(part, out, *acc):
+        return pl.pallas_call(
+            functools.partial(pg_kernel, part),
+            grid=(1,),
+            out_shape=out,
+            in_specs=[whole()] * 6
+            + [pl.BlockSpec((PG_ROWS, 2 * D), lambda i: (part, 0))]
+            + [whole()] * len(acc),
+            out_specs=whole(),
+            scratch_shapes=[vmem((OWN, PG_ROWS), bf16), vmem((NB, 2, ROWS), f32)],
+            compiler_params=params(26),
+            cost_estimate=pl.CostEstimate(
+                flops=4850000000, bytes_accessed=4000000, transcendentals=6300000
+            ),
+            name="pg",
+        )(*rz_all, in_vmem(pt), in_vmem(cb), in_hbm(feats_all), *acc)
+
+    acc = pg(0, vmem((OWN, D), f32))
+    dz, acc = pl.pallas_call(
+        joined_kernel,
+        out_shape=(vmem((half, D), f32), vmem((OWN, D), f32)),
+        in_specs=[whole()] * 3,
+        out_specs=(whole(), whole()),
+        input_output_aliases={2: 1},
+        compiler_params=params(26),
+        name="joined",
+    )(dz, beside, in_vmem(acc))
+    parts = (dz, lax.ppermute(dz, "z", [(i, i ^ 3) for i in range(4)]))
+    proto_grad = pg(1, sds((D, OWN), f32), in_vmem(acc))
 
     parts, proto_grad, student_feats = lax.optimization_barrier(
         (parts, proto_grad, student_feats)
@@ -491,7 +506,7 @@
     grad = pl.pallas_call(
         end_kernel,
         out_shape=vmem((half, D), f32),
-        in_specs=[whole()] * 5,
+        in_specs=[whole()] * 3,
         out_specs=whole(),
         compiler_params=params(5),
         name="feat_end",

time: 154 us -> 158 us (1.026)
  Pallas kernels: 53 us -> 55.1 us
    ppermute x0 -> x2, starting transfers between devices: none -> 4.02 us  [the longest x1 2.74 us: shards(): parts = (dz, lax.ppermute(dz, 'z', [(i, i ^ 3) for i in range(4)]))]
    ppermute x36 -> x33, starting transfers between devices: 46.3 us -> 42.8 us  [around(): parts.append(lax.ppermute(x, axis, [(i, (i + d) % 4) for i in range(4)]))]
    pallas_call x1 -> x3, Pallas kernels: 16.1 us -> 18.2 us  [the longest x2 18.2 us: pg(): pl.pallas_call(functools.partial(pg_kernel, part), grid=(1,), out_shape=o...]
    ppermute x36 -> x33, waiting for transfers between devices: 19 us -> 20.3 us  [around(): parts.append(lax.ppermute(x, axis, [(i, (i + d) % 4) for i in range(4)]))]
  transfers between devices with their start and end apart: 42 -> 41, of which waited for: 25 -> 27; matrix products, arithmetic and copies ran while one was open for 0% -> 0% of each run, Pallas kernels for 33% -> 33%
where the time goes in v6:
time: 158 us
  starting transfers between devices  65 us (41%)
  Pallas kernels  55.1 us (35%)
  waiting for transfers between devices  23.8 us (15%)
  between operations  14.2 us (9%)
    ppermute x33, starting transfers between devices, around(): parts.append(lax.ppermute(x, axis, [(i, (i + d) % 4) for i in range(4)]))  42.8 us
    ppermute x33, waiting for transfers between devices, around(): parts.append(lax.ppermute(x, axis, [(i, (i + d) % 4) for i in range(4)]))  20.3 us
    pallas_call x2, Pallas kernels, pg(): pl.pallas_call(functools.partial(pg_kernel, part), grid=(1,), out_shape=o...  18.2 us
    ppermute x3, starting transfers between devices, row_terms(): lax.ppermute(rowp, 'c', [(0, 1), (1, 0)])  13.8 us
    pallas_call x1, Pallas kernels, shards(): pl.pallas_call(first_kernel, out_shape=(packed, kept, vmem((GROUPS, 128),...  9.24 us
    pallas_call x1, Pallas kernels, shards(): pl.pallas_call(dz_kernel, out_shape=(vmem((half, D), f32), vmem((half, D)...  8.46 us
    pallas_call x2, Pallas kernels, z_call(): pl.pallas_call(functools.partial(z_kernel, half), out_shape=pltpu.VMEM((1...  4.34 us
    pallas_call x2, Pallas kernels, shards(): pl.pallas_call(col_kernel, out_shape=[vmem((GROUPS, 128), f32)] + shapes,...  4.29 us
  transfers between devices with their start and end apart: 41, of which 27 were waited for; matrix products, arithmetic and copies ran while one was open for 0% of the time, Pallas kernels for 33%

profile of v6, /device:TPU:1, one launch (start us, length us, event | category | flops | bytes accessed | tf_op | source)
XLA Modules:
  0.0 158.1 jit_solution(12045243882373806932)
XLA Ops:
  9.1 9.2 %first.1 = (bf16[8,256,2048]{2,1,0:T(8,128)(2,1)S(1)}, f32[384,16384]{1,0:T(8,128)S(1)}, f32[128,128]{1,0:T(8,128)S(1)}) custom-call(bf16[256,16384]{1,0:T(8,128)(2,1)} %w_ref.1, bf16[768,256]{1,0:T(8,128)(2,1)S(1)} %get-tuple-element.39.f_ref), custom_call_target="tpu_custom_call" | custom-call | tf_op jit(solution)/shard_map/first/pallas_call | solution.py:347
  18.3 2.2 %collective-permute-start = (f32[128,128]{1,0:T(8,128)S(1)}, f32[128,128]{1,0:T(8,128)S(1)}, u32[]{:S(2)}, u32[]{:S(2)}) collective-permute-start(f32[128,128]{1,0:T(8,128)S(1)} %get-tuple-element.40.a_ref), channel_id=1, source_target_pairs={{0,8},{8,16},{16,24},{24,0},{1,9},{9,17},{17,25},{25,1},{2,10},{10... | collective-permute-start | bytes 196616 | tf_op jit(solution)/shard_map/ppermute | solution.py:303
  20.5 2.6 %collective-permute-start.1 = (f32[128,128]{1,0:T(8,128)S(1)}, f32[128,128]{1,0:T(8,128)S(1)}, u32[]{:S(2)}, u32[]{:S(2)}) collective-permute-start(f32[128,128]{1,0:T(8,128)S(1)} %get-tuple-element.40.a_ref), channel_id=1, source_target_pairs={{0,16},{8,24},{16,0},{24,8},{1,17},{9,25},{17,1},{25,9},{2,18},{10... | collective-permute-start | bytes 196616 | tf_op jit(solution)/shard_map/ppermute | solution.py:303
  27.9 2.4 %collective-permute-start.4 = (f32[128,128]{1,0:T(8,128)S(1)}, f32[128,128]{1,0:T(8,128)S(1)}, u32[]{:S(2)}, u32[]{:S(2)}) collective-permute-start(f32[128,128]{1,0:T(8,128)S(1)} %sum.2.c0), channel_id=1, source_target_pairs={{0,64},{32,96},{64,0},{96,32},{1,65},{33,97},{65,1},{97,33},{2,66}... | collective-permute-start | bytes 196616 | tf_op jit(solution)/shard_map/ppermute | solution.py:303
  33.9 2.4 %row.2 = (f32[1,384]{1,0:T(1,128)S(1)}, f32[384,16384]{1,0:T(8,128)S(1)}, bf16[8,256,2048]{2,1,0:T(8,128)(2,1)S(1)}) custom-call(f32[128,128]{1,0:T(8,128)S(1)} %sum.2.c0, f32[128,128]{1,0:T(8,128)S(1)} %collective-permute-done.3.c1, f32[128,128]{1,0:T(8,128)S(1)} %collective-permute-done.4.c2, ...), custom_call_target="tpu_custom_call", output_to_operand_aliasing={{1}: (4, {}), {2}: (5, {})} | custom-call | tf_op jit(solution)/shard_map/row/pallas_call | solution.py:384
  36.3 3.4 %collective-permute-start.6 = (f32[1,384]{1,0:T(1,128)S(1)}, f32[1,384]{1,0:T(1,128)S(1)}, u32[]{:S(2)}, u32[]{:S(2)}) collective-permute-start(f32[1,384]{1,0:T(1,128)S(1)} %get-tuple-element.43.a_ref), channel_id=1, source_target_pairs={{0,1},{1,0},{2,3},{3,2},{4,5},{5,4},{6,7},{7,6},{8,9},{9,8},{10,11... | collective-permute-start | bytes 4616 | tf_op jit(solution)/shard_map/ppermute | solution.py:315
  42.4 3.2 %collective-permute-start.8 = (f32[1,384]{1,0:T(1,128)S(1)}, f32[1,384]{1,0:T(1,128)S(1)}, u32[]{:S(2)}, u32[]{:S(2)}) collective-permute-start(f32[1,384]{1,0:T(1,128)S(1)} %pair.3.r0), channel_id=1, source_target_pairs={{0,4},{2,6},{4,0},{6,2},{1,5},{3,7},{5,1},{7,3},{8,12},{10,14},{12... | collective-permute-start | bytes 4616 | tf_op jit(solution)/shard_map/ppermute | solution.py:303
  50.7 3.4 %collective-permute-start.11 = (f32[128,128]{1,0:T(8,128)S(1)}, f32[128,128]{1,0:T(8,128)S(1)}, u32[]{:S(2)}, u32[]{:S(2)}) collective-permute-start(f32[128,128]{1,0:T(8,128)S(1)} %get-tuple-element.46.a_ref), channel_id=1, source_target_pairs={{0,16},{8,24},{16,0},{24,8},{1,17},{9,25},{17,1},{25,9},{2,18},{10... | collective-permute-start | bytes 196616 | tf_op jit(solution)/shard_map/ppermute | solution.py:303
  58.4 2.6 %collective-permute-start.14 = (f32[128,128]{1,0:T(8,128)S(1)}, f32[128,128]{1,0:T(8,128)S(1)}, u32[]{:S(2)}, u32[]{:S(2)}) collective-permute-start(f32[128,128]{1,0:T(8,128)S(1)} %sum.3.after_ref.c0), channel_id=1, source_target_pairs={{0,64},{32,96},{64,0},{96,32},{1,65},{33,97},{65,1},{97,33},{2,66}... | collective-permute-start | bytes 196616 | tf_op jit(solution)/shard_map/ppermute | solution.py:303
  61.1 2.2 %zden.2.z_ref = f32[1,384]{1,0:T(1,128)S(1)} custom-call(f32[128,128]{1,0:T(8,128)S(1)} %sum.3.after_ref.c0, bf16[768,256]{1,0:T(8,128)(2,1)S(1)} %get-tuple-element.39.f_ref, bf16[8,256,2048]{2,1,0:T(8,128)(2,1)S(1)} %get-tuple-element.47.p_ref.refs_1_), custom_call_target="tpu_custom_call" | custom-call | tf_op jit(solution)/shard_map/zden/pallas_call | solution.py:320
  64.2 2.4 %row.3 = (f32[1,384]{1,0:T(1,128)S(1)}, f32[1,384]{1,0:T(1,128)S(1)}, f32[384,16384]{1,0:T(8,128)S(1)}, bf16[8,256,2048]{2,1,0:T(8,128)(2,1)S(1)}) custom-call(f32[128,128]{1,0:T(8,128)S(1)} %sum.3.after_ref.c0, f32[128,128]{1,0:T(8,128)S(1)} %collective-permute-done.13.c1, ...), custom_call_target="tpu_custom_call", output_to_operand_aliasing={{2}: (5, {}), {3}: (6, {})} | custom-call | tf_op jit(solution)/shard_map/row/pallas_call | solution.py:396
  66.6 5.8 %collective-permute-start.16 = (f32[1,384]{1,0:T(1,128)S(1)}, f32[1,384]{1,0:T(1,128)S(1)}, u32[]{:S(2)}, u32[]{:S(2)}) collective-permute-start(f32[1,384]{1,0:T(1,128)S(1)} %get-tuple-element.49.a_ref), channel_id=1, source_target_pairs={{0,1},{1,0},{2,3},{3,2},{4,5},{5,4},{6,7},{7,6},{8,9},{9,8},{10,11... | collective-permute-start | bytes 4616 | tf_op jit(solution)/shard_map/ppermute | solution.py:315
  73.3 3.3 %collective-permute-start.18 = (f32[1,384]{1,0:T(1,128)S(1)}, f32[1,384]{1,0:T(1,128)S(1)}, u32[]{:S(2)}, u32[]{:S(2)}) collective-permute-start(f32[1,384]{1,0:T(1,128)S(1)} %pair.4.r0), channel_id=1, source_target_pairs={{0,4},{2,6},{4,0},{6,2},{1,5},{3,7},{5,1},{7,3},{8,12},{10,14},{12... | collective-permute-start | bytes 4616 | tf_op jit(solution)/shard_map/ppermute | solution.py:303
  84.3 2.2 %zden.3.z_ref = f32[1,384]{1,0:T(1,128)S(1)} custom-call(f32[128,128]{1,0:T(8,128)S(1)} %get-tuple-element.52.after_ref.a_ref, bf16[768,256]{1,0:T(8,128)(2,1)S(1)} %get-tuple-element.39.f_ref, bf16[8,256,2048]{2,1,0:T(8,128)(2,1)S(1)} %get-tuple-element.53.p_ref.refs_1_), custom_call_target="tpu_custom_call" | custom-call | tf_op jit(solution)/shard_map/zden/pallas_call | solution.py:320
  90.0 2.3 %collective-permute-done.23.c1 = f32[128,128]{1,0:T(8,128)S(1)} collective-permute-done((f32[128,128]{1,0:T(8,128)S(1)}, f32[128,128]{1,0:T(8,128)S(1)}, u32[]{:S(2)}, u32[]{:S(2)}) %collective-permute-start.23) | collective-permute-done | bytes 65568 | tf_op jit(solution)/shard_map/ppermute | solution.py:303
  93.0 2.4 %row_last.1 = (f32[128,128]{1,0:T(8,128)S(1)}, f32[2,384]{1,0:T(2,128)S(1)}, f32[384,16384]{1,0:T(8,128)S(1)}, bf16[8,256,2048]{2,1,0:T(8,128)(2,1)S(1)}) custom-call(f32[128,128]{1,0:T(8,128)S(1)} %get-tuple-element.54.c0, f32[128,128]{1,0:T(8,128)S(1)} %collective-permute-done.23.c1, ...), custom_call_target="tpu_custom_call", output_to_operand_aliasing={{2}: (6, {}), {3}: (7, {})} | custom-call | tf_op jit(solution)/shard_map/row_last/pallas_call | solution.py:418
  95.4 4.6 %collective-permute-start.26 = (f32[2,384]{1,0:T(2,128)S(1)}, f32[2,384]{1,0:T(2,128)S(1)}, u32[]{:S(2)}, u32[]{:S(2)}) collective-permute-start(f32[2,384]{1,0:T(2,128)S(1)} %get-tuple-element.58.a_ref), channel_id=1, source_target_pairs={{0,1},{1,0},{2,3},{3,2},{4,5},{5,4},{6,7},{7,6},{8,9},{9,8},{10,11... | collective-permute-start | bytes 9224 | tf_op jit(solution)/shard_map/ppermute | solution.py:315
  106.8 2.5 %collective-permute-start.31 = (f32[2,384]{1,0:T(2,128)S(1)}, f32[2,384]{1,0:T(2,128)S(1)}, u32[]{:S(2)}, u32[]{:S(2)}) collective-permute-start(f32[2,384]{1,0:T(2,128)S(1)} %rz.1.rz_ref.a_ref), channel_id=1, source_target_pairs={{0,16},{8,24},{16,0},{24,8},{1,17},{9,25},{17,1},{25,9},{2,18},{10... | collective-permute-start | bytes 9224 | tf_op jit(solution)/shard_map/ppermute | solution.py:303
  109.3 8.5 %dz.1 = (f32[192,256]{1,0:T(8,128)S(1)}, f32[192,256]{1,0:T(8,128)S(1)}) custom-call(f32[2,384]{1,0:T(2,128)S(1)} %rz.1.rz_ref.a_ref, f32[128,128]{1,0:T(8,128)S(1)} %get-tuple-element.59.c_ref, bf16[768,256]{1,0:T(8,128)(2,1)S(1)} %get-tuple-element.39.f_ref, f32[384,16384]{1,0:T(8,128)S(1)} %get-tuple-element.62.e_ref, ...), custom_call_target="tpu_custom_call" | custom-call | tf_op jit(solution)/shard_map/dz/pallas_call | solution.py:448
  117.8 2.4 %collective-permute-start.33 = (f32[192,256]{1,0:T(8,128)S(1)}, f32[192,256]{1,0:T(8,128)S(1)}, u32[]{:S(2)}, u32[]{:S(2)}) collective-permute-start(f32[192,256]{1,0:T(8,128)S(1)} %get-tuple-element.65), channel_id=1, source_target_pairs={{0,1},{1,0},{2,3},{3,2},{4,5},{5,4},{6,7},{7,6},{8,9},{9,8},{10,11... | collective-permute-start | bytes 589832 | tf_op jit(solution)/shard_map/ppermute | solution.py:469
  121.1 2.5 %collective-permute-start.36 = (f32[4,2,384]{2,1,0:T(2,128)S(1)}, f32[4,2,384]{2,1,0:T(2,128)S(1)}, u32[]{:S(2)}, u32[]{:S(2)}) collective-permute-start(f32[4,2,384]{2,1,0:T(2,128)S(1)} %get-tuple-element.66.r0), channel_id=1, source_target_pairs={{0,64},{32,96},{64,0},{96,32},{1,65},{33,97},{65,1},{97,33},{2,66}... | collective-permute-start | bytes 36872 | tf_op jit(solution)/shard_map/ppermute | solution.py:303
  126.3 8.6 %pg.2.acc_ref = f32[1024,256]{1,0:T(8,128)S(1)} custom-call(f32[4,2,384]{2,1,0:T(2,128)S(1)} %get-tuple-element.66.r0, f32[4,2,384]{2,1,0:T(2,128)S(1)} %collective-permute-done.35.r1, f32[4,2,384]{2,1,0:T(2,128)S(1)} %collective-permute-done.36.r2, f32[4,2,384]{2,1,0:T(2,128)S(1)} %collective-permute-done.37.r3, ...), custom_call_target="tpu_custom_call" | custom-call | flops 4849999872 | bytes 4000000 | tf_op jit(solution)/shard_map/pg/pallas_call | solution.py:474
  134.9 2.7 %collective-permute-start.38 = (f32[192,256]{1,0:T(8,128)S(1)}, f32[192,256]{1,0:T(8,128)S(1)}, u32[]{:S(2)}, u32[]{:S(2)}) collective-permute-start(f32[192,256]{1,0:T(8,128)S(1)} %get-tuple-element.72.a_ref), channel_id=1, source_target_pairs={{0,6},{2,4},{4,2},{6,0},{1,7},{3,5},{5,3},{7,1},{8,14},{10,12},{12... | collective-permute-start | bytes 589832 | tf_op jit(solution)/shard_map/ppermute | solution.py:500
  137.6 9.6 %pg.3 = f32[256,1024]{1,0:T(8,128)} custom-call(f32[4,2,384]{2,1,0:T(2,128)S(1)} %get-tuple-element.66.r0, f32[4,2,384]{2,1,0:T(2,128)S(1)} %collective-permute-done.35.r1, f32[4,2,384]{2,1,0:T(2,128)S(1)} %collective-permute-done.36.r2, f32[4,2,384]{2,1,0:T(2,128)S(1)} %collective-permute-done.37.r3, bf16[1024,256]{1,0:T(8,128)(2,1)S(1)} %get-tuple-element.67.pt, ...), custom_call_target="tpu_custom_call" | custom-call | flops 4849999872 | bytes 4000000 | tf_op jit(solution)/shard_map/pg/pallas_call | solution.py:474
  (86 shorter events, 50.2 us)
Async XLA Ops:
  7.2 119.1 %all-gather.2.cloned.1.call-start = ((), (), s32[]{:S(2)}) async-start(), calls=%async_computation | async-start | bytes 6340608 | tf_op jit(solution)/shard_map/all_gather | solution.py:344
  18.3 5.9 %collective-permute-start = (f32[128,128]{1,0:T(8,128)S(1)}, f32[128,128]{1,0:T(8,128)S(1)}, u32[]{:S(2)}, u32[]{:S(2)}) collective-permute-start(f32[128,128]{1,0:T(8,128)S(1)} %get-tuple-element.40.a_ref), channel_id=1, source_target_pairs={{0,8},{8,16},{16,24},{24,0},{1,9},{9,17},{17,25},{25,1},{2,10},{10... | collective-permute-start | bytes 196616 | tf_op jit(solution)/shard_map/ppermute | solution.py:303
  20.5 5.2 %collective-permute-start.1 = (f32[128,128]{1,0:T(8,128)S(1)}, f32[128,128]{1,0:T(8,128)S(1)}, u32[]{:S(2)}, u32[]{:S(2)}) collective-permute-start(f32[128,128]{1,0:T(8,128)S(1)} %get-tuple-element.40.a_ref), channel_id=1, source_target_pairs={{0,16},{8,24},{16,0},{24,8},{1,17},{9,25},{17,1},{25,9},{2,18},{10... | collective-permute-start | bytes 196616 | tf_op jit(solution)/shard_map/ppermute | solution.py:303
  26.6 4.9 %collective-permute-start.3 = (f32[128,128]{1,0:T(8,128)S(1)}, f32[128,128]{1,0:T(8,128)S(1)}, u32[]{:S(2)}, u32[]{:S(2)}) collective-permute-start(f32[128,128]{1,0:T(8,128)S(1)} %sum.2.c0), channel_id=1, source_target_pairs={{0,32},{32,64},{64,96},{96,0},{1,33},{33,65},{65,97},{97,1},{2,34}... | collective-permute-start | bytes 196616 | tf_op jit(solution)/shard_map/ppermute | solution.py:303
  27.9 4.8 %collective-permute-start.4 = (f32[128,128]{1,0:T(8,128)S(1)}, f32[128,128]{1,0:T(8,128)S(1)}, u32[]{:S(2)}, u32[]{:S(2)}) collective-permute-start(f32[128,128]{1,0:T(8,128)S(1)} %sum.2.c0), channel_id=1, source_target_pairs={{0,64},{32,96},{64,0},{96,32},{1,65},{33,97},{65,1},{97,33},{2,66}... | collective-permute-start | bytes 196616 | tf_op jit(solution)/shard_map/ppermute | solution.py:303
  40.6 5.8 %collective-permute-start.7 = (f32[1,384]{1,0:T(1,128)S(1)}, f32[1,384]{1,0:T(1,128)S(1)}, u32[]{:S(2)}, u32[]{:S(2)}) collective-permute-start(f32[1,384]{1,0:T(1,128)S(1)} %pair.3.r0), channel_id=1, source_target_pairs={{0,2},{2,4},{4,6},{6,0},{1,3},{3,5},{5,7},{7,1},{8,10},{10,12},{12... | collective-permute-start | bytes 4616 | tf_op jit(solution)/shard_map/ppermute | solution.py:303
  50.6 4.4 %collective-permute-start.10 = (f32[128,128]{1,0:T(8,128)S(1)}, f32[128,128]{1,0:T(8,128)S(1)}, u32[]{:S(2)}, u32[]{:S(2)}) collective-permute-start(f32[128,128]{1,0:T(8,128)S(1)} %get-tuple-element.46.a_ref), channel_id=1, source_target_pairs={{0,8},{8,16},{16,24},{24,0},{1,9},{9,17},{17,25},{25,1},{2,10},{10... | collective-permute-start | bytes 196616 | tf_op jit(solution)/shard_map/ppermute | solution.py:303
  50.7 5.7 %collective-permute-start.11 = (f32[128,128]{1,0:T(8,128)S(1)}, f32[128,128]{1,0:T(8,128)S(1)}, u32[]{:S(2)}, u32[]{:S(2)}) collective-permute-start(f32[128,128]{1,0:T(8,128)S(1)} %get-tuple-element.46.a_ref), channel_id=1, source_target_pairs={{0,16},{8,24},{16,0},{24,8},{1,17},{9,25},{17,1},{25,9},{2,18},{10... | collective-permute-start | bytes 196616 | tf_op jit(solution)/shard_map/ppermute | solution.py:303
  57.4 5.8 %collective-permute-start.13 = (f32[128,128]{1,0:T(8,128)S(1)}, f32[128,128]{1,0:T(8,128)S(1)}, u32[]{:S(2)}, u32[]{:S(2)}) collective-permute-start(f32[128,128]{1,0:T(8,128)S(1)} %sum.3.after_ref.c0), channel_id=1, source_target_pairs={{0,32},{32,64},{64,96},{96,0},{1,33},{33,65},{65,97},{97,1},{2,34}... | collective-permute-start | bytes 196616 | tf_op jit(solution)/shard_map/ppermute | solution.py:303
  58.4 5.0 %collective-permute-start.14 = (f32[128,128]{1,0:T(8,128)S(1)}, f32[128,128]{1,0:T(8,128)S(1)}, u32[]{:S(2)}, u32[]{:S(2)}) collective-permute-start(f32[128,128]{1,0:T(8,128)S(1)} %sum.3.after_ref.c0), channel_id=1, source_target_pairs={{0,64},{32,96},{64,0},{96,32},{1,65},{33,97},{65,1},{97,33},{2,66}... | collective-permute-start | bytes 196616 | tf_op jit(solution)/shard_map/ppermute | solution.py:303
  66.6 6.6 %collective-permute-start.16 = (f32[1,384]{1,0:T(1,128)S(1)}, f32[1,384]{1,0:T(1,128)S(1)}, u32[]{:S(2)}, u32[]{:S(2)}) collective-permute-start(f32[1,384]{1,0:T(1,128)S(1)} %get-tuple-element.49.a_ref), channel_id=1, source_target_pairs={{0,1},{1,0},{2,3},{3,2},{4,5},{5,4},{6,7},{7,6},{8,9},{9,8},{10,11... | collective-permute-start | bytes 4616 | tf_op jit(solution)/shard_map/ppermute | solution.py:315
  73.3 4.4 %collective-permute-start.18 = (f32[1,384]{1,0:T(1,128)S(1)}, f32[1,384]{1,0:T(1,128)S(1)}, u32[]{:S(2)}, u32[]{:S(2)}) collective-permute-start(f32[1,384]{1,0:T(1,128)S(1)} %pair.4.r0), channel_id=1, source_target_pairs={{0,4},{2,6},{4,0},{6,2},{1,5},{3,7},{5,1},{7,3},{8,12},{10,14},{12... | collective-permute-start | bytes 4616 | tf_op jit(solution)/shard_map/ppermute | solution.py:303
  81.6 5.0 %collective-permute-start.20 = (f32[128,128]{1,0:T(8,128)S(1)}, f32[128,128]{1,0:T(8,128)S(1)}, u32[]{:S(2)}, u32[]{:S(2)}) collective-permute-start(f32[128,128]{1,0:T(8,128)S(1)} %get-tuple-element.52.after_ref.a_ref), channel_id=1, source_target_pairs={{0,8},{8,16},{16,24},{24,0},{1,9},{9,17},{17,25},{25,1},{2,10},{10... | collective-permute-start | bytes 196616 | tf_op jit(solution)/shard_map/ppermute | solution.py:303
  81.7 5.1 %collective-permute-start.21 = (f32[128,128]{1,0:T(8,128)S(1)}, f32[128,128]{1,0:T(8,128)S(1)}, u32[]{:S(2)}, u32[]{:S(2)}) collective-permute-start(f32[128,128]{1,0:T(8,128)S(1)} %get-tuple-element.52.after_ref.a_ref), channel_id=1, source_target_pairs={{0,16},{8,24},{16,0},{24,8},{1,17},{9,25},{17,1},{25,9},{2,18},{10... | collective-permute-start | bytes 196616 | tf_op jit(solution)/shard_map/ppermute | solution.py:303
  87.3 5.1 %collective-permute-start.23 = (f32[128,128]{1,0:T(8,128)S(1)}, f32[128,128]{1,0:T(8,128)S(1)}, u32[]{:S(2)}, u32[]{:S(2)}) collective-permute-start(f32[128,128]{1,0:T(8,128)S(1)} %get-tuple-element.54.c0), channel_id=1, source_target_pairs={{0,32},{32,64},{64,96},{96,0},{1,33},{33,65},{65,97},{97,1},{2,34}... | collective-permute-start | bytes 196616 | tf_op jit(solution)/shard_map/ppermute | solution.py:303
  87.4 5.0 %collective-permute-start.24 = (f32[128,128]{1,0:T(8,128)S(1)}, f32[128,128]{1,0:T(8,128)S(1)}, u32[]{:S(2)}, u32[]{:S(2)}) collective-permute-start(f32[128,128]{1,0:T(8,128)S(1)} %get-tuple-element.54.c0), channel_id=1, source_target_pairs={{0,64},{32,96},{64,0},{96,32},{1,65},{33,97},{65,1},{97,33},{2,66}... | collective-permute-start | bytes 196616 | tf_op jit(solution)/shard_map/ppermute | solution.py:303
  95.4 5.4 %collective-permute-start.26 = (f32[2,384]{1,0:T(2,128)S(1)}, f32[2,384]{1,0:T(2,128)S(1)}, u32[]{:S(2)}, u32[]{:S(2)}) collective-permute-start(f32[2,384]{1,0:T(2,128)S(1)} %get-tuple-element.58.a_ref), channel_id=1, source_target_pairs={{0,1},{1,0},{2,3},{3,2},{4,5},{5,4},{6,7},{7,6},{8,9},{9,8},{10,11... | collective-permute-start | bytes 9224 | tf_op jit(solution)/shard_map/ppermute | solution.py:315
  105.7 12.1 %collective-permute-start.30 = (f32[2,384]{1,0:T(2,128)S(1)}, f32[2,384]{1,0:T(2,128)S(1)}, u32[]{:S(2)}, u32[]{:S(2)}) collective-permute-start(f32[2,384]{1,0:T(2,128)S(1)} %rz.1.rz_ref.a_ref), channel_id=1, source_target_pairs={{0,8},{8,16},{16,24},{24,0},{1,9},{9,17},{17,25},{25,1},{2,10},{10... | collective-permute-start | bytes 9224 | tf_op jit(solution)/shard_map/ppermute | solution.py:303
  106.8 11.0 %collective-permute-start.31 = (f32[2,384]{1,0:T(2,128)S(1)}, f32[2,384]{1,0:T(2,128)S(1)}, u32[]{:S(2)}, u32[]{:S(2)}) collective-permute-start(f32[2,384]{1,0:T(2,128)S(1)} %rz.1.rz_ref.a_ref), channel_id=1, source_target_pairs={{0,16},{8,24},{16,0},{24,8},{1,17},{9,25},{17,1},{25,9},{2,18},{10... | collective-permute-start | bytes 9224 | tf_op jit(solution)/shard_map/ppermute | solution.py:303
  109.3 8.5 %collective-permute-start.32 = (f32[2,384]{1,0:T(2,128)S(1)}, f32[2,384]{1,0:T(2,128)S(1)}, u32[]{:S(2)}, u32[]{:S(2)}) collective-permute-start(f32[2,384]{1,0:T(2,128)S(1)} %rz.1.rz_ref.a_ref), channel_id=1, source_target_pairs={{0,24},{8,0},{16,8},{24,16},{1,25},{9,1},{17,9},{25,17},{2,26},{10... | collective-permute-start | bytes 9224 | tf_op jit(solution)/shard_map/ppermute | solution.py:303
  117.8 5.8 %collective-permute-start.33 = (f32[192,256]{1,0:T(8,128)S(1)}, f32[192,256]{1,0:T(8,128)S(1)}, u32[]{:S(2)}, u32[]{:S(2)}) collective-permute-start(f32[192,256]{1,0:T(8,128)S(1)} %get-tuple-element.65), channel_id=1, source_target_pairs={{0,1},{1,0},{2,3},{3,2},{4,5},{5,4},{6,7},{7,6},{8,9},{9,8},{10,11... | collective-permute-start | bytes 589832 | tf_op jit(solution)/shard_map/ppermute | solution.py:469
  120.2 4.8 %collective-permute-start.35 = (f32[4,2,384]{2,1,0:T(2,128)S(1)}, f32[4,2,384]{2,1,0:T(2,128)S(1)}, u32[]{:S(2)}, u32[]{:S(2)}) collective-permute-start(f32[4,2,384]{2,1,0:T(2,128)S(1)} %get-tuple-element.66.r0), channel_id=1, source_target_pairs={{0,32},{32,64},{64,96},{96,0},{1,33},{33,65},{65,97},{97,1},{2,34}... | collective-permute-start | bytes 36872 | tf_op jit(solution)/shard_map/ppermute | solution.py:303
  123.7 11.1 %collective-permute-start.34 = (f32[192,256]{1,0:T(8,128)S(1)}, f32[192,256]{1,0:T(8,128)S(1)}, u32[]{:S(2)}, u32[]{:S(2)}) collective-permute-start(f32[192,256]{1,0:T(8,128)S(1)} %add.3.a_ref), channel_id=1, source_target_pairs={{0,2},{2,0},{4,6},{6,4},{1,3},{3,1},{5,7},{7,5},{8,10},{10,8},{12,... | collective-permute-start | bytes 589832 | tf_op jit(solution)/shard_map/ppermute | solution.py:471
  134.9 12.4 %collective-permute-start.38 = (f32[192,256]{1,0:T(8,128)S(1)}, f32[192,256]{1,0:T(8,128)S(1)}, u32[]{:S(2)}, u32[]{:S(2)}) collective-permute-start(f32[192,256]{1,0:T(8,128)S(1)} %get-tuple-element.72.a_ref), channel_id=1, source_target_pairs={{0,6},{2,4},{4,2},{6,0},{1,7},{3,5},{5,3},{7,1},{8,14},{10,12},{12... | collective-permute-start | bytes 589832 | tf_op jit(solution)/shard_map/ppermute | solution.py:500
  (18 other events, 69.3 us)
Sparse Core Ops, SparseCore 0:
  11.6 71.9 all-gather.1

commit v7 on v5

--- a/solution.py
+++ b/solution.py
@@ -53,7 +53,9 @@
     return jnp.sum(jnp.transpose(acc), axis=0, keepdims=True)
 
 
-def norm_kernel(t_ref, s_ref, out_ref, share_ref):
+def norm_kernel(t_ref, s_ref, w_ref, out_ref, share_ref, w0_ref, sem):
+    copy = pltpu.make_async_copy(w_ref.at[:, pl.ds(0, CHUNK)], w0_ref, sem)
+    copy.start()
     for src, rows in ((t_ref, slice(0, ROWS)), (s_ref, slice(ROWS, 2 * ROWS))):
         feats = src[...].astype(f32)
         out_ref[rows, :] = (feats * row_norm(feats)).astype(bf16)
@@ -61,16 +63,18 @@
     for k in range(2):
         rows = pl.ds(pl.multiple_of(k * ROWS + start, SHARE), SHARE)
         share_ref[:, k * D : (k + 1) * D] = out_ref[rows, :]
-
-
-def first_kernel(w_ref, f_ref, p_ref, e_ref, col_ref, sems):
+    copy.wait()
+
+
+def first_kernel(w_ref, w0_ref, f_ref, p_ref, e_ref, col_ref, sems):
     count = COLS // CHUNK
 
     def fetch(k):
         lanes = pl.ds(pl.multiple_of(k * CHUNK, CHUNK), CHUNK)
         return pltpu.make_async_copy(w_ref.at[:, lanes], p_ref.at[k], sems.at[k])
 
-    for k in range(count):
+    pltpu.make_async_copy(w0_ref, p_ref.at[0], sems.at[0]).start()
+    for k in range(1, count):
         fetch(k).start()
 
     @pl.loop(0, count)
@@ -332,27 +336,29 @@
     vmem = pltpu.VMEM
     kept = vmem((ROWS, COLS), f32)
 
-    feats, share = pl.pallas_call(
+    feats, share, w0 = pl.pallas_call(
         norm_kernel,
         grid=(1,),
-        out_shape=(vmem((2 * ROWS, D), bf16), sds((SHARE, 2 * D), bf16)),
-        in_specs=[pl.BlockSpec((ROWS, D), lambda i: (0, 0))] * 2,
-        out_specs=(whole(), whole()),
+        out_shape=(vmem((2 * ROWS, D), bf16), sds((SHARE, 2 * D), bf16), vmem((D, CHUNK), bf16)),
+        in_specs=[pl.BlockSpec((ROWS, D), lambda i: (0, 0))] * 2
+        + [pl.BlockSpec(memory_space=pl.ANY)],
+        out_specs=(whole(),) * 3,
+        scratch_shapes=[pltpu.SemaphoreType.DMA(())],
         compiler_params=params(5),
         name="norm",
-    )(in_hbm(teacher_feats), in_hbm(student_feats))
+    )(in_hbm(teacher_feats), in_hbm(student_feats), in_hbm(proto_weight))
     feats_all = lax.all_gather(share, ALL, axis=0, tiled=True)
 
     packed = vmem((COLS // CHUNK, D, CHUNK), bf16)
     protos, expo, colp = pl.pallas_call(
         first_kernel,
         out_shape=(packed, kept, vmem((GROUPS, 128), f32)),
-        in_specs=[pl.BlockSpec(memory_space=pl.ANY), whole()],
+        in_specs=[pl.BlockSpec(memory_space=pl.ANY), whole(), whole()],
         out_specs=(whole(), whole(), whole()),
         scratch_shapes=[pltpu.SemaphoreType.DMA((COLS // CHUNK,))],
         compiler_params=params(5),
         name="first",
-    )(in_hbm(proto_weight), in_vmem(feats))
+    )(in_hbm(proto_weight), in_vmem(w0), in_vmem(feats))
 
     keep = [expo, protos]
     shapes = [kept, packed]

time: 154 us -> 152 us (0.987)
  transfers between devices with their start and end apart: 42 -> 42, of which waited for: 25 -> 23; matrix products, arithmetic and copies ran while one was open for 0% -> 0% of each run, Pallas kernels for 33% -> 31%
where the time goes in v7:
time: 152 us
  starting transfers between devices  65.3 us (43%)
  Pallas kernels  51.5 us (34%)
  waiting for transfers between devices  21.2 us (14%)
  between operations  14.2 us (9%)
    ppermute x36, starting transfers between devices, around(): parts.append(lax.ppermute(x, axis, [(i, (i + d) % 4) for i in range(4)]))  46.9 us
    ppermute x36, waiting for transfers between devices, around(): parts.append(lax.ppermute(x, axis, [(i, (i + d) % 4) for i in range(4)]))  17.7 us
    pallas_call x1, Pallas kernels, shards(): pl.pallas_call(pg_kernel, grid=(NB * ROWS // PG_ROWS,), out_shape=sds((D,...  15.6 us
    ppermute x3, starting transfers between devices, row_terms(): lax.ppermute(rowp, 'c', [(0, 1), (1, 0)])  14.2 us
    pallas_call x1, Pallas kernels, shards(): pl.pallas_call(first_kernel, out_shape=(packed, kept, vmem((GROUPS, 128),...  8.21 us
    pallas_call x1, Pallas kernels, shards(): pl.pallas_call(dz_kernel, out_shape=(vmem((half, D), f32), vmem((half, D)...  7.92 us
    pallas_call x2, Pallas kernels, z_call(): pl.pallas_call(functools.partial(z_kernel, half), out_shape=pltpu.VMEM((1...  4.35 us
    pallas_call x2, Pallas kernels, shards(): pl.pallas_call(col_kernel, out_shape=[vmem((GROUPS, 128), f32)] + shapes,...  3.92 us
  transfers between devices with their start and end apart: 42, of which 23 were waited for; matrix products, arithmetic and copies ran while one was open for 0% of the time, Pallas kernels for 31%

profile of v7, /device:TPU:1, one launch (start us, length us, event | category | flops | bytes accessed | tf_op | source)
XLA Modules:
  0.0 152.3 jit_solution(6107067117757856084)
XLA Ops:
  7.2 2.9 %norm.1 = (bf16[768,256]{1,0:T(8,128)(2,1)S(1)}, bf16[48,512]{1,0:T(8,128)(2,1)}, bf16[256,2048]{1,0:T(8,128)(2,1)S(1)}) custom-call(bf16[384,256]{1,0:T(8,128)(2,1)} %t_ref.1, bf16[384,256]{1,0:T(8,128)(2,1)} %s_ref.2, bf16[256,16384]{1,0:T(8,128)(2,1)} %w_ref.3), custom_call_target="tpu_custom_call" | custom-call | tf_op jit(solution)/shard_map/norm/pallas_call | solution.py:339
  10.1 8.2 %first.1 = (bf16[8,256,2048]{2,1,0:T(8,128)(2,1)S(1)}, f32[384,16384]{1,0:T(8,128)S(1)}, f32[128,128]{1,0:T(8,128)S(1)}) custom-call(bf16[256,16384]{1,0:T(8,128)(2,1)} %w_ref.3, bf16[256,2048]{1,0:T(8,128)(2,1)S(1)} %get-tuple-element.40.w0_ref, bf16[768,256]{1,0:T(8,128)(2,1)S(1)} %get-tuple-element.41.f_ref), custom_call_target="tpu_custom_call" | custom-call | tf_op jit(solution)/shard_map/first/pallas_call | solution.py:353
  18.3 2.2 %collective-permute-start = (f32[128,128]{1,0:T(8,128)S(1)}, f32[128,128]{1,0:T(8,128)S(1)}, u32[]{:S(2)}, u32[]{:S(2)}) collective-permute-start(f32[128,128]{1,0:T(8,128)S(1)} %get-tuple-element.42.a_ref), channel_id=1, source_target_pairs={{0,8},{8,16},{16,24},{24,0},{1,9},{9,17},{17,25},{25,1},{2,10},{10... | collective-permute-start | bytes 196616 | tf_op jit(solution)/shard_map/ppermute | solution.py:307
  20.5 2.6 %collective-permute-start.1 = (f32[128,128]{1,0:T(8,128)S(1)}, f32[128,128]{1,0:T(8,128)S(1)}, u32[]{:S(2)}, u32[]{:S(2)}) collective-permute-start(f32[128,128]{1,0:T(8,128)S(1)} %get-tuple-element.42.a_ref), channel_id=1, source_target_pairs={{0,16},{8,24},{16,0},{24,8},{1,17},{9,25},{17,1},{25,9},{2,18},{10... | collective-permute-start | bytes 196616 | tf_op jit(solution)/shard_map/ppermute | solution.py:307
  27.9 2.4 %collective-permute-start.4 = (f32[128,128]{1,0:T(8,128)S(1)}, f32[128,128]{1,0:T(8,128)S(1)}, u32[]{:S(2)}, u32[]{:S(2)}) collective-permute-start(f32[128,128]{1,0:T(8,128)S(1)} %sum.2.c0), channel_id=1, source_target_pairs={{0,64},{32,96},{64,0},{96,32},{1,65},{33,97},{65,1},{97,33},{2,66}... | collective-permute-start | bytes 196616 | tf_op jit(solution)/shard_map/ppermute | solution.py:307
  33.9 2.4 %row.2 = (f32[1,384]{1,0:T(1,128)S(1)}, f32[384,16384]{1,0:T(8,128)S(1)}, bf16[8,256,2048]{2,1,0:T(8,128)(2,1)S(1)}) custom-call(f32[128,128]{1,0:T(8,128)S(1)} %sum.2.c0, f32[128,128]{1,0:T(8,128)S(1)} %collective-permute-done.3.c1, f32[128,128]{1,0:T(8,128)S(1)} %collective-permute-done.4.c2, ...), custom_call_target="tpu_custom_call", output_to_operand_aliasing={{1}: (4, {}), {2}: (5, {})} | custom-call | tf_op jit(solution)/shard_map/row/pallas_call | solution.py:390
  36.3 3.4 %collective-permute-start.6 = (f32[1,384]{1,0:T(1,128)S(1)}, f32[1,384]{1,0:T(1,128)S(1)}, u32[]{:S(2)}, u32[]{:S(2)}) collective-permute-start(f32[1,384]{1,0:T(1,128)S(1)} %get-tuple-element.45.a_ref), channel_id=1, source_target_pairs={{0,1},{1,0},{2,3},{3,2},{4,5},{5,4},{6,7},{7,6},{8,9},{9,8},{10,11... | collective-permute-start | bytes 4616 | tf_op jit(solution)/shard_map/ppermute | solution.py:319
  42.4 3.2 %collective-permute-start.8 = (f32[1,384]{1,0:T(1,128)S(1)}, f32[1,384]{1,0:T(1,128)S(1)}, u32[]{:S(2)}, u32[]{:S(2)}) collective-permute-start(f32[1,384]{1,0:T(1,128)S(1)} %pair.3.r0), channel_id=1, source_target_pairs={{0,4},{2,6},{4,0},{6,2},{1,5},{3,7},{5,1},{7,3},{8,12},{10,14},{12... | collective-permute-start | bytes 4616 | tf_op jit(solution)/shard_map/ppermute | solution.py:307
  50.5 3.4 %collective-permute-start.11 = (f32[128,128]{1,0:T(8,128)S(1)}, f32[128,128]{1,0:T(8,128)S(1)}, u32[]{:S(2)}, u32[]{:S(2)}) collective-permute-start(f32[128,128]{1,0:T(8,128)S(1)} %get-tuple-element.48.a_ref), channel_id=1, source_target_pairs={{0,16},{8,24},{16,0},{24,8},{1,17},{9,25},{17,1},{25,9},{2,18},{10... | collective-permute-start | bytes 196616 | tf_op jit(solution)/shard_map/ppermute | solution.py:307
  58.0 3.0 %collective-permute-start.14 = (f32[128,128]{1,0:T(8,128)S(1)}, f32[128,128]{1,0:T(8,128)S(1)}, u32[]{:S(2)}, u32[]{:S(2)}) collective-permute-start(f32[128,128]{1,0:T(8,128)S(1)} %sum.3.after_ref.c0), channel_id=1, source_target_pairs={{0,64},{32,96},{64,0},{96,32},{1,65},{33,97},{65,1},{97,33},{2,66}... | collective-permute-start | bytes 196616 | tf_op jit(solution)/shard_map/ppermute | solution.py:307
  61.0 2.2 %zden.2.z_ref = f32[1,384]{1,0:T(1,128)S(1)} custom-call(f32[128,128]{1,0:T(8,128)S(1)} %sum.3.after_ref.c0, bf16[768,256]{1,0:T(8,128)(2,1)S(1)} %get-tuple-element.41.f_ref, bf16[8,256,2048]{2,1,0:T(8,128)(2,1)S(1)} %get-tuple-element.49.p_ref.refs_1_), custom_call_target="tpu_custom_call" | custom-call | tf_op jit(solution)/shard_map/zden/pallas_call | solution.py:324
  64.1 2.4 %row.3 = (f32[1,384]{1,0:T(1,128)S(1)}, f32[1,384]{1,0:T(1,128)S(1)}, f32[384,16384]{1,0:T(8,128)S(1)}, bf16[8,256,2048]{2,1,0:T(8,128)(2,1)S(1)}) custom-call(f32[128,128]{1,0:T(8,128)S(1)} %sum.3.after_ref.c0, f32[128,128]{1,0:T(8,128)S(1)} %collective-permute-done.13.c1, ...), custom_call_target="tpu_custom_call", output_to_operand_aliasing={{2}: (5, {}), {3}: (6, {})} | custom-call | tf_op jit(solution)/shard_map/row/pallas_call | solution.py:402
  66.5 5.9 %collective-permute-start.16 = (f32[1,384]{1,0:T(1,128)S(1)}, f32[1,384]{1,0:T(1,128)S(1)}, u32[]{:S(2)}, u32[]{:S(2)}) collective-permute-start(f32[1,384]{1,0:T(1,128)S(1)} %get-tuple-element.51.a_ref), channel_id=1, source_target_pairs={{0,1},{1,0},{2,3},{3,2},{4,5},{5,4},{6,7},{7,6},{8,9},{9,8},{10,11... | collective-permute-start | bytes 4616 | tf_op jit(solution)/shard_map/ppermute | solution.py:319
  80.1 2.5 %collective-permute-start.21 = (f32[128,128]{1,0:T(8,128)S(1)}, f32[128,128]{1,0:T(8,128)S(1)}, u32[]{:S(2)}, u32[]{:S(2)}) collective-permute-start(f32[128,128]{1,0:T(8,128)S(1)} %get-tuple-element.54.after_ref.a_ref), channel_id=1, source_target_pairs={{0,16},{8,24},{16,0},{24,8},{1,17},{9,25},{17,1},{25,9},{2,18},{10... | collective-permute-start | bytes 196616 | tf_op jit(solution)/shard_map/ppermute | solution.py:307
  83.4 2.2 %zden.3.z_ref = f32[1,384]{1,0:T(1,128)S(1)} custom-call(f32[128,128]{1,0:T(8,128)S(1)} %get-tuple-element.54.after_ref.a_ref, bf16[768,256]{1,0:T(8,128)(2,1)S(1)} %get-tuple-element.41.f_ref, bf16[8,256,2048]{2,1,0:T(8,128)(2,1)S(1)} %get-tuple-element.55.p_ref.refs_1_), custom_call_target="tpu_custom_call" | custom-call | tf_op jit(solution)/shard_map/zden/pallas_call | solution.py:324
  85.8 2.7 %collective-permute-start.24 = (f32[128,128]{1,0:T(8,128)S(1)}, f32[128,128]{1,0:T(8,128)S(1)}, u32[]{:S(2)}, u32[]{:S(2)}) collective-permute-start(f32[128,128]{1,0:T(8,128)S(1)} %get-tuple-element.56.c0), channel_id=1, source_target_pairs={{0,64},{32,96},{64,0},{96,32},{1,65},{33,97},{65,1},{97,33},{2,66}... | collective-permute-start | bytes 196616 | tf_op jit(solution)/shard_map/ppermute | solution.py:307
  91.6 2.4 %row_last.1 = (f32[128,128]{1,0:T(8,128)S(1)}, f32[2,384]{1,0:T(2,128)S(1)}, f32[384,16384]{1,0:T(8,128)S(1)}, bf16[8,256,2048]{2,1,0:T(8,128)(2,1)S(1)}) custom-call(f32[128,128]{1,0:T(8,128)S(1)} %get-tuple-element.56.c0, f32[128,128]{1,0:T(8,128)S(1)} %collective-permute-done.23.c1, ...), custom_call_target="tpu_custom_call", output_to_operand_aliasing={{2}: (6, {}), {3}: (7, {})} | custom-call | tf_op jit(solution)/shard_map/row_last/pallas_call | solution.py:424
  94.0 4.8 %collective-permute-start.26 = (f32[2,384]{1,0:T(2,128)S(1)}, f32[2,384]{1,0:T(2,128)S(1)}, u32[]{:S(2)}, u32[]{:S(2)}) collective-permute-start(f32[2,384]{1,0:T(2,128)S(1)} %get-tuple-element.60.a_ref), channel_id=1, source_target_pairs={{0,1},{1,0},{2,3},{3,2},{4,5},{5,4},{6,7},{7,6},{8,9},{9,8},{10,11... | collective-permute-start | bytes 9224 | tf_op jit(solution)/shard_map/ppermute | solution.py:319
  106.1 2.5 %collective-permute-start.31 = (f32[2,384]{1,0:T(2,128)S(1)}, f32[2,384]{1,0:T(2,128)S(1)}, u32[]{:S(2)}, u32[]{:S(2)}) collective-permute-start(f32[2,384]{1,0:T(2,128)S(1)} %rz.1.rz_ref.a_ref), channel_id=1, source_target_pairs={{0,16},{8,24},{16,0},{24,8},{1,17},{9,25},{17,1},{25,9},{2,18},{10... | collective-permute-start | bytes 9224 | tf_op jit(solution)/shard_map/ppermute | solution.py:307
  108.7 7.9 %dz.1 = (f32[192,256]{1,0:T(8,128)S(1)}, f32[192,256]{1,0:T(8,128)S(1)}) custom-call(f32[2,384]{1,0:T(2,128)S(1)} %rz.1.rz_ref.a_ref, f32[128,128]{1,0:T(8,128)S(1)} %get-tuple-element.61.c_ref, bf16[768,256]{1,0:T(8,128)(2,1)S(1)} %get-tuple-element.41.f_ref, f32[384,16384]{1,0:T(8,128)S(1)} %get-tuple-element.64.e_ref, ...), custom_call_target="tpu_custom_call" | custom-call | tf_op jit(solution)/shard_map/dz/pallas_call | solution.py:454
  116.6 2.5 %collective-permute-start.33 = (f32[192,256]{1,0:T(8,128)S(1)}, f32[192,256]{1,0:T(8,128)S(1)}, u32[]{:S(2)}, u32[]{:S(2)}) collective-permute-start(f32[192,256]{1,0:T(8,128)S(1)} %get-tuple-element.67), channel_id=1, source_target_pairs={{0,1},{1,0},{2,3},{3,2},{4,5},{5,4},{6,7},{7,6},{8,9},{9,8},{10,11... | collective-permute-start | bytes 589832 | tf_op jit(solution)/shard_map/ppermute | solution.py:475
  120.1 2.5 %collective-permute-start.38 = (f32[4,2,384]{2,1,0:T(2,128)S(1)}, f32[4,2,384]{2,1,0:T(2,128)S(1)}, u32[]{:S(2)}, u32[]{:S(2)}) collective-permute-start(f32[4,2,384]{2,1,0:T(2,128)S(1)} %get-tuple-element.68.r0), channel_id=1, source_target_pairs={{0,64},{32,96},{64,0},{96,32},{1,65},{33,97},{65,1},{97,33},{2,66}... | collective-permute-start | bytes 36872 | tf_op jit(solution)/shard_map/ppermute | solution.py:307
  123.2 2.5 %collective-permute-start.35 = (f32[192,256]{1,0:T(8,128)S(1)}, f32[192,256]{1,0:T(8,128)S(1)}, u32[]{:S(2)}, u32[]{:S(2)}) collective-permute-start(f32[192,256]{1,0:T(8,128)S(1)} %add.3.a_ref), channel_id=1, source_target_pairs={{0,4},{2,6},{4,0},{6,2},{1,5},{3,7},{5,1},{7,3},{8,12},{10,14},{12... | collective-permute-start | bytes 589832 | tf_op jit(solution)/shard_map/ppermute | solution.py:307
  126.1 15.6 %pg.1 = f32[256,1024]{1,0:T(8,128)} custom-call(f32[4,2,384]{2,1,0:T(2,128)S(1)} %get-tuple-element.68.r0, f32[4,2,384]{2,1,0:T(2,128)S(1)} %collective-permute-done.37.r1, f32[4,2,384]{2,1,0:T(2,128)S(1)} %collective-permute-done.38.r2, f32[4,2,384]{2,1,0:T(2,128)S(1)} %collective-permute-done.39.r3, bf16[1024,256]{1,0:T(8,128)(2,1)S(1)} %get-tuple-element.69.pt, ...), custom_call_target="tpu_custom_call" | custom-call | flops 9699999744 | bytes 8000000 | tf_op jit(solution)/shard_map/pg/pallas_call | solution.py:478
  (86 shorter events, 45.6 us)
Async XLA Ops:
  7.2 118.9 %all-gather.2.cloned.1.call-start = ((), (), s32[]{:S(2)}) async-start(), calls=%async_computation | async-start | bytes 6340608 | tf_op jit(solution)/shard_map/all_gather | solution.py:350
  18.3 5.9 %collective-permute-start = (f32[128,128]{1,0:T(8,128)S(1)}, f32[128,128]{1,0:T(8,128)S(1)}, u32[]{:S(2)}, u32[]{:S(2)}) collective-permute-start(f32[128,128]{1,0:T(8,128)S(1)} %get-tuple-element.42.a_ref), channel_id=1, source_target_pairs={{0,8},{8,16},{16,24},{24,0},{1,9},{9,17},{17,25},{25,1},{2,10},{10... | collective-permute-start | bytes 196616 | tf_op jit(solution)/shard_map/ppermute | solution.py:307
  20.5 5.2 %collective-permute-start.1 = (f32[128,128]{1,0:T(8,128)S(1)}, f32[128,128]{1,0:T(8,128)S(1)}, u32[]{:S(2)}, u32[]{:S(2)}) collective-permute-start(f32[128,128]{1,0:T(8,128)S(1)} %get-tuple-element.42.a_ref), channel_id=1, source_target_pairs={{0,16},{8,24},{16,0},{24,8},{1,17},{9,25},{17,1},{25,9},{2,18},{10... | collective-permute-start | bytes 196616 | tf_op jit(solution)/shard_map/ppermute | solution.py:307
  26.6 4.9 %collective-permute-start.3 = (f32[128,128]{1,0:T(8,128)S(1)}, f32[128,128]{1,0:T(8,128)S(1)}, u32[]{:S(2)}, u32[]{:S(2)}) collective-permute-start(f32[128,128]{1,0:T(8,128)S(1)} %sum.2.c0), channel_id=1, source_target_pairs={{0,32},{32,64},{64,96},{96,0},{1,33},{33,65},{65,97},{97,1},{2,34}... | collective-permute-start | bytes 196616 | tf_op jit(solution)/shard_map/ppermute | solution.py:307
  27.9 4.8 %collective-permute-start.4 = (f32[128,128]{1,0:T(8,128)S(1)}, f32[128,128]{1,0:T(8,128)S(1)}, u32[]{:S(2)}, u32[]{:S(2)}) collective-permute-start(f32[128,128]{1,0:T(8,128)S(1)} %sum.2.c0), channel_id=1, source_target_pairs={{0,64},{32,96},{64,0},{96,32},{1,65},{33,97},{65,1},{97,33},{2,66}... | collective-permute-start | bytes 196616 | tf_op jit(solution)/shard_map/ppermute | solution.py:307
  40.6 5.8 %collective-permute-start.7 = (f32[1,384]{1,0:T(1,128)S(1)}, f32[1,384]{1,0:T(1,128)S(1)}, u32[]{:S(2)}, u32[]{:S(2)}) collective-permute-start(f32[1,384]{1,0:T(1,128)S(1)} %pair.3.r0), channel_id=1, source_target_pairs={{0,2},{2,4},{4,6},{6,0},{1,3},{3,5},{5,7},{7,1},{8,10},{10,12},{12... | collective-permute-start | bytes 4616 | tf_op jit(solution)/shard_map/ppermute | solution.py:307
  50.4 4.5 %collective-permute-start.10 = (f32[128,128]{1,0:T(8,128)S(1)}, f32[128,128]{1,0:T(8,128)S(1)}, u32[]{:S(2)}, u32[]{:S(2)}) collective-permute-start(f32[128,128]{1,0:T(8,128)S(1)} %get-tuple-element.48.a_ref), channel_id=1, source_target_pairs={{0,8},{8,16},{16,24},{24,0},{1,9},{9,17},{17,25},{25,1},{2,10},{10... | collective-permute-start | bytes 196616 | tf_op jit(solution)/shard_map/ppermute | solution.py:307
  50.5 5.7 %collective-permute-start.11 = (f32[128,128]{1,0:T(8,128)S(1)}, f32[128,128]{1,0:T(8,128)S(1)}, u32[]{:S(2)}, u32[]{:S(2)}) collective-permute-start(f32[128,128]{1,0:T(8,128)S(1)} %get-tuple-element.48.a_ref), channel_id=1, source_target_pairs={{0,16},{8,24},{16,0},{24,8},{1,17},{9,25},{17,1},{25,9},{2,18},{10... | collective-permute-start | bytes 196616 | tf_op jit(solution)/shard_map/ppermute | solution.py:307
  57.3 5.9 %collective-permute-start.13 = (f32[128,128]{1,0:T(8,128)S(1)}, f32[128,128]{1,0:T(8,128)S(1)}, u32[]{:S(2)}, u32[]{:S(2)}) collective-permute-start(f32[128,128]{1,0:T(8,128)S(1)} %sum.3.after_ref.c0), channel_id=1, source_target_pairs={{0,32},{32,64},{64,96},{96,0},{1,33},{33,65},{65,97},{97,1},{2,34}... | collective-permute-start | bytes 196616 | tf_op jit(solution)/shard_map/ppermute | solution.py:307
  58.0 5.3 %collective-permute-start.14 = (f32[128,128]{1,0:T(8,128)S(1)}, f32[128,128]{1,0:T(8,128)S(1)}, u32[]{:S(2)}, u32[]{:S(2)}) collective-permute-start(f32[128,128]{1,0:T(8,128)S(1)} %sum.3.after_ref.c0), channel_id=1, source_target_pairs={{0,64},{32,96},{64,0},{96,32},{1,65},{33,97},{65,1},{97,33},{2,66}... | collective-permute-start | bytes 196616 | tf_op jit(solution)/shard_map/ppermute | solution.py:307
  66.5 6.7 %collective-permute-start.16 = (f32[1,384]{1,0:T(1,128)S(1)}, f32[1,384]{1,0:T(1,128)S(1)}, u32[]{:S(2)}, u32[]{:S(2)}) collective-permute-start(f32[1,384]{1,0:T(1,128)S(1)} %get-tuple-element.51.a_ref), channel_id=1, source_target_pairs={{0,1},{1,0},{2,3},{3,2},{4,5},{5,4},{6,7},{7,6},{8,9},{9,8},{10,11... | collective-permute-start | bytes 4616 | tf_op jit(solution)/shard_map/ppermute | solution.py:319
  80.0 5.5 %collective-permute-start.20 = (f32[128,128]{1,0:T(8,128)S(1)}, f32[128,128]{1,0:T(8,128)S(1)}, u32[]{:S(2)}, u32[]{:S(2)}) collective-permute-start(f32[128,128]{1,0:T(8,128)S(1)} %get-tuple-element.54.after_ref.a_ref), channel_id=1, source_target_pairs={{0,8},{8,16},{16,24},{24,0},{1,9},{9,17},{17,25},{25,1},{2,10},{10... | collective-permute-start | bytes 196616 | tf_op jit(solution)/shard_map/ppermute | solution.py:307
  80.1 5.5 %collective-permute-start.21 = (f32[128,128]{1,0:T(8,128)S(1)}, f32[128,128]{1,0:T(8,128)S(1)}, u32[]{:S(2)}, u32[]{:S(2)}) collective-permute-start(f32[128,128]{1,0:T(8,128)S(1)} %get-tuple-element.54.after_ref.a_ref), channel_id=1, source_target_pairs={{0,16},{8,24},{16,0},{24,8},{1,17},{9,25},{17,1},{25,9},{2,18},{10... | collective-permute-start | bytes 196616 | tf_op jit(solution)/shard_map/ppermute | solution.py:307
  85.8 5.0 %collective-permute-start.24 = (f32[128,128]{1,0:T(8,128)S(1)}, f32[128,128]{1,0:T(8,128)S(1)}, u32[]{:S(2)}, u32[]{:S(2)}) collective-permute-start(f32[128,128]{1,0:T(8,128)S(1)} %get-tuple-element.56.c0), channel_id=1, source_target_pairs={{0,64},{32,96},{64,0},{96,32},{1,65},{33,97},{65,1},{97,33},{2,66}... | collective-permute-start | bytes 196616 | tf_op jit(solution)/shard_map/ppermute | solution.py:307
  94.0 5.7 %collective-permute-start.26 = (f32[2,384]{1,0:T(2,128)S(1)}, f32[2,384]{1,0:T(2,128)S(1)}, u32[]{:S(2)}, u32[]{:S(2)}) collective-permute-start(f32[2,384]{1,0:T(2,128)S(1)} %get-tuple-element.60.a_ref), channel_id=1, source_target_pairs={{0,1},{1,0},{2,3},{3,2},{4,5},{5,4},{6,7},{7,6},{8,9},{9,8},{10,11... | collective-permute-start | bytes 9224 | tf_op jit(solution)/shard_map/ppermute | solution.py:319
  105.2 11.4 %collective-permute-start.30 = (f32[2,384]{1,0:T(2,128)S(1)}, f32[2,384]{1,0:T(2,128)S(1)}, u32[]{:S(2)}, u32[]{:S(2)}) collective-permute-start(f32[2,384]{1,0:T(2,128)S(1)} %rz.1.rz_ref.a_ref), channel_id=1, source_target_pairs={{0,8},{8,16},{16,24},{24,0},{1,9},{9,17},{17,25},{25,1},{2,10},{10... | collective-permute-start | bytes 9224 | tf_op jit(solution)/shard_map/ppermute | solution.py:307
  106.1 10.5 %collective-permute-start.31 = (f32[2,384]{1,0:T(2,128)S(1)}, f32[2,384]{1,0:T(2,128)S(1)}, u32[]{:S(2)}, u32[]{:S(2)}) collective-permute-start(f32[2,384]{1,0:T(2,128)S(1)} %rz.1.rz_ref.a_ref), channel_id=1, source_target_pairs={{0,16},{8,24},{16,0},{24,8},{1,17},{9,25},{17,1},{25,9},{2,18},{10... | collective-permute-start | bytes 9224 | tf_op jit(solution)/shard_map/ppermute | solution.py:307
  108.7 8.0 %collective-permute-start.32 = (f32[2,384]{1,0:T(2,128)S(1)}, f32[2,384]{1,0:T(2,128)S(1)}, u32[]{:S(2)}, u32[]{:S(2)}) collective-permute-start(f32[2,384]{1,0:T(2,128)S(1)} %rz.1.rz_ref.a_ref), channel_id=1, source_target_pairs={{0,24},{8,0},{16,8},{24,16},{1,25},{9,1},{17,9},{25,17},{2,26},{10... | collective-permute-start | bytes 9224 | tf_op jit(solution)/shard_map/ppermute | solution.py:307
  116.6 6.0 %collective-permute-start.33 = (f32[192,256]{1,0:T(8,128)S(1)}, f32[192,256]{1,0:T(8,128)S(1)}, u32[]{:S(2)}, u32[]{:S(2)}) collective-permute-start(f32[192,256]{1,0:T(8,128)S(1)} %get-tuple-element.67), channel_id=1, source_target_pairs={{0,1},{1,0},{2,3},{3,2},{4,5},{5,4},{6,7},{7,6},{8,9},{9,8},{10,11... | collective-permute-start | bytes 589832 | tf_op jit(solution)/shard_map/ppermute | solution.py:475
  119.1 6.6 %collective-permute-start.37 = (f32[4,2,384]{2,1,0:T(2,128)S(1)}, f32[4,2,384]{2,1,0:T(2,128)S(1)}, u32[]{:S(2)}, u32[]{:S(2)}) collective-permute-start(f32[4,2,384]{2,1,0:T(2,128)S(1)} %get-tuple-element.68.r0), channel_id=1, source_target_pairs={{0,32},{32,64},{64,96},{96,0},{1,33},{33,65},{65,97},{97,1},{2,34}... | collective-permute-start | bytes 36872 | tf_op jit(solution)/shard_map/ppermute | solution.py:307
  120.1 6.0 %collective-permute-start.38 = (f32[4,2,384]{2,1,0:T(2,128)S(1)}, f32[4,2,384]{2,1,0:T(2,128)S(1)}, u32[]{:S(2)}, u32[]{:S(2)}) collective-permute-start(f32[4,2,384]{2,1,0:T(2,128)S(1)} %get-tuple-element.68.r0), channel_id=1, source_target_pairs={{0,64},{32,96},{64,0},{96,32},{1,65},{33,97},{65,1},{97,33},{2,66}... | collective-permute-start | bytes 36872 | tf_op jit(solution)/shard_map/ppermute | solution.py:307
  122.7 19.0 %collective-permute-start.34 = (f32[192,256]{1,0:T(8,128)S(1)}, f32[192,256]{1,0:T(8,128)S(1)}, u32[]{:S(2)}, u32[]{:S(2)}) collective-permute-start(f32[192,256]{1,0:T(8,128)S(1)} %add.3.a_ref), channel_id=1, source_target_pairs={{0,2},{2,4},{4,6},{6,0},{1,3},{3,5},{5,7},{7,1},{8,10},{10,12},{12... | collective-permute-start | bytes 589832 | tf_op jit(solution)/shard_map/ppermute | solution.py:307
  123.2 18.5 %collective-permute-start.35 = (f32[192,256]{1,0:T(8,128)S(1)}, f32[192,256]{1,0:T(8,128)S(1)}, u32[]{:S(2)}, u32[]{:S(2)}) collective-permute-start(f32[192,256]{1,0:T(8,128)S(1)} %add.3.a_ref), channel_id=1, source_target_pairs={{0,4},{2,6},{4,0},{6,2},{1,5},{3,7},{5,1},{7,3},{8,12},{10,14},{12... | collective-permute-start | bytes 589832 | tf_op jit(solution)/shard_map/ppermute | solution.py:307
  125.7 16.0 %collective-permute-start.36 = (f32[192,256]{1,0:T(8,128)S(1)}, f32[192,256]{1,0:T(8,128)S(1)}, u32[]{:S(2)}, u32[]{:S(2)}) collective-permute-start(f32[192,256]{1,0:T(8,128)S(1)} %add.3.a_ref), channel_id=1, source_target_pairs={{0,6},{2,0},{4,2},{6,4},{1,7},{3,1},{5,3},{7,5},{8,14},{10,8},{12,... | collective-permute-start | bytes 589832 | tf_op jit(solution)/shard_map/ppermute | solution.py:307
  (19 other events, 78.6 us)
Sparse Core Ops, SparseCore 0:
  11.6 72.5 all-gather.1
